TPU v7x, 128 devices: a whole 4x4x4 slice. The times are simulated.
128 devices in a mesh: blocks: 32 (over z, x, core), chan: 4 (over y).
Axes of the slice: x: 4, y: 4, z: 4, core: 2. Of those that a mesh axis runs over, the one named last changes fastest.
Arguments:
- feats: bfloat16 [1024, 256, 512], P('blocks', 'chan')
- conv_weights: bfloat16 [3, 7, 256, 256], P(None, None, 'chan'), may hold values from -0.125 to 0.125
- norm_gain: float32 [3, 256], P(None, 'chan'), may hold values from 0.25 to 1.75
- norm_bias: float32 [3, 256], P(None, 'chan'), may hold values from -3 to 3
- time_bias: float32 [256], P('chan'), may hold values from -4 to 4
- local_nbr: int32 [1024, 6], P('blocks'), may hold values from 0 to 32, as said below
- face_links: int32 [32, 32, 2], P('blocks'), may hold values from 0 to 192, as said below
- coarse_send: int32 [32, 32, 2], P('blocks'), may hold values from 0 to 32, as said below
- coarse_recv: int32 [32, 32, 2], P('blocks'), may hold values from 0 to 64, as said below
Outputs:
- updated: bfloat16 [1024, 256, 512], P('blocks', 'chan')
Inputs may be any that keep to these rules, and one draw needn't show every extreme that they name: local_nbr[s * 32 + b, f] is a slot of device s other than b, or 32 for none; the relation is mutual across faces f and f XOR 1. face_links[s, p, k] = 6 b + f names slot b and face f of device s for the k-th link of the pair s, p, and face_links[p, s, k] names the block and face f XOR 1 on p; 192 marks an unused link, at the same k on both sides and always for p = s; no face of a block appears twice on a device or also has a neighbour in local_nbr; some pair uses all 2 links. coarse_send[s, p, k] is a slot of device s sent to device p, or 32 for an unused place; every slot of every device appears exactly once; some pair uses all 2 places. coarse_recv[p, s, k] = 8 t + o is a tile and octant of device p, and equals 64 exactly where coarse_send[s, p, k] is 32; no code appears twice on a device; some device fills all 64 codes.
All inputs are finite; a program needn't handle non-finite values.
Results may differ from a plain program's by a relative error of at most 0.0029.
Values may be sent and summed in bfloat16 or wider, within the bound.
No kernel may reach another device: no remote copies, remote signals or barrier semaphores. Data moves between devices by JAX's collectives and lax.ppermute only.
A program may use at most 320 MiB of HBM per device.

v0:
```python
import jax
import jax.numpy as jnp
import numpy as np
from jax import lax
from jax.sharding import PartitionSpec as P

GROUP = 8
SIDE = 8
TILE_DEV = 8


EPS = 1e-05
OPPOSITE = (1, 0, 3, 2, 5, 4)


def face_tables():
    cube = SIDE * SIDE * SIDE
    places = np.arange(cube)
    coords = (places // (SIDE * SIDE), places // SIDE % SIDE, places % SIDE)
    extract = np.zeros((6, cube, SIDE * SIDE), np.float32)
    on_face = np.zeros((6, cube), bool)
    for which_face in range(6):
        along = which_face // 2
        others = [coords[k] for k in range(3) if k != along]
        plane_index = SIDE * others[0] + others[1]
        edge = 0 if which_face % 2 == 0 else SIDE - 1
        chosen = coords[along] == edge
        extract[which_face, places[chosen], plane_index[chosen]] = 1.0
        on_face[which_face] = chosen
    return (extract, on_face)


def coarse_tables():
    cube = SIDE * SIDE * SIDE
    half_side = SIDE // 2
    coarse_cube = half_side**3
    places = np.arange(cube)
    big_x, big_y, big_z = (places // (SIDE * SIDE), places // SIDE % SIDE, places % SIDE)
    lifting = np.zeros((coarse_cube, cube), np.float32)
    lifting[big_x // 2 * half_side * half_side + big_y // 2 * half_side + big_z // 2, places] = 1.0
    octant_of = big_x // half_side * 4 + big_y // half_side * 2 + big_z // half_side
    inner = (
        big_x % half_side * half_side * half_side
        + big_y % half_side * half_side
        + big_z % half_side
    )
    placing = np.zeros((8, coarse_cube, cube), np.float32)
    placing[octant_of, inner, places] = 1.0
    return (lifting, placing)


def extract_layers(volume):
    extract, on_face = face_tables()
    table = jnp.asarray(extract, jnp.bfloat16)
    return jnp.einsum("bcv,fvu->bfcu", volume, table, preferred_element_type=jnp.float32).astype(
        volume.dtype
    )


def add_taps(volume, border, weights):
    extract, on_face = face_tables()
    cube = volume.shape[2]
    strides = (SIDE * SIDE, SIDE, 1)
    taps = [volume]
    for which_face in range(6):
        step = strides[which_face // 2]
        blank = jnp.zeros(volume.shape[:2] + (step,), volume.dtype)
        if which_face % 2 == 1:
            shifted = jnp.concatenate([volume[:, :, step:], blank], axis=2)
        else:
            shifted = jnp.concatenate([blank, volume[:, :, : cube - step]], axis=2)
        mask = jnp.asarray(on_face[which_face])
        if border is None:
            moved = jnp.where(mask[None, None, :], jnp.zeros((), volume.dtype), shifted)
        else:
            table = jnp.asarray(extract[which_face], jnp.bfloat16)
            placed = jnp.einsum(
                "bcu,vu->bcv", border[:, which_face], table, preferred_element_type=jnp.float32
            ).astype(volume.dtype)
            moved = jnp.where(mask[None, None, :], placed, shifted)
        taps.append(moved)
    stacked = jnp.stack(taps, axis=1)
    return jnp.einsum("toc,btcv->bov", weights, stacked, preferred_element_type=jnp.float32)


def inverse_index(indices, extent, default_value):
    flat_codes = indices.reshape(-1)
    lookup = jnp.full((extent + 1,), default_value, jnp.int32)
    lookup = lookup.at[flat_codes].set(jnp.arange(flat_codes.shape[0], dtype=jnp.int32))
    return lookup[:extent]


def build_border(volume, remote, local_src, remote_src):
    blocks_here, channels = (volume.shape[0], volume.shape[1])
    plane = SIDE * SIDE
    layers = extract_layers(volume).reshape(blocks_here * 6, channels, plane)
    blank = jnp.zeros((1, channels, plane), volume.dtype)
    nearby = jnp.concatenate([layers, blank], axis=0)[local_src]
    distant = jnp.concatenate([remote, blank], axis=0)[remote_src]
    return (nearby + distant).reshape(blocks_here, 6, channels, plane)


def group_terms(values):
    rows, channels, cells = values.shape
    grouped = values.reshape(rows, channels // GROUP, GROUP, cells)
    return (jnp.sum(grouped, axis=(0, 2, 3)), jnp.sum(grouped * grouped, axis=(0, 2, 3)))


def normalize_silu(values, totals, squares, entries, gain_row, bias_row):
    average = totals / entries
    spread = squares / entries - average * average
    inverse = lax.rsqrt(spread + EPS)
    average_full = jnp.repeat(average, GROUP)
    inverse_full = jnp.repeat(inverse, GROUP) * gain_row
    return jax.nn.silu(
        (values - average_full[None, :, None]) * inverse_full[None, :, None]
        + bias_row[None, :, None]
    )


def global_sums(stacked):
    return lax.psum(stacked, "blocks")


def coarse_route(buffer):
    return lax.all_to_all(buffer, "blocks", split_axis=0, concat_axis=0, tiled=True)


def mixing_conv(activation, remote, local_src, remote_src, weights):
    if remote is None:
        return add_taps(lax.all_gather(activation, "chan", axis=1, tiled=True), None, weights)
    act_piece = lax.all_gather(activation, "chan", axis=1, tiled=True)
    remote_piece = lax.all_gather(remote, "chan", axis=1, tiled=True)
    border = build_border(act_piece, remote_piece, local_src, remote_src)
    return add_taps(act_piece, border, weights)


def face_conv(activation, weights, local_src, remote_src, face_links):
    blocks_here, channels, voxels = activation.shape
    plane = SIDE * SIDE
    layers = extract_layers(activation).reshape(blocks_here * 6, channels * plane)
    padded = jnp.concatenate([layers, jnp.zeros((1, layers.shape[1]), activation.dtype)], axis=0)
    outgoing = padded[face_links[0]]
    incoming = lax.all_to_all(outgoing, "blocks", split_axis=0, concat_axis=0, tiled=True)
    remote = incoming.reshape(-1, channels, plane)
    return mixing_conv(activation, remote, local_src, remote_src, weights)


def local(
    feats,
    conv_weights,
    norm_gain,
    norm_bias,
    time_bias,
    local_nbr,
    face_links,
    coarse_send,
    coarse_recv,
):
    blocks_here, channels, voxels = feats.shape
    half_side = SIDE // 2
    coarse_cells = half_side**3
    devices = lax.axis_size("blocks")
    fine_entries = float(devices * blocks_here * voxels * GROUP)
    coarse_entries = float(devices * blocks_here * coarse_cells * GROUP)
    lifting_np, placing_np = coarse_tables()
    lifting = jnp.asarray(lifting_np, jnp.bfloat16)
    placing = jnp.asarray(placing_np, jnp.bfloat16)
    pooling = jnp.asarray(lifting_np.T * 0.125, jnp.bfloat16)
    opposite = jnp.array(OPPOSITE, jnp.int32)
    local_src = jnp.where(
        local_nbr < blocks_here, local_nbr * 6 + opposite[None, :], blocks_here * 6
    ).reshape(-1)
    remote_src = inverse_index(face_links, blocks_here * 6, face_links.size)
    tile_src = inverse_index(coarse_recv, 8 * TILE_DEV, coarse_recv.size)
    block_src = inverse_index(coarse_send, blocks_here, coarse_send.size)
    filled = (tile_src < coarse_recv.size).astype(jnp.float32)
    widened = feats.astype(jnp.float32)
    pooled = jnp.einsum("bcv,vu->bcu", feats, pooling, preferred_element_type=jnp.float32).astype(
        jnp.bfloat16
    )
    fine_totals, fine_squares = group_terms(widened)
    summed = global_sums(jnp.stack([fine_totals, fine_squares]))
    first_act = normalize_silu(
        widened, summed[0], summed[1], fine_entries, norm_gain[0], norm_bias[0]
    ).astype(jnp.bfloat16)
    hidden = (
        face_conv(first_act, conv_weights[0], local_src, remote_src, face_links)
        + time_bias[None, :, None]
    )
    hidden_totals, hidden_squares = group_terms(hidden)
    middle = global_sums(jnp.stack([hidden_totals, hidden_squares]))
    second_act = normalize_silu(
        hidden, middle[0], middle[1], fine_entries, norm_gain[1], norm_bias[1]
    ).astype(jnp.bfloat16)
    branch = face_conv(second_act, conv_weights[1], local_src, remote_src, face_links)
    blank_row = jnp.zeros((1, channels * coarse_cells), jnp.bfloat16)
    outgoing = jnp.concatenate([pooled.reshape(blocks_here, -1), blank_row], axis=0)[coarse_send[0]]
    arrived = coarse_route(outgoing).reshape(-1, channels * coarse_cells)
    octants = (
        jnp.concatenate([arrived, blank_row], axis=0)[tile_src]
        .reshape(8 * TILE_DEV, channels, coarse_cells)
        .astype(jnp.float32)
    )
    tile_totals, tile_squares = group_terms(octants)
    late_sums = global_sums(jnp.stack([tile_totals, tile_squares]))
    coarse_totals, coarse_squares = (late_sums[0], late_sums[1])
    third_act = normalize_silu(
        octants, coarse_totals, coarse_squares, coarse_entries, norm_gain[2], norm_bias[2]
    )
    third_act = (third_act * filled[:, None, None]).astype(jnp.bfloat16)
    grouped_octants = third_act.reshape(TILE_DEV, 8, channels, coarse_cells)
    tile_cubes = jnp.einsum(
        "tocu,ouv->tcv", grouped_octants, placing, preferred_element_type=jnp.float32
    ).astype(jnp.bfloat16)
    coarse = mixing_conv(tile_cubes, None, None, None, conv_weights[2]).astype(jnp.bfloat16)
    pieces = jnp.einsum(
        "tcv,ouv->tocu", coarse, placing, preferred_element_type=jnp.float32
    ).astype(jnp.bfloat16)
    pieces = pieces.reshape(8 * TILE_DEV, channels * coarse_cells)
    returning = jnp.concatenate([pieces, blank_row], axis=0)[coarse_recv[0]]
    returned = coarse_route(returning).reshape(-1, channels * coarse_cells)[block_src]
    lifted = jnp.einsum(
        "bcu,uv->bcv",
        returned.reshape(blocks_here, channels, coarse_cells),
        lifting,
        preferred_element_type=jnp.float32,
    )
    return (widened + branch + lifted).astype(jnp.bfloat16)


def solution(mesh):
    in_specs = (
        P("blocks", "chan", None),
        P(None, None, "chan", None),
        P(None, "chan"),
        P(None, "chan"),
        P("chan"),
        P("blocks", None),
        P("blocks", None, None),
        P("blocks", None, None),
        P("blocks", None, None),
    )
    out_specs = P("blocks", "chan", None)
    return jax.shard_map(local, mesh=mesh, in_specs=in_specs, out_specs=out_specs, check_vma=False)
```

profile of v0, /device:TPU:1, one launch (start us, length us, event | category | flops | bytes accessed | tf_op | source)
XLA Modules:
  0.0 771.8 jit_solution(18066224837224306198)
XLA Ops:
  6.5 2.3 convert_reduce_fusion
  9.3 64.8 %psum.21 = f32[2,8]{1,0:T(2,128)S(1)} all-reduce(f32[2,8]{1,0:T(2,128)S(1)} %pad_maximum_fusion), channel_id=1, replica_groups=mesh['blocks'=32,'chan'=4] {'blocks'}, use_global_device_ids=true, to_apply=%region_4.5 | all-reduce | flops 16 | bytes 128 | tf_op jit(solution)/shard_map/psum | solution.py:122
  75.9 3.0 fusion.12
  78.9 3.7 convert_bitcast_fusion.1
  82.6 5.1 reshape.349
  88.0 2.8 concatenate.82
  90.8 3.2 gather_fusion.1
  94.3 20.0 %all_to_all.20 = bf16[32,2,4096]{2,1,0:T(2,128)(2,1)} all-to-all(bf16[32,2,4096]{2,1,0:T(2,128)(2,1)S(1)} %reshape.375), channel_id=1, replica_groups=mesh['blocks'=32,'chan'=4] {'blocks'}, dimensions={0} | all-to-all | bytes 1048576 | tf_op jit(solution)/shard_map/all_to_all | solution.py:144
  114.3 2.3 reshape.350
  124.0 4.0 all-to-all-start.2
  130.7 9.0 %all-to-all-done.2 = bf16[32,2,4096]{2,1,0:T(2,128)(2,1)S(1)} async-done(((bf16[32,2,4096]{2,1,0:T(2,128)(2,1)}), bf16[32,2,4096]{2,1,0:T(2,128)(2,1)S(1)}, u32[]{:S(2)}, u32[]{:S(2)}) %all-to-all-start.2) | async-done | bytes 524320 | tf_op jit(solution)/shard_map/all_to_all | solution.py:126
  141.5 23.0 %all-gather.8.cloned.1.call-done = bf16[64,256,64]{2,0,1:T(8,128)(2,1)} async-done(((bf16[64,64,64]{2,0,1:T(8,128)(2,1)}), bf16[64,256,64]{2,0,1:T(8,128)(2,1)}) %all-gather.8.cloned.1.call-update) | async-done | bytes 2097168 | tf_op jit(solution)/shard_map/all_gather | solution.py:133
  164.4 5.9 copy.127
  172.1 7.8 %gather_fusion.2 = bf16[192,256,64]{1,2,0:T(8,128)(2,1)} fusion(bf16[65,256,64]{1,2,0:T(8,128)(2,1)S(1)} %concatenate.83, s32[1024]{0:T(1024)S(1)} %get-tuple-element.39), kind=kCustom, calls=%fused_computation.2 | custom fusion | bytes 12583680 | tf_op jit(solution)/shard_map/gather | solution.py:99
  179.9 69.7 %all-gather.6.cloned.1.call-done = bf16[32,256,512]{2,1,0:T(8,128)(2,1)} async-done(((bf16[32,64,512]{2,1,0:T(8,128)(2,1)}), bf16[32,256,512]{2,1,0:T(8,128)(2,1)}) %all-gather.6.cloned.1.call-update) | async-done | bytes 8388624 | tf_op jit(solution)/shard_map/all_gather | solution.py:132
  249.6 9.2 %fusion.20 = bf16[32,256,6,64]{1,3,2,0:T(8,128)(2,1)S(1)} fusion(bf16[6,512,64,1]{1,2,0,3:T(8,128)(2,1)S(1)} %copy-done.26, bf16[32,256,512]{2,1,0:T(8,128)(2,1)} %all-gather.6.cloned.1.call-done), kind=kOutput, calls=%fused_computation.55 | convolution fusion | flops 3224371200 | bytes 15073280 | tf_op jit(solution)/shard_map/bcv,fvu->bfcu/dot_general | solution.py:55
  258.8 3.3 concatenate.81
  262.1 10.6 %gather_fusion = bf16[192,256,64]{1,2,0:T(8,128)(2,1)} fusion(bf16[193,256,64]{1,2,0:T(8,128)(2,1)} %concatenate.81, s32[1024]{0:T(1024)S(1)} %get-tuple-element.40), kind=kCustom, calls=%fused_computation | custom fusion | bytes 12583680 | tf_op jit(solution)/shard_map/gather | solution.py:98
  272.7 10.9 %add.261 = bf16[192,256,64]{1,2,0:T(8,128)(2,1)} add(bf16[192,256,64]{1,2,0:T(8,128)(2,1)} %gather_fusion, bf16[192,256,64]{1,2,0:T(8,128)(2,1)} %gather_fusion.2) | non-fusion elementwise | flops 3145728 | bytes 18874368 | tf_op jit(solution)/shard_map/add | solution.py:100
  283.6 14.7 %fusion.63 = (bf16[32,256,448]{2,1,0:T(8,128)(2,1)}, bf16[32,256,448]{2,1,0:T(8,128)(2,1)}) fusion(bf16[32,256,512]{2,1,0:T(8,128)(2,1)} %all-gather.6.cloned.1.call-done), kind=kLoop, calls=%fused_computation.154 | loop fusion | bytes 29360128 | tf_op jit(solution)/shard_map/slice | solution.py:69
  298.3 7.7 bitcast_dynamic-update-slice_fusion.13
  306.0 11.0 %bitcast_dynamic-update-slice_fusion.12 = bf16[32,7,256,512]{3,2,0,1:T(8,128)(2,1)} fusion(bf16[32,7,256,512]{3,2,0,1:T(8,128)(2,1)} %bitcast_dynamic-update-slice_fusion.13, bf16[32,256,448]{2,1,0:T(8,128)(2,1)} %get-tuple-element.24, pred[512]{0:T(512)(128)(4,1)S(1)} %copy-done.22, bf16[512,64,1]{0,1,2:T(8,128)(2,1)S(1)} %copy-done.39, ...), kind=kOutput, calls=%fused_computation.29 | convolution fusion | flops 545259520 | bytes 17891840 | tf_op jit(solution)/shard_map/bcu,vu->bcv/dot_general | solution.py:77
  317.1 6.1 bitcast_dynamic-update-slice_fusion.11
  323.2 6.2 fusion.62
  329.5 10.9 %bitcast_dynamic-update-slice_fusion.10 = bf16[32,7,256,512]{3,2,0,1:T(8,128)(2,1)} fusion(bf16[32,7,256,512]{3,2,0,1:T(8,128)(2,1)} %bitcast_dynamic-update-slice_fusion.11, bf16[32,256,504]{2,1,0:T(8,128)(2,1)} %get-tuple-element.22, pred[512]{0:T(512)(128)(4,1)S(1)} %copy-done.20, bf16[512,64,1]{0,1,2:T(8,128)(2,1)S(1)} %copy-done.35, ...), kind=kOutput, calls=%fused_computation.27 | convolution fusion | flops 545259520 | bytes 17891840 | tf_op jit(solution)/shard_map/bcu,vu->bcv/dot_general | solution.py:77
  340.3 6.2 bitcast_dynamic-update-slice_fusion.9
  346.5 6.2 fusion.61
  352.7 10.9 %bitcast_dynamic-update-slice_fusion.8 = bf16[32,7,256,512]{3,2,0,1:T(8,128)(2,1)} fusion(bf16[32,7,256,512]{3,2,0,1:T(8,128)(2,1)} %bitcast_dynamic-update-slice_fusion.9, bf16[32,256,511]{2,1,0:T(8,128)(2,1)} %get-tuple-element.20, pred[512]{0:T(512)(128)(4,1)S(1)} %copy-done.18, bf16[512,64,1]{0,1,2:T(8,128)(2,1)S(1)} %copy-done.31, ...), kind=kOutput, calls=%fused_computation.25 | convolution fusion | flops 545259520 | bytes 17891840 | tf_op jit(solution)/shard_map/bcu,vu->bcv/dot_general | solution.py:77
  363.6 5.9 bitcast_dynamic-update-slice_fusion.7
  369.6 23.8 %fusion.19 = (f32[64]{0:T(128)S(1)}, f32[64]{0:T(128)S(1)}, f32[32,512,64,1]{1,2,0,3:T(8,128)}) fusion(f32[64]{0:T(128)S(1)} %copy-done.16, bf16[32,7,256,512]{3,2,0,1:T(8,128)(2,1)} %bitcast_dynamic-update-slice_fusion.7, bf16[3,7,64,256]{3,2,1,0:T(8,128)(2,1)S(1)} %copy-done.6), kind=kOutput, calls=%fused_computation.54 | convolution fusion | flops 3762290688 | bytes 63144960 | tf_op jit(solution)/shard_map/toc,btcv->bov/dot_general | solution.py:83
  394.8 62.8 %all-reduce.27 = (f32[2,8]{1,0:T(2,128)S(1)}, f32[2,8]{1,0:T(2,128)S(1)}) all-reduce(f32[2,8]{1,0:T(2,128)S(1)} %pad_maximum_fusion.2, f32[2,8]{1,0:T(2,128)S(1)} %pad_maximum_fusion.1), channel_id=1, replica_groups=mesh['blocks'=32,'chan'=4] {'blocks'}, use_global_device_ids=true, to_apply=%region_16.17 | all-reduce | flops 32 | bytes 256 | tf_op jit(solution)/shard_map/psum | solution.py:122
  458.1 2.9 fusion.29
  461.2 3.6 fusion.18
  464.8 3.7 convert_bitcast_fusion
  468.5 5.2 reshape.354
  476.5 19.3 %all_to_all.21 = bf16[32,2,4096]{2,1,0:T(2,128)(2,1)S(1)} all-to-all(bf16[32,2,4096]{2,1,0:T(2,128)(2,1)S(1)} %reshape.399), channel_id=1, replica_groups=mesh['blocks'=32,'chan'=4] {'blocks'}, dimensions={0} | all-to-all | bytes 1048576 | tf_op jit(solution)/shard_map/all_to_all | solution.py:144
  499.0 3.2 bitcast_dynamic-update-slice_fusion.20
  503.5 2.5 bitcast_dynamic-update-slice_fusion.19
  506.0 1.8 bitcast_dynamic-update-slice_fusion.18
  509.0 2.6 bitcast_dynamic-update-slice_fusion.17
  511.6 1.8 bitcast_dynamic-update-slice_fusion.16
  514.7 2.5 bitcast_dynamic-update-slice_fusion.15
  519.0 8.6 %fusion.28 = bf16[8,8,64,64]{3,2,1,0:T(8,128)(2,1)S(1)} fusion(bf16[8,64,512,1]{2,1,0,3:T(8,128)(2,1)S(1)} %copy-done.7, bf16[8,7,256,512]{3,2,0,1:T(8,128)(2,1)} %bitcast_dynamic-update-slice_fusion.14, bf16[3,7,64,256]{3,2,1,0:T(8,128)(2,1)S(1)} %copy-done.6), kind=kOutput, calls=%fused_computation.70 | convolution fusion | flops 1208483840 | bytes 15958016 | tf_op jit(solution)/shard_map/tcv,ouv->tocu/dot_general | solution.py:217
  530.5 4.2 all-to-all-start.3
  535.5 8.3 %all-gather.12.cloned.1.call-done = bf16[64,256,64]{2,0,1:T(8,128)(2,1)} async-done(((bf16[64,64,64]{2,0,1:T(8,128)(2,1)}), bf16[64,256,64]{2,0,1:T(8,128)(2,1)}) %all-gather.12.cloned.1.call-update) | async-done | bytes 2097168 | tf_op jit(solution)/shard_map/all_gather | solution.py:133
  543.8 5.9 copy.136
  551.5 7.8 %gather_fusion.5 = bf16[192,256,64]{1,2,0:T(8,128)(2,1)} fusion(bf16[65,256,64]{1,2,0:T(8,128)(2,1)S(1)} %concatenate.92, s32[1024]{0:T(1024)S(1)} %get-tuple-element.39), kind=kCustom, calls=%fused_computation.5 | custom fusion | bytes 12583680 | tf_op jit(solution)/shard_map/gather | solution.py:99
  560.7 2.7 fusion.67
  563.4 65.4 %all-gather.10.cloned.1.call-done = bf16[32,256,512]{2,1,0:T(8,128)(2,1)} async-done(((bf16[32,64,512]{2,1,0:T(8,128)(2,1)}), bf16[32,256,512]{2,1,0:T(8,128)(2,1)}) %all-gather.10.cloned.1.call-update) | async-done | bytes 8388624 | tf_op jit(solution)/shard_map/all_gather | solution.py:132
  628.8 9.1 %fusion.23 = bf16[32,256,6,64]{1,3,2,0:T(8,128)(2,1)S(1)} fusion(bf16[6,512,64,1]{1,2,0,3:T(8,128)(2,1)S(1)} %copy-done.28, bf16[32,256,512]{2,1,0:T(8,128)(2,1)} %all-gather.10.cloned.1.call-done), kind=kOutput, calls=%fused_computation.56 | convolution fusion | flops 3224371200 | bytes 15073280 | tf_op jit(solution)/shard_map/bcv,fvu->bfcu/dot_general | solution.py:55
  638.0 3.3 concatenate.90
  641.2 10.9 %gather_fusion.3 = bf16[192,256,64]{1,2,0:T(8,128)(2,1)} fusion(bf16[193,256,64]{1,2,0:T(8,128)(2,1)} %concatenate.90, s32[1024]{0:T(1024)} %copy-done.11), kind=kCustom, calls=%fused_computation.3 | custom fusion | bytes 12583680 | tf_op jit(solution)/shard_map/gather | solution.py:98
  652.1 10.9 %add.271 = bf16[192,256,64]{1,2,0:T(8,128)(2,1)} add(bf16[192,256,64]{1,2,0:T(8,128)(2,1)} %gather_fusion.3, bf16[192,256,64]{1,2,0:T(8,128)(2,1)} %gather_fusion.5) | non-fusion elementwise | flops 3145728 | bytes 18874368 | tf_op jit(solution)/shard_map/add | solution.py:100
  663.0 7.5 bitcast_dynamic-update-slice_fusion.6
  670.6 9.9 %fusion.60 = (bf16[32,256,448]{2,1,0:T(8,128)(2,1)S(1)}, bf16[32,256,448]{2,1,0:T(8,128)(2,1)S(1)}) fusion(bf16[32,256,512]{2,1,0:T(8,128)(2,1)} %all-gather.10.cloned.1.call-done), kind=kLoop, calls=%fused_computation.151 | loop fusion | bytes 29360128 | tf_op jit(solution)/shard_map/slice | solution.py:69
  680.5 9.0 %bitcast_dynamic-update-slice_fusion.5 = bf16[32,7,256,512]{3,2,0,1:T(8,128)(2,1)} fusion(bf16[32,7,256,512]{3,2,0,1:T(8,128)(2,1)} %bitcast_dynamic-update-slice_fusion.6, bf16[32,256,448]{2,1,0:T(8,128)(2,1)S(1)} %get-tuple-element.18, pred[512]{0:T(512)(128)(4,1)S(1)} %copy-done.22, bf16[512,64,1]{0,1,2:T(8,128)(2,1)S(1)} %copy-done.40, ...), kind=kOutput, calls=%fused_computation.22 | convolution fusion | flops 545259520 | bytes 16843264 | tf_op jit(solution)/shard_map/bcu,vu->bcv/dot_general | solution.py:77
  689.5 6.1 bitcast_dynamic-update-slice_fusion.4
  695.6 6.5 fusion.59
  702.1 10.9 %bitcast_dynamic-update-slice_fusion.3 = bf16[32,7,256,512]{3,2,0,1:T(8,128)(2,1)} fusion(bf16[32,7,256,512]{3,2,0,1:T(8,128)(2,1)} %bitcast_dynamic-update-slice_fusion.4, bf16[32,256,504]{2,1,0:T(8,128)(2,1)} %get-tuple-element.16, pred[512]{0:T(512)(128)(4,1)S(1)} %copy-done.20, bf16[512,64,1]{0,1,2:T(8,128)(2,1)S(1)} %copy-done.36, ...), kind=kOutput, calls=%fused_computation.20 | convolution fusion | flops 545259520 | bytes 17891840 | tf_op jit(solution)/shard_map/bcu,vu->bcv/dot_general | solution.py:77
  713.0 6.0 bitcast_dynamic-update-slice_fusion.2
  719.0 6.2 fusion.58
  725.2 9.2 %bitcast_dynamic-update-slice_fusion.1 = bf16[32,7,256,512]{3,2,0,1:T(8,128)(2,1)} fusion(bf16[32,7,256,512]{3,2,0,1:T(8,128)(2,1)} %bitcast_dynamic-update-slice_fusion.2, bf16[32,256,511]{2,1,0:T(8,128)(2,1)S(1)} %get-tuple-element.14, pred[512]{0:T(512)(128)(4,1)S(1)} %copy-done.18, bf16[512,64,1]{0,1,2:T(8,128)(2,1)S(1)} %copy-done.32, ...), kind=kOutput, calls=%fused_computation.18 | convolution fusion | flops 545259520 | bytes 17875456 | tf_op jit(solution)/shard_map/bcu,vu->bcv/dot_general | solution.py:77
  734.4 6.0 bitcast_dynamic-update-slice_fusion
  740.4 24.3 %fusion.14 = bf16[32,64,512]{2,1,0:T(8,128)(2,1)} fusion(f32[32,64,512]{2,1,0:T(8,128)} %fusion.67, bf16[32,64,512]{2,1,0:T(8,128)(2,1)S(1)} %copy-done.2, bf16[32,7,256,512]{3,2,0,1:T(8,128)(2,1)} %bitcast_dynamic-update-slice_fusion, bf16[3,7,64,256]{3,2,1,0:T(8,128)(2,1)S(1)} %copy-done.6), kind=kOutput, calls=%fused_computation.45 | convolution fusion | flops 3762290688 | bytes 67338240 | tf_op jit(solution)/shard_map/toc,btcv->bov/dot_general | solution.py:83
  (214 shorter events, 36.5 us)
Async XLA Ops:
  6.5 72.3 %copy-start.25 = (bf16[6,512,64,1]{1,2,0,3:T(8,128)(2,1)S(1)}, bf16[6,512,64,1]{1,2,0,3:T(8,128)(2,1)}, u32[]{:S(2)}) copy-start(bf16[6,512,64,1]{1,2,0,3:T(8,128)(2,1)} %constant.166) | copy-start | bytes 1179652
  6.5 157.9 %all-gather.8.cloned.1.call-start = ((), (), s32[]{:S(2)}) async-start(), calls=%async_computation.5 | async-start | bytes 5242880 | tf_op jit(solution)/shard_map/all_gather | solution.py:133
  78.8 8.9 %copy-start.3 = (bf16[32,64,512]{2,1,0:T(8,128)(2,1)}, bf16[32,64,512]{2,1,0:T(8,128)(2,1)S(1)}, u32[]{:S(2)}) copy-start(bf16[32,64,512]{2,1,0:T(8,128)(2,1)S(1)} %fusion.12) | copy-start | bytes 6291460
  78.9 8.9 %copy-start.12 = (s32[1,32,2]{1,2,0:T(2,128)S(1)}, s32[1,32,2]{1,2,0:T(2,128)}, u32[]{:S(2)}) copy-start(s32[1,32,2]{1,2,0:T(2,128)} %param.53) | copy-start | bytes 772
  90.8 28.3 %copy-start.14 = (s32[1,32,2]{1,2,0:T(2,128)S(1)}, s32[1,32,2]{1,2,0:T(2,128)}, u32[]{:S(2)}) copy-start(s32[1,32,2]{1,2,0:T(2,128)} %param.54) | copy-start | bytes 772
  90.8 28.5 %copy-start.13 = (s32[1,32,2]{1,2,0:T(2,128)S(1)}, s32[1,32,2]{1,2,0:T(2,128)}, u32[]{:S(2)}) copy-start(s32[1,32,2]{1,2,0:T(2,128)} %param.55) | copy-start | bytes 772
  90.8 28.7 %copy-start.1 = (bf16[32,64,512]{2,1,0:T(8,128)(2,1)S(1)}, bf16[32,64,512]{2,1,0:T(8,128)(2,1)}, u32[]{:S(2)}) copy-start(bf16[32,64,512]{2,1,0:T(8,128)(2,1)} %param.47) | copy-start | bytes 6291460
  90.8 28.8 %copy-start.10 = (bf16[512,64,1]{0,1,2:T(8,128)(2,1)S(1)}, bf16[512,64,1]{0,1,2:T(8,128)(2,1)}, u32[]{:S(2)}) copy-start(bf16[512,64,1]{0,1,2:T(8,128)(2,1)} %constant.173) | copy-start | bytes 196612
  118.3 131.3 %all-gather.6.cloned.1.call-start = ((), (), s32[]{:S(2)}) async-start(), calls=%async_computation.4 | async-start | bytes 10485760 | tf_op jit(solution)/shard_map/all_gather | solution.py:132
  119.1 9.2 %copy-start.15 = (s32[32,6]{0,1:T(8,128)S(1)}, s32[32,6]{0,1:T(8,128)}, u32[]{:S(2)}) copy-start(s32[32,6]{0,1:T(8,128)} %param.52) | copy-start | bytes 2308
  119.1 9.2 %copy-start.24 = (s32[6]{0:T(128)S(1)}, s32[6]{0:T(128)}, u32[]{:S(2)}) copy-start(s32[6]{0:T(128)} %constant.48.clone) | copy-start | bytes 76
  124.0 15.7 %all-to-all-start.2 = ((bf16[32,2,4096]{2,1,0:T(2,128)(2,1)}), bf16[32,2,4096]{2,1,0:T(2,128)(2,1)S(1)}, u32[]{:S(2)}, u32[]{:S(2)}) async-start(bf16[32,2,4096]{2,1,0:T(2,128)(2,1)} %reshape.415), calls=%async_computation.2 | async-start | bytes 1048576 | tf_op jit(solution)/shard_map/all_to_all | solution.py:126
  128.0 371.0 %all-gather.14.cloned.1.call-start = ((), (), s32[]{:S(2)}) async-start(), calls=%async_computation.8 | async-start | bytes 2621440 | tf_op jit(solution)/shard_map/all_gather | solution.py:131
  130.7 131.4 %copy-start.11 = (s32[1024]{0:T(1024)}, s32[1024]{0:T(1024)S(1)}, u32[]{:S(2)}) copy-start(s32[1024]{0:T(1024)S(1)} %get-tuple-element.40) | copy-start | bytes 12292
  172.1 77.5 %copy-start.26 = (bf16[6,512,64,1]{1,2,0,3:T(8,128)(2,1)S(1)}, bf16[6,512,64,1]{1,2,0,3:T(8,128)(2,1)}, u32[]{:S(2)}) copy-start(bf16[6,512,64,1]{1,2,0,3:T(8,128)(2,1)} %constant.166) | copy-start | bytes 1179652
  298.3 7.7 copy-start.22
  298.3 7.7 copy-start.39
  298.3 18.7 %slice-start.4 = ((s8[8388608]{0:T(1024)(128)(4,1)}), s8[4194304]{0:T(1024)(128)(4,1)S(1)}, s32[]{:S(2)}) async-start(s8[8388608]{0:T(1024)(128)(4,1)} %bitcast.321), calls=%async_computation.13 | async-start | bytes 8388608
  306.0 11.0 %slice-start.5 = ((s8[8388608]{0:T(1024)(128)(4,1)}), s8[4194304]{0:T(1024)(128)(4,1)S(1)}, s32[]{:S(2)}) async-start(s8[8388608]{0:T(1024)(128)(4,1)} %bitcast.321), calls=%async_computation.14 | async-start | bytes 8388608
  306.0 11.0 %copy-start.21 = (pred[512]{0:T(512)(128)(4,1)S(1)}, pred[512]{0:T(512)(128)(4,1)}, u32[]{:S(2)}) copy-start(pred[512]{0:T(512)(128)(4,1)} %constant.52.clone) | copy-start | bytes 1540
  306.0 11.0 %copy-start.37 = (bf16[512,64,1]{0,1,2:T(8,128)(2,1)S(1)}, bf16[512,64,1]{0,1,2:T(8,128)(2,1)}, u32[]{:S(2)}) copy-start(bf16[512,64,1]{0,1,2:T(8,128)(2,1)} %constant.168) | copy-start | bytes 196612
  317.0 6.2 slice-start
  317.1 6.1 slice-start.1
  323.2 6.3 copy-start.20
  323.2 6.3 copy-start.35
  329.4 10.9 %copy-start.19 = (pred[512]{0:T(512)(128)(4,1)S(1)}, pred[512]{0:T(512)(128)(4,1)}, u32[]{:S(2)}) copy-start(pred[512]{0:T(512)(128)(4,1)} %constant.30.clone) | copy-start | bytes 1540
  329.4 10.9 %copy-start.33 = (bf16[512,64,1]{0,1,2:T(8,128)(2,1)S(1)}, bf16[512,64,1]{0,1,2:T(8,128)(2,1)}, u32[]{:S(2)}) copy-start(bf16[512,64,1]{0,1,2:T(8,128)(2,1)} %constant.170) | copy-start | bytes 196612
  346.5 6.2 copy-start.18
  346.5 6.2 copy-start.31
  352.7 10.9 %copy-start.17 = (pred[512]{0:T(512)(128)(4,1)S(1)}, pred[512]{0:T(512)(128)(4,1)}, u32[]{:S(2)}) copy-start(pred[512]{0:T(512)(128)(4,1)} %constant.107.clone) | copy-start | bytes 1540
  352.7 10.9 %copy-start.29 = (bf16[512,64,1]{0,1,2:T(8,128)(2,1)S(1)}, bf16[512,64,1]{0,1,2:T(8,128)(2,1)}, u32[]{:S(2)}) copy-start(bf16[512,64,1]{0,1,2:T(8,128)(2,1)} %constant.172) | copy-start | bytes 196612
  363.6 6.0 copy-start.6
  363.6 5.9 copy-start.16
  369.5 88.5 %copy-start.23 = (f32[3,64]{1,0:T(4,128)S(1)}, f32[3,64]{1,0:T(4,128)}, u32[]{:S(2)}) copy-start(f32[3,64]{1,0:T(4,128)} %param.49) | copy-start | bytes 2308
  461.0 3.8 copy-start.27
  461.0 82.9 %all-gather.12.cloned.1.call-start = ((), (), s32[]{:S(2)}) async-start(), calls=%async_computation.7 | async-start | bytes 5242880 | tf_op jit(solution)/shard_map/all_gather | solution.py:133
  464.8 3.8 copy-start.4
  498.2 130.6 %all-gather.10.cloned.1.call-start = ((), (), s32[]{:S(2)}) async-start(), calls=%async_computation.6 | async-start | bytes 10485760 | tf_op jit(solution)/shard_map/all_gather | solution.py:132
  499.0 3.2 copy-start
  514.7 4.3 copy-start.7
  519.0 9.5 %copy-start.8 = (s32[1024]{0:T(1024)S(1)}, s32[1024]{0:T(1024)}, u32[]{:S(2)}) copy-start(s32[1024]{0:T(1024)} %get-tuple-element.37) | copy-start | bytes 12292
  530.5 28.8 %all-to-all-start.3 = ((bf16[32,2,4096]{2,1,0:T(2,128)(2,1)}), bf16[32,2,4096]{2,1,0:T(2,128)(2,1)S(1)}, u32[]{:S(2)}, u32[]{:S(2)}) async-start(bf16[32,2,4096]{2,1,0:T(2,128)(2,1)} %reshape.431), calls=%async_computation.3 | async-start | bytes 1048576 | tf_op jit(solution)/shard_map/all_to_all | solution.py:126
  551.5 9.3 %copy-start.9 = (bf16[64,512,1]{1,0,2:T(8,128)(2,1)S(1)}, bf16[64,512,1]{1,0,2:T(8,128)(2,1)}, u32[]{:S(2)}) copy-start(bf16[64,512,1]{1,0,2:T(8,128)(2,1)} %constant.175) | copy-start | bytes 196612
  559.3 69.6 %copy-start.28 = (bf16[6,512,64,1]{1,2,0,3:T(8,128)(2,1)S(1)}, bf16[6,512,64,1]{1,2,0,3:T(8,128)(2,1)}, u32[]{:S(2)}) copy-start(bf16[6,512,64,1]{1,2,0,3:T(8,128)(2,1)} %constant.166) | copy-start | bytes 1179652
  670.6 9.9 %copy-start.40 = (bf16[512,64,1]{0,1,2:T(8,128)(2,1)S(1)}, bf16[512,64,1]{0,1,2:T(8,128)(2,1)}, u32[]{:S(2)}) copy-start(bf16[512,64,1]{0,1,2:T(8,128)(2,1)} %constant.167) | copy-start | bytes 196612
  680.5 9.0 %copy-start.38 = (bf16[512,64,1]{0,1,2:T(8,128)(2,1)S(1)}, bf16[512,64,1]{0,1,2:T(8,128)(2,1)}, u32[]{:S(2)}) copy-start(bf16[512,64,1]{0,1,2:T(8,128)(2,1)} %constant.168) | copy-start | bytes 196612
  689.5 6.1 slice-start.2
  689.5 6.1 slice-start.3
  695.6 6.5 copy-start.36
  702.1 10.9 %copy-start.34 = (bf16[512,64,1]{0,1,2:T(8,128)(2,1)S(1)}, bf16[512,64,1]{0,1,2:T(8,128)(2,1)}, u32[]{:S(2)}) copy-start(bf16[512,64,1]{0,1,2:T(8,128)(2,1)} %constant.170) | copy-start | bytes 196612
  718.9 6.2 copy-start.32
  725.2 9.2 %copy-start.5 = (bf16[32,256,511]{2,1,0:T(8,128)(2,1)S(1)}, bf16[32,256,511]{2,1,0:T(8,128)(2,1)}, u32[]{:S(2)}) copy-start(bf16[32,256,511]{2,1,0:T(8,128)(2,1)} %get-tuple-element.13) | copy-start | bytes 25116676
  725.2 9.2 %copy-start.30 = (bf16[512,64,1]{0,1,2:T(8,128)(2,1)S(1)}, bf16[512,64,1]{0,1,2:T(8,128)(2,1)}, u32[]{:S(2)}) copy-start(bf16[512,64,1]{0,1,2:T(8,128)(2,1)} %constant.172) | copy-start | bytes 196612
  734.4 6.0 copy-start.2
Sparse Core Ops, SparseCore 0:
  118.4 45.9 all-gather.7
  166.1 83.4 all-gather.5
  461.1 31.1 all-gather.13
  498.3 45.4 all-gather.11
  545.3 83.4 all-gather.9
where the time goes:
time: 781 us; the launch traced here: 772 us
  matrix products  187 us (24%)
  waiting for transfers between devices  176 us (23%)
  local copies, waits for them, and re-layouts  172 us (22%)
  blocking collectives  167 us (21%)
  other arithmetic  46.2 us (6%)
  between operations  14.5 us (2%)
  starting transfers between devices  8.75 us (1%)
    all_gather x2, waiting for transfers between devices, mixing_conv(): act_piece = lax.all_gather(activation, 'chan', axis=1, tiled=True)  135 us
    psum x2, blocking collectives, global_sums(): return lax.psum(stacked, 'blocks')  128 us
    dot_general x12, matrix products, add_taps(): jnp.einsum('bcu,vu->bcv', border[:, which_face], table, preferred_element...  98 us
    slice x9, local copies, waits for them, and re-layouts, add_taps(): shifted = jnp.concatenate([volume[:, :, step:], blank], axis=2)  53.4 us
    dot_general x2, matrix products, add_taps(): jnp.einsum('toc,btcv->bov', weights, stacked, preferred_element_type=jnp....  48.2 us
    all_to_all x2, blocking collectives, face_conv(): lax.all_to_all(outgoing, 'blocks', split_axis=0, concat_axis=0, tiled=True)  39.3 us
    all_gather x2, waiting for transfers between devices, mixing_conv(): remote_piece = lax.all_gather(remote, 'chan', axis=1, tiled=True)  31.3 us
    dot_general x4, matrix products, extract_layers(): jnp.einsum('bcv,fvu->bfcu', volume, table, preferred_element_type=jnp.flo...  25.8 us
  transfers between devices with their start and end apart: 7, of which 5 were waited for; matrix products, arithmetic and copies ran while one was open for 12% of the time, Pallas kernels for 0%

commit v1 on v0

v1 whole, which is shorter than its diff:
```python
import functools

import jax
import jax.numpy as jnp
import numpy as np
from jax import lax
from jax.experimental import pallas as pl
from jax.experimental.pallas import tpu as pltpu
from jax.sharding import PartitionSpec as P

GROUP = 8
SIDE = 8
VOX = 512
SLOTS = 32
DEVS = 32
QUART = 8
TILES = 2
FACES = 6 * SLOTS
CODES = 64
EPS = 1e-05
F32 = jnp.float32
BF16 = jnp.bfloat16
HIGH = lax.Precision.HIGHEST
NT = (((1,), (1,)), ((), ()))
NN = (((1,), (0,)), ((), ()))
VMEM = pl.BlockSpec(memory_space=pltpu.VMEM)
SMEM = pl.BlockSpec(memory_space=pltpu.SMEM)
LIMIT = 56 * 1024 * 1024


def tables():
    places = np.arange(VOX)
    coords = (places // 64, places // 8 % 8, places % 8)
    extract = np.zeros((7 * 64, VOX), np.float32)
    for face in range(6):
        along = face // 2
        others = [coords[k] for k in range(3) if k != along]
        chosen = coords[along] == (0 if face % 2 == 0 else SIDE - 1)
        extract[face * 64 + (8 * others[0] + others[1])[chosen], places[chosen]] = 1.0
    x, y, z = coords
    coarse = x // 2 * 16 + y // 2 * 4 + z // 2
    extract[384 + coarse, places] = 0.125
    lift = np.zeros((VOX, 64), np.float32)
    lift[places, coarse] = 1.0
    octant = x // 4 * 4 + y // 4 * 2 + z // 4
    inner = x % 4 * 16 + y % 4 * 4 + z % 4
    place = np.zeros((VOX, VOX), np.float32)
    place[places, octant * 64 + inner] = 1.0
    return extract, lift, place


def lanes(rows):
    return lax.broadcasted_iota(jnp.int32, (rows, 128), 1)


def terms(value):
    high = value.astype(BF16).astype(F32)
    rest = value - high
    middle = rest.astype(BF16).astype(F32)
    return high, middle, rest - middle


def joined(block, row):
    return (block[row + 2 : row + 3] + block[row + 1 : row + 2]) + block[row : row + 1]


def put_terms(ref, row, value):
    for k, part in enumerate(terms(value)):
        ref[row + k : row + k + 1, :] = part


def silu(u):
    return u * (1.0 / (1.0 + jnp.exp(-u)))


def group_matrix():
    row = lax.broadcasted_iota(jnp.int32, (128, 128), 0) % 64 // GROUP
    col = lax.broadcasted_iota(jnp.int32, (128, 128), 1) % 64 // GROUP
    return (row == col).astype(F32)


def group_sum(row):
    wide = jnp.broadcast_to(row, (8, 128))
    return lax.dot_general(wide, group_matrix(), NN, precision=HIGH, preferred_element_type=F32)[0:1]


def norm_rows(total, square, entries, gain):
    mean = total * (1.0 / entries)
    spread = square * (1.0 / entries) - mean * mean
    return mean, lax.rsqrt(spread + EPS) * gain


def invert(codes_ref, count, limit, out_ref, extent):
    def clear(i, _):
        out_ref[i] = 0
        return 0

    lax.fori_loop(0, extent, clear, 0)

    def mark(i, _):
        code = codes_ref[i]

        @pl.when(code < limit)
        def _():
            out_ref[code] = i + 1

        return 0

    lax.fori_loop(0, count, mark, 0)


def unpack(parts):
    left = lanes(32) < 64
    low, high = [], []
    for a, b in ((parts[0], parts[1]), (parts[2], parts[3])):
        low.append(jnp.where(left, a, pltpu.roll(b, 64, 1)))
        high.append(jnp.where(left, pltpu.roll(a, 64, 1), b))
    return jnp.concatenate(
        [jnp.concatenate(low, axis=1), jnp.concatenate(high, axis=1)], axis=0
    )


def pack(cells):
    left = lanes(32) < 64
    parts = []
    for half in range(2):
        low = cells[0:32, 128 * half : 128 * half + 128]
        high = cells[32:64, 128 * half : 128 * half + 128]
        parts.append(jnp.where(left, low, pltpu.roll(high, 64, 1)))
        parts.append(jnp.where(left, pltpu.roll(low, 64, 1), high))
    return parts


def spread_row(row):
    left = lanes(1) < 64
    parts = []
    for half in range(2):
        part = row[:, 128 * half : 128 * half + 128]
        turned = pltpu.roll(jnp.broadcast_to(part, (8, 128)), 64, 1)[0:1]
        parts.append(jnp.where(left, part, turned))
        parts.append(jnp.where(left, turned, part))
    return parts


def gather_row(rows):
    left = lanes(1) < 64
    return jnp.concatenate(
        [jnp.where(left, rows[0], rows[1]), jnp.where(left, rows[2], rows[3])], axis=1
    )


def extract_kernel(links, csend, feats, table, faces, out, pooled, stat):
    left = lanes(32) < 64

    def step(j, carry):
        s, q, ps, pq = carry
        rows = []
        for k in range(4):
            x = feats[4 * j + k]
            rows += [x, x]
            wide = x.astype(F32)
            for v in range(4):
                piece = wide[:, 128 * v : 128 * v + 128]
                s = s + piece
                q = q + piece * piece
        layers = lax.dot_general(
            table[...], jnp.concatenate(rows, axis=0), NT, preferred_element_type=F32
        )
        for k in range(4):
            for f in range(7):
                low = layers[64 * f : 64 * f + 32, 128 * k : 128 * k + 128]
                high = layers[64 * f + 32 : 64 * f + 64, 128 * k : 128 * k + 128]
                unit = jnp.where(left, low, high).astype(BF16)
                if f < 6:
                    faces[(4 * j + k) * 6 + f] = unit
                else:
                    pooled[4 * j + k] = unit
                    wide = unit.astype(F32)
                    ps = ps + wide
                    pq = pq + wide * wide
        return s, q, ps, pq

    zero = jnp.zeros((64, 128), F32)
    small = jnp.zeros((32, 128), F32)
    s, q, ps, pq = lax.fori_loop(0, 8, step, (zero, zero, small, small))
    ones = jnp.ones((8, 128), F32)

    def by_lane(sums):
        twice = jnp.concatenate([sums, sums], axis=0)
        return lax.dot_general(ones, twice, NT, precision=HIGH, preferred_element_type=F32)[0:1]

    stat[...] = jnp.zeros((32, 128), F32)
    put_terms(stat, 0, by_lane(s))
    put_terms(stat, 3, by_lane(q))
    put_terms(stat, 6, jnp.sum(ps, axis=0, keepdims=True))
    put_terms(stat, 9, jnp.sum(pq, axis=0, keepdims=True))
    sums = stat[...].astype(BF16)

    def send(p, _):
        for k in range(2):
            out[p * 5 + k] = faces[jnp.minimum(links[2 * p + k], FACES - 1)]
            out[p * 5 + 2 + k] = pooled[jnp.minimum(csend[2 * p + k], SLOTS - 1)]
        out[p * 5 + 4] = sums
        return 0

    lax.fori_loop(0, DEVS, send, 0)


def border1_kernel(nbr, links, crecv, me, faces, recv, par, o0, o1, o2, o3, inv, tinv, stat):
    invert(links, 2 * DEVS, FACES, inv, FACES)
    invert(crecv, 2 * DEVS, CODES, tinv, CODES)
    y = me[0]

    def add(s, total):
        return total + recv[s * 5 + 4].astype(F32)

    sums = lax.fori_loop(0, DEVS, add, jnp.zeros((32, 128), F32))
    fine = float(DEVS * SLOTS * VOX * GROUP)
    rough = float(DEVS * SLOTS * 64 * GROUP)
    mean1, scale1 = norm_rows(
        group_sum(joined(sums, 0)) * 0.5, group_sum(joined(sums, 3)) * 0.5, fine, par[0:1]
    )
    mean3, scale3 = norm_rows(
        group_sum(joined(sums, 6)), group_sum(joined(sums, 9)), rough, par[2:3]
    )
    bias1, bias3 = par[1:2], par[3:4]
    stat[...] = jnp.zeros((32, 128), F32)
    put_terms(stat, 0, mean1)
    put_terms(stat, 3, scale1)
    put_terms(stat, 6, bias1)
    put_terms(stat, 9, par[4:5])
    told = stat[...].astype(BF16)
    for r, o in enumerate((o0, o1, o2, o3)):
        q = (y + r) & 3

        def face(i, _):
            for f in range(6):
                at = q * 48 + i * 6 + f
                near, far = nbr[at], inv[at]
                link = jnp.maximum(far - 1, 0)
                here = faces[jnp.minimum(near, SLOTS - 1) * 6 + (f ^ 1)].astype(F32)
                there = recv[(link // 2) * 5 + link % 2].astype(F32)
                u = jnp.where(near < SLOTS, here, there)
                v = silu((u - mean1) * scale1 + bias1)
                some = jnp.logical_or(near < SLOTS, far > 0)
                o[i * 6 + f] = jnp.where(some, v, 0.0).astype(BF16)
            return 0

        lax.fori_loop(0, QUART, face, 0)

        def octant(i, _):
            for k in range(4):
                far = tinv[q * 16 + i * 4 + k]
                link = jnp.maximum(far - 1, 0)
                u = recv[(link // 2) * 5 + 2 + link % 2].astype(F32)
                v = silu((u - mean3) * scale3 + bias3)
                o[48 + i * 4 + k] = jnp.where(far > 0, v, 0.0).astype(BF16)
            return 0

        lax.fori_loop(0, 4, octant, 0)
        o[64] = told


def build_taps(act, border, taps, shift):
    wide = act.astype(F32)
    cube = wide.reshape(8, 8, 8, 256)
    taps[:, 0:256] = act
    taps[0:64, 256:512] = border(0).astype(BF16)
    taps[64:512, 256:512] = act[0:448]
    taps[0:448, 512:768] = act[64:512]
    taps[448:512, 512:768] = border(1).astype(BF16)
    low = jnp.concatenate([border(2).reshape(8, 1, 8, 256), cube[:, 0:7]], axis=1)
    taps[:, 768:1024] = low.reshape(512, 256).astype(BF16)
    high = jnp.concatenate([cube[:, 1:8], border(3).reshape(8, 1, 8, 256)], axis=1)
    taps[:, 1024:1280] = high.reshape(512, 256).astype(BF16)
    for f, amount in ((4, 1), (5, 511)):
        turned = pltpu.roll(wide, amount, 0)
        edge = border(f)
        for half in range(2):
            shift[...] = turned[:, 128 * half : 128 * half + 128]
            shift[pl.ds(0 if f == 4 else 7, 64, stride=8), :] = edge[:, 128 * half : 128 * half + 128]
            taps[:, 256 * (f + 1) + 128 * half : 256 * (f + 1) + 128 * half + 128] = shift[
                ...
            ].astype(BF16)


def fill_weights(dst, gathered, which):
    for c in range(4):
        for t in range(7):
            dst[64 * c : 64 * c + 64, 256 * t : 256 * t + 256] = gathered[c, which, t]


def conv1_kernel(
    me, v0, v1, v2, v3, u0, u1, u2, u3, weights, place, place_t,
    hid, o0, o1, o2, o3,
    units, outs, wfine, wrough, rows, taps, shift, cube, stat, sums,
):
    step = pl.program_id(0)
    y = me[0]

    @pl.when(step == 0)
    def _():
        for r, u in enumerate((u0, u1, u2, u3)):
            units[(y - r) & 3] = u[...]
        fill_weights(wfine, weights, 0)
        fill_weights(wrough, weights, 2)
        for k in range(4):
            rows[k : k + 1, :] = gather_row([joined(units[c, 64].astype(F32), 3 * k) for c in range(4)])
        sums[...] = jnp.zeros((8, 256), F32)
        stat[...] = jnp.zeros((4, 32, 128), F32)

    def unit(i):
        return unpack([units[c, i].astype(F32) for c in range(4)])

    @pl.when(step < QUART)
    def _():
        for r, v in enumerate((v0, v1, v2, v3)):
            at = pl.multiple_of(((y - r) & 3) * 64, 64)
            cube[pl.ds(at, 64), :] = v[0].astype(F32)
        x = cube[...].T
        act = silu((x - rows[0:1]) * rows[1:2] + rows[2:3]).astype(BF16)
        build_taps(act, lambda f: unit(step * 6 + f), taps, shift)
        h = lax.dot_general(taps[...], wfine[...], NT, preferred_element_type=F32) + rows[3:4]
        hid[0] = h
        total = jnp.sum(h, axis=0, keepdims=True)
        sums[0:1] += total
        sums[1:2] += jnp.sum(h * h, axis=0, keepdims=True)
        centre = (total * (1.0 / VOX)).astype(BF16).astype(F32)
        for c, part in enumerate(spread_row(centre)):
            stat[c, pl.ds(step, 1), :] = part
        deep = h.reshape(8, 8, 8, 256)
        edges = [[], []]
        for half in range(2):
            shift[...] = h[:, 128 * half : 128 * half + 128]
            for side in range(2):
                edges[side].append(shift[pl.ds(7 * side, 64, stride=8), :])
        for f in range(6):
            if f < 2:
                layer = h[448 * f : 448 * f + 64]
            elif f < 4:
                layer = deep[:, 7 * (f - 2)].reshape(64, 256)
            else:
                layer = jnp.concatenate(edges[f - 4], axis=1)
            for c, part in enumerate(pack(layer - centre)):
                outs[c, step * 6 + f] = part.astype(BF16)

    @pl.when(step >= QUART)
    def _():
        t = step - QUART
        octants = jnp.concatenate([unit(48 + 8 * t + o).astype(BF16) for o in range(8)], axis=0)
        act = lax.dot_general(place[...], octants, NN, preferred_element_type=F32).astype(BF16)
        blank = jnp.zeros((64, 256), F32)
        build_taps(act, lambda f: blank, taps, shift)
        h = lax.dot_general(taps[...], wrough[...], NT, preferred_element_type=F32).astype(BF16)
        pieces = lax.dot_general(place_t[...], h, NN, preferred_element_type=F32)
        for o in range(8):
            for c, part in enumerate(pack(pieces[64 * o : 64 * o + 64])):
                outs[c, 48 + 8 * t + o] = part.astype(BF16)

    @pl.when(step == QUART + TILES - 1)
    def _():
        totals = spread_row(sums[0:1])
        squares = spread_row(sums[1:2])
        for c in range(4):
            for k, part in enumerate(terms(totals[c])):
                stat[c, 8 + k : 9 + k, :] = part
            for k, part in enumerate(terms(squares[c])):
                stat[c, 11 + k : 12 + k, :] = part
            outs[c, 64] = stat[c].astype(BF16)
        for r, o in enumerate((o0, o1, o2, o3)):
            o[...] = outs[(y + r) & 3]


def route2_kernel(links, crecv, me, v0, v1, v2, v3, held, out, cen, stat):
    y = me[0]
    for r, v in enumerate((v0, v1, v2, v3)):
        held[(y - r) & 3] = v[...]
    total = jnp.zeros((32, 128), F32)
    for q in range(4):
        told = held[q, 64].astype(F32)
        cen[8 * q : 8 * q + 8, :] = told[0:8]
        total = total + told
    stat[...] = jnp.zeros((32, 128), F32)
    put_terms(stat, 2, joined(total, 8))
    put_terms(stat, 5, joined(total, 11))

    def send(p, _):
        for k in range(2):
            code = jnp.minimum(links[2 * p + k], FACES - 1)
            slot = code // 6
            q = slot // 8
            out[p * 5 + k] = held[q, code - 48 * q]
            stat[k : k + 1, :] = cen[pl.ds(slot, 1), :]
            place = jnp.minimum(crecv[2 * p + k], CODES - 1)
            q = place // 16
            out[p * 5 + 2 + k] = held[q, 48 + place - 16 * q]
        out[p * 5 + 4] = stat[...].astype(BF16)
        return 0

    lax.fori_loop(0, DEVS, send, 0)


def border2_kernel(
    nbr, links, csend, me, held, recv, par, o0, o1, o2, o3, inv, sinv, cen, far_cen, stat
):
    invert(links, 2 * DEVS, FACES, inv, FACES)
    invert(csend, 2 * DEVS, SLOTS, sinv, SLOTS)
    y = me[0]
    for q in range(4):
        cen[8 * q : 8 * q + 8, :] = held[q, 64].astype(F32)[0:8]

    def add(s, total):
        told = recv[s * 5 + 4].astype(F32)
        far_cen[pl.ds(2 * s, 2), :] = told[0:2]
        return total + told

    sums = lax.fori_loop(0, DEVS, add, jnp.zeros((32, 128), F32))
    fine = float(DEVS * SLOTS * VOX * GROUP)
    mean, scale = norm_rows(
        group_sum(joined(sums, 2)) * 0.5, group_sum(joined(sums, 5)) * 0.5, fine, par[0:1]
    )
    bias = par[1:2]
    stat[...] = jnp.zeros((32, 128), F32)
    put_terms(stat, 0, mean)
    put_terms(stat, 3, scale)
    put_terms(stat, 6, bias)
    told = stat[...].astype(BF16)
    for r, o in enumerate((o0, o1, o2, o3)):
        q = (y + r) & 3

        def face(i, _):
            for f in range(6):
                at = q * 48 + i * 6 + f
                near, far = nbr[at], inv[at]
                link = jnp.maximum(far - 1, 0)
                slot = jnp.minimum(near, SLOTS - 1)
                quarter = slot // 8
                here = held[quarter, (slot - 8 * quarter) * 6 + (f ^ 1)].astype(F32)
                there = recv[(link // 2) * 5 + link % 2].astype(F32)
                u = jnp.where(near < SLOTS, here, there)
                centre = jnp.where(
                    near < SLOTS, cen[pl.ds(slot, 1), :], far_cen[pl.ds(link, 1), :]
                )
                v = silu((u + (centre - mean)) * scale + bias)
                some = jnp.logical_or(near < SLOTS, far > 0)
                o[i * 6 + f] = jnp.where(some, v, 0.0).astype(BF16)
            link = jnp.maximum(sinv[q * 8 + i] - 1, 0)
            o[48 + i] = recv[(link // 2) * 5 + 2 + link % 2]
            return 0

        lax.fori_loop(0, QUART, face, 0)
        o[56] = told


def conv2_kernel(
    me, hid, v0, v1, v2, v3, u0, u1, u2, u3, weights, lift,
    o0, o1, o2, o3,
    units, wfine, rows, taps, shift, cube,
):
    step = pl.program_id(0)
    y = me[0]

    @pl.when(step == 0)
    def _():
        for r, u in enumerate((u0, u1, u2, u3)):
            units[(y - r) & 3] = u[...]
        fill_weights(wfine, weights, 1)
        for k in range(3):
            rows[k : k + 1, :] = gather_row([joined(units[c, 56].astype(F32), 3 * k) for c in range(4)])

    def unit(i):
        return unpack([units[c, i].astype(F32) for c in range(4)])

    act = silu((hid[0] - rows[0:1]) * rows[1:2] + rows[2:3]).astype(BF16)
    build_taps(act, lambda f: unit(step * 6 + f), taps, shift)
    branch = lax.dot_general(taps[...], wfine[...], NT, preferred_element_type=F32)
    lifted = lax.dot_general(
        lift[...], unit(48 + step).astype(BF16), NN, preferred_element_type=F32
    )
    for r, v in enumerate((v0, v1, v2, v3)):
        at = pl.multiple_of(((y - r) & 3) * 64, 64)
        cube[pl.ds(at, 64), :] = v[0].astype(F32)
    cube[...] += (branch + lifted).T
    for r, o in enumerate((o0, o1, o2, o3)):
        at = pl.multiple_of(((y + r) & 3) * 64, 64)
        o[0] = cube[pl.ds(at, 64), :].astype(BF16)


def shape(*dims, dtype=BF16):
    return jax.ShapeDtypeStruct(dims, dtype)


def params(**more):
    return pltpu.CompilerParams(vmem_limit_bytes=LIMIT, **more)


def exchange(parts):
    out = [parts[0]]
    got = {}
    for r in (2, 1, 3):
        got[r] = lax.ppermute(parts[r], "chan", [(i, (i + r) % 4) for i in range(4)])
    return out + [got[1], got[2], got[3]]


def over_blocks(units):
    return lax.all_to_all(units, "blocks", split_axis=0, concat_axis=0, tiled=True)


def local(
    feats,
    conv_weights,
    norm_gain,
    norm_bias,
    time_bias,
    local_nbr,
    face_links,
    coarse_send,
    coarse_recv,
):
    extract_np, lift_np, place_np = tables()
    y = lax.axis_index("chan").astype(jnp.int32)
    me = y[None]
    nbr = local_nbr.reshape(-1)
    links = face_links.reshape(-1)
    csend = coarse_send.reshape(-1)
    crecv = coarse_recv.reshape(-1)

    def twice(rows):
        block = jnp.stack(rows)
        block = jnp.concatenate([block, block], axis=1)
        return jnp.pad(block, ((0, 8 - block.shape[0]), (0, 0)))

    par1 = twice([norm_gain[0], norm_bias[0], norm_gain[2], norm_bias[2], time_bias])
    par2 = twice([norm_gain[1], norm_bias[1]])
    weights = lax.all_gather(conv_weights, "chan", axis=0, tiled=False)

    volumes = exchange(
        [
            lax.dynamic_slice_in_dim(feats, QUART * ((y + r) % 4), QUART, axis=0)
            for r in range(4)
        ]
    )

    faces, outgoing = pl.pallas_call(
        extract_kernel,
        out_shape=(shape(FACES, 32, 128), shape(5 * DEVS, 32, 128)),
        in_specs=[SMEM, SMEM, VMEM, VMEM],
        out_specs=(VMEM, VMEM),
        scratch_shapes=[pltpu.VMEM((SLOTS, 32, 128), BF16), pltpu.VMEM((32, 128), F32)],
        compiler_params=params(),
        name="extract",
    )(links, csend, feats, jnp.asarray(extract_np, BF16))
    arrived = over_blocks(outgoing)

    parts = pl.pallas_call(
        border1_kernel,
        out_shape=(shape(65, 32, 128),) * 4,
        in_specs=[SMEM] * 4 + [VMEM] * 3,
        out_specs=(VMEM,) * 4,
        scratch_shapes=[
            pltpu.SMEM((FACES,), jnp.int32),
            pltpu.SMEM((CODES,), jnp.int32),
            pltpu.VMEM((32, 128), F32),
        ],
        compiler_params=params(),
        name="border1",
    )(nbr, links, crecv, me, faces, arrived, par1)
    units1 = exchange(parts)

    block = pl.BlockSpec((1, 64, VOX), lambda i: (jnp.minimum(i, QUART - 1), 0, 0))
    hidden, *parts = pl.pallas_call(
        conv1_kernel,
        grid=(QUART + TILES,),
        out_shape=(shape(QUART, VOX, 256, dtype=F32),) + (shape(65, 32, 128),) * 4,
        in_specs=[SMEM] + [block] * 4 + [VMEM] * 7,
        out_specs=(pl.BlockSpec((1, VOX, 256), lambda i: (jnp.minimum(i, QUART - 1), 0, 0)),)
        + (VMEM,) * 4,
        scratch_shapes=[
            pltpu.VMEM((4, 65, 32, 128), BF16),
            pltpu.VMEM((4, 65, 32, 128), BF16),
            pltpu.VMEM((256, 1792), BF16),
            pltpu.VMEM((256, 1792), BF16),
            pltpu.VMEM((8, 256), F32),
            pltpu.VMEM((VOX, 1792), BF16),
            pltpu.VMEM((VOX, 128), F32),
            pltpu.VMEM((256, VOX), F32),
            pltpu.VMEM((4, 32, 128), F32),
            pltpu.VMEM((8, 256), F32),
        ],
        compiler_params=params(),
        name="conv1",
    )(
        me, *volumes, *units1, weights, jnp.asarray(place_np, BF16), jnp.asarray(place_np.T, BF16)
    )
    parts = exchange(parts)

    held, outgoing = pl.pallas_call(
        route2_kernel,
        out_shape=(shape(4, 65, 32, 128), shape(5 * DEVS, 32, 128)),
        in_specs=[SMEM] * 3 + [VMEM] * 4,
        out_specs=(VMEM, VMEM),
        scratch_shapes=[pltpu.VMEM((SLOTS, 128), F32), pltpu.VMEM((32, 128), F32)],
        compiler_params=params(),
        name="route2",
    )(links, crecv, me, *parts)
    arrived = over_blocks(outgoing)

    parts = pl.pallas_call(
        border2_kernel,
        out_shape=(shape(57, 32, 128),) * 4,
        in_specs=[SMEM] * 4 + [VMEM] * 3,
        out_specs=(VMEM,) * 4,
        scratch_shapes=[
            pltpu.SMEM((FACES,), jnp.int32),
            pltpu.SMEM((SLOTS,), jnp.int32),
            pltpu.VMEM((SLOTS, 128), F32),
            pltpu.VMEM((2 * DEVS, 128), F32),
            pltpu.VMEM((32, 128), F32),
        ],
        compiler_params=params(),
        name="border2",
    )(nbr, links, csend, me, held, arrived, par2)
    units2 = exchange(parts)

    block = pl.BlockSpec((1, 64, VOX), lambda i: (i, 0, 0))
    parts = pl.pallas_call(
        conv2_kernel,
        grid=(QUART,),
        out_shape=(shape(QUART, 64, VOX),) * 4,
        in_specs=[SMEM, pl.BlockSpec((1, VOX, 256), lambda i: (i, 0, 0))]
        + [block] * 4
        + [VMEM] * 6,
        out_specs=(block,) * 4,
        scratch_shapes=[
            pltpu.VMEM((4, 57, 32, 128), BF16),
            pltpu.VMEM((256, 1792), BF16),
            pltpu.VMEM((8, 256), F32),
            pltpu.VMEM((VOX, 1792), BF16),
            pltpu.VMEM((VOX, 128), F32),
            pltpu.VMEM((256, VOX), F32),
        ],
        compiler_params=params(),
        name="conv2",
    )(me, hidden, *volumes, *units2, weights, jnp.asarray(lift_np, BF16))
    parts = exchange(parts)

    out = jnp.zeros(feats.shape, feats.dtype)
    for r in range(4):
        out = lax.dynamic_update_slice_in_dim(out, parts[r], QUART * ((y - r) % 4), axis=0)
    return out


def solution(mesh):
    in_specs = (
        P("blocks", "chan", None),
        P(None, None, "chan", None),
        P(None, "chan"),
        P(None, "chan"),
        P("chan"),
        P("blocks", None),
        P("blocks", None, None),
        P("blocks", None, None),
        P("blocks", None, None),
    )
    out_specs = P("blocks", "chan", None)
    return jax.shard_map(local, mesh=mesh, in_specs=in_specs, out_specs=out_specs, check_vma=False)
```

time: 781 us -> 270 us (0.35); the launches traced: 772 us -> 269 us
  matrix products: 187 us -> 0 us
  blocking collectives: 167 us -> 0 us
  local copies, waits for them, and re-layouts: 172 us -> 13.6 us
  Pallas kernels: 0 us -> 63.7 us
  other arithmetic: 46.2 us -> 1.34 us
  waiting for transfers between devices: 176 us -> 139 us
  starting transfers between devices: 8.75 us -> 37.6 us
    dot_general x22 -> x0, matrix products: 187 us -> none  [the longest x12 98 us: add_taps(): jnp.einsum('bcu,vu->bcv', border[:, which_face], table, preferred_element...]
    all_gather x5 -> x1, waiting for transfers between devices: 166 us -> 0.02 us  [local(): weights = lax.all_gather(conv_weights, 'chan', axis=0, tiled=False)]
    psum x2 -> x0, blocking collectives: 128 us -> none  [global_sums(): return lax.psum(stacked, 'blocks')]
    ppermute x0 -> x15, waiting for transfers between devices: none -> 106 us  [exchange(): lax.ppermute(parts[r], 'chan', [(i, (i + r) % 4) for i in range(4)])]
    pallas_call x0 -> x6, Pallas kernels: none -> 63.7 us  [the longest x1 19 us: local(): pl.pallas_call(conv1_kernel, grid=(QUART + TILES,), out_shape=(shape(QUAR...]
    slice x9 -> x1, local copies, waits for them, and re-layouts: 53.4 us -> 0.01 us  [local(): par2 = twice([norm_gain[1], norm_bias[1]])]
    gather x14 -> x0, local copies, waits for them, and re-layouts: 47.3 us -> none  [the longest x2 21.5 us: build_border(): nearby = jnp.concatenate([layers, blank], axis=0)[local_src]]
    all_to_all x2 -> x0, blocking collectives: 39.3 us -> none  [face_conv(): lax.all_to_all(outgoing, 'blocks', split_axis=0, concat_axis=0, tiled=True)]
  transfers between devices with their start and end apart: 7 -> 18, of which waited for: 5 -> 11; matrix products, arithmetic and copies ran while one was open for 12% -> 3% of each run, Pallas kernels for 0% -> 6%
where the time goes in v1:
time: 270 us; the launch traced here: 269 us
  waiting for transfers between devices  139 us (51%)
  Pallas kernels  63.7 us (24%)
  starting transfers between devices  37.6 us (14%)
  between operations  13.7 us (5%)
  local copies, waits for them, and re-layouts  13.6 us (5%)
    ppermute x15, waiting for transfers between devices, exchange(): lax.ppermute(parts[r], 'chan', [(i, (i + r) % 4) for i in range(4)])  106 us
    all_to_all x2, waiting for transfers between devices, over_blocks(): lax.all_to_all(units, 'blocks', split_axis=0, concat_axis=0, tiled=True)  32.4 us
    ppermute x15, starting transfers between devices, exchange(): lax.ppermute(parts[r], 'chan', [(i, (i + r) % 4) for i in range(4)])  22.2 us
    pallas_call x1, Pallas kernels, local(): pl.pallas_call(conv1_kernel, grid=(QUART + TILES,), out_shape=(shape(QUAR...  19 us
    all_to_all x2, starting transfers between devices, over_blocks(): lax.all_to_all(units, 'blocks', split_axis=0, concat_axis=0, tiled=True)  15.4 us
    pallas_call x1, Pallas kernels, local(): pl.pallas_call(conv2_kernel, grid=(QUART,), out_shape=(shape(QUART, 64, V...  13.1 us
    pallas_call x1, Pallas kernels, local(): pl.pallas_call(border2_kernel, out_shape=(shape(57, 32, 128),) * 4, in_sp...  9.49 us
    pallas_call x1, Pallas kernels, local(): pl.pallas_call(border1_kernel, out_shape=(shape(65, 32, 128),) * 4, in_sp...  9.4 us
  transfers between devices with their start and end apart: 18, of which 11 were waited for; matrix products, arithmetic and copies ran while one was open for 3% of the time, Pallas kernels for 6%

profile of v1, /device:TPU:1, one launch (start us, length us, event | category | flops | bytes accessed | tf_op | source)
XLA Modules:
  0.0 269.4 jit_solution(9664035624529730810)
XLA Ops:
  6.5 0.7 all-gather.3.cloned.1.call-update
  7.3 0.8 copy.22
  8.0 0.7 reshape.13.links
  8.7 0.8 copy.24
  9.5 0.7 reshape.15.csend
  10.1 7.7 %extract.1 = (bf16[192,32,128]{2,1,0:T(8,128)(2,1)}, bf16[160,32,128]{2,1,0:T(8,128)(2,1)}) custom-call(s32[64]{0:T(128)} %reshape.13.links, s32[64]{0:T(128)} %reshape.15.csend, bf16[32,64,512]{2,1,0:T(8,128)(2,1)} %feats.1, bf16[448,512]{1,0:T(8,128)(2,1)} %constant.71.clone.table), custom_call_target="tpu_custom_call" | custom-call | tf_op jit(solution)/shard_map/extract/pallas_call | solution.py:544
  17.9 9.4 %all-to-all-start = ((bf16[160,32,128]{2,1,0:T(8,128)(2,1)}), bf16[160,32,128]{2,1,0:T(8,128)(2,1)S(1)}, u32[]{:S(2)}, u32[]{:S(2)}) async-start(bf16[160,32,128]{2,1,0:T(8,128)(2,1)} %get-tuple-element.27), calls=%async_computation | async-start | bytes 2621440 | tf_op jit(solution)/shard_map/all_to_all | solution.py:506
  27.4 0.0 copy-start.19
  27.4 0.0 copy-start.22
  27.4 0.0 copy-start.20
  27.4 0.0 copy-start.21
  27.4 0.0 copy-start.23
  27.4 1.5 constant_dynamic-slice_fusion
  28.9 1.3 collective-permute-start
  30.2 0.1 copy.21
  30.3 0.6 reshape.12.nbr
  30.9 0.1 copy.23
  31.0 0.6 reshape.14.crecv
  31.7 0.7 select_maximum_fusion.2.par
  32.4 14.0 %all-to-all-done.recv = bf16[160,32,128]{2,1,0:T(8,128)(2,1)S(1)} async-done(((bf16[160,32,128]{2,1,0:T(8,128)(2,1)}), bf16[160,32,128]{2,1,0:T(8,128)(2,1)S(1)}, u32[]{:S(2)}, u32[]{:S(2)}) %all-to-all-start) | async-done | bytes 1310752 | tf_op jit(solution)/shard_map/all_to_all | solution.py:506
  46.4 1.1 copy-done.2
  47.5 9.4 %border1.1 = (bf16[65,32,128]{2,1,0:T(8,128)(2,1)}, bf16[65,32,128]{2,1,0:T(8,128)(2,1)}, bf16[65,32,128]{2,1,0:T(8,128)(2,1)}, bf16[65,32,128]{2,1,0:T(8,128)(2,1)}) custom-call(s32[192]{0:T(256)} %reshape.12.nbr, s32[64]{0:T(128)} %reshape.13.links, s32[64]{0:T(128)} %reshape.14.crecv, s32[1]{0:T(128)} %bitcast.me, ...), custom_call_target="tpu_custom_call" | custom-call | tf_op jit(solution)/shard_map/border1/pallas_call | solution.py:555
  56.9 1.3 collective-permute-start.3
  58.2 2.6 collective-permute-start.4
  60.8 1.1 collective-permute-start.5
  61.9 0.1 collective-permute-start.1
  62.0 2.7 %collective-permute-start.2 = (bf16[8,64,512]{2,1,0:T(8,128)(2,1)S(1)}, bf16[8,64,512]{2,1,0:T(8,128)(2,1)S(1)}, u32[]{:S(2)}, u32[]{:S(2)}) collective-permute-start(bf16[8,64,512]{2,1,0:T(8,128)(2,1)S(1)} %copy-done.14), channel_id=1, source_target_pairs={{0,3},{1,0},{2,1},{3,2},{4,7},{5,4},{6,5},{7,6},{8,11},{9,8},{10,9... | collective-permute-start | bytes 1572872 | tf_op jit(solution)/shard_map/ppermute | solution.py:501
  64.7 29.1 %collective-permute-done.1.v2 = bf16[8,64,512]{2,1,0:T(8,128)(2,1)S(1)} collective-permute-done((bf16[8,64,512]{2,1,0:T(8,128)(2,1)S(1)}, bf16[8,64,512]{2,1,0:T(8,128)(2,1)S(1)}, u32[]{:S(2)}, u32[]{:S(2)}) %collective-permute-start.1) | collective-permute-done | bytes 524320 | tf_op jit(solution)/shard_map/ppermute | solution.py:501
  93.9 12.0 %collective-permute-done.2.v3 = bf16[8,64,512]{2,1,0:T(8,128)(2,1)S(1)} collective-permute-done((bf16[8,64,512]{2,1,0:T(8,128)(2,1)S(1)}, bf16[8,64,512]{2,1,0:T(8,128)(2,1)S(1)}, u32[]{:S(2)}, u32[]{:S(2)}) %collective-permute-start.2) | collective-permute-done | bytes 524320 | tf_op jit(solution)/shard_map/ppermute | solution.py:501
  105.9 0.0 all-gather.3.cloned.1.call-done
  105.9 0.7 copy-done.5
  106.6 0.2 copy-done.7
  106.8 0.2 copy-done.8
  107.1 0.1 copy-done.9
  107.2 19.0 %conv1.1 = (f32[8,512,256]{2,1,0:T(8,128)}, bf16[65,32,128]{2,1,0:T(8,128)(2,1)}, bf16[65,32,128]{2,1,0:T(8,128)(2,1)}, bf16[65,32,128]{2,1,0:T(8,128)(2,1)}, bf16[65,32,128]{2,1,0:T(8,128)(2,1)}) custom-call(s32[1]{0:T(128)} %bitcast.me, bf16[8,64,512]{2,1,0:T(8,128)(2,1)} %get-tuple-element.50.v0, bf16[8,64,512]{2,1,0:T(8,128)(2,1)} %copy-done.3, ...), custom_call_target="tpu_custom_call" | custom-call | tf_op jit(solution)/shard_map/conv1/pallas_call | solution.py:571
  126.1 1.7 collective-permute-start.6
  127.8 3.0 %collective-permute-start.7 = (bf16[65,32,128]{2,1,0:T(8,128)(2,1)}, bf16[65,32,128]{2,1,0:T(8,128)(2,1)S(1)}, u32[]{:S(2)}, u32[]{:S(2)}) collective-permute-start(bf16[65,32,128]{2,1,0:T(8,128)(2,1)} %get-tuple-element.35), channel_id=1, source_target_pairs={{0,2},{1,3},{2,0},{3,1},{4,6},{5,7},{6,4},{7,5},{8,10},{9,11},{10,... | collective-permute-start | bytes 1597448 | tf_op jit(solution)/shard_map/ppermute | solution.py:501
  130.8 10.3 %collective-permute-done.6.v1 = bf16[65,32,128]{2,1,0:T(8,128)(2,1)S(1)} collective-permute-done((bf16[65,32,128]{2,1,0:T(8,128)(2,1)}, bf16[65,32,128]{2,1,0:T(8,128)(2,1)S(1)}, u32[]{:S(2)}, u32[]{:S(2)}) %collective-permute-start.6) | collective-permute-done | bytes 532512 | tf_op jit(solution)/shard_map/ppermute | solution.py:501
  141.1 13.0 %collective-permute-done.7.v2 = bf16[65,32,128]{2,1,0:T(8,128)(2,1)S(1)} collective-permute-done((bf16[65,32,128]{2,1,0:T(8,128)(2,1)}, bf16[65,32,128]{2,1,0:T(8,128)(2,1)S(1)}, u32[]{:S(2)}, u32[]{:S(2)}) %collective-permute-start.7) | collective-permute-done | bytes 532512 | tf_op jit(solution)/shard_map/ppermute | solution.py:501
  154.1 0.8 copy-done.11
  155.0 0.2 copy-done.12
  155.1 5.0 %route2.1 = (bf16[4,65,32,128]{3,2,1,0:T(8,128)(2,1)}, bf16[160,32,128]{2,1,0:T(8,128)(2,1)}) custom-call(s32[64]{0:T(128)} %reshape.13.links, s32[64]{0:T(128)} %reshape.14.crecv, s32[1]{0:T(128)} %bitcast.me, bf16[65,32,128]{2,1,0:T(8,128)(2,1)} %get-tuple-element.33.v0, bf16[65,32,128]{2,1,0:T(8,128)(2,1)} %copy-done.10, bf16[65,32,128]{2,1,0:T(8,128)(2,1)} %copy-done.11, ...), custom_call_target="tpu_custom_call" | custom-call | tf_op jit(solution)/shard_map/route2/pallas_call | solution.py:597
  160.1 6.0 %all-to-all-start.1 = ((bf16[160,32,128]{2,1,0:T(8,128)(2,1)}), bf16[160,32,128]{2,1,0:T(8,128)(2,1)S(1)}, u32[]{:S(2)}, u32[]{:S(2)}) async-start(bf16[160,32,128]{2,1,0:T(8,128)(2,1)} %get-tuple-element.38), calls=%async_computation.1 | async-start | bytes 2621440 | tf_op jit(solution)/shard_map/all_to_all | solution.py:506
  166.1 0.7 fusion.par
  166.8 18.4 %all-to-all-done.1.recv = bf16[160,32,128]{2,1,0:T(8,128)(2,1)S(1)} async-done(((bf16[160,32,128]{2,1,0:T(8,128)(2,1)}), bf16[160,32,128]{2,1,0:T(8,128)(2,1)S(1)}, u32[]{:S(2)}, u32[]{:S(2)}) %all-to-all-start.1) | async-done | bytes 1310752 | tf_op jit(solution)/shard_map/all_to_all | solution.py:506
  185.2 1.1 copy-done.1
  186.2 9.5 %border2.1 = (bf16[57,32,128]{2,1,0:T(8,128)(2,1)}, bf16[57,32,128]{2,1,0:T(8,128)(2,1)}, bf16[57,32,128]{2,1,0:T(8,128)(2,1)}, bf16[57,32,128]{2,1,0:T(8,128)(2,1)}) custom-call(s32[192]{0:T(256)} %reshape.12.nbr, s32[64]{0:T(128)} %reshape.13.links, s32[64]{0:T(128)} %reshape.15.csend, s32[1]{0:T(128)} %bitcast.me, ...), custom_call_target="tpu_custom_call" | custom-call | tf_op jit(solution)/shard_map/border2/pallas_call | solution.py:608
  195.7 2.4 collective-permute-start.10
  198.1 1.0 collective-permute-start.11
  199.2 0.4 collective-permute-start.9
  199.6 8.1 %collective-permute-done.10.u2 = bf16[57,32,128]{2,1,0:T(8,128)(2,1)S(1)} collective-permute-done((bf16[57,32,128]{2,1,0:T(8,128)(2,1)}, bf16[57,32,128]{2,1,0:T(8,128)(2,1)S(1)}, u32[]{:S(2)}, u32[]{:S(2)}) %collective-permute-start.10) | collective-permute-done | bytes 466976 | tf_op jit(solution)/shard_map/ppermute | solution.py:501
  207.7 11.0 %collective-permute-done.11.u3 = bf16[57,32,128]{2,1,0:T(8,128)(2,1)S(1)} collective-permute-done((bf16[57,32,128]{2,1,0:T(8,128)(2,1)}, bf16[57,32,128]{2,1,0:T(8,128)(2,1)S(1)}, u32[]{:S(2)}, u32[]{:S(2)}) %collective-permute-start.11) | collective-permute-done | bytes 466976 | tf_op jit(solution)/shard_map/ppermute | solution.py:501
  218.7 1.3 collective-permute-done.9.u1
  220.1 0.8 copy-done.18
  220.8 13.1 %conv2.1 = (bf16[8,64,512]{2,1,0:T(8,128)(2,1)}, bf16[8,64,512]{2,1,0:T(8,128)(2,1)}, bf16[8,64,512]{2,1,0:T(8,128)(2,1)}, bf16[8,64,512]{2,1,0:T(8,128)(2,1)}) custom-call(s32[1]{0:T(128)} %bitcast.me, f32[8,512,256]{2,1,0:T(8,128)} %get-tuple-element.32.hid, bf16[8,64,512]{2,1,0:T(8,128)(2,1)} %get-tuple-element.50.v0, bf16[8,64,512]{2,1,0:T(8,128)(2,1)} %copy-done.3, ...), custom_call_target="tpu_custom_call" | custom-call | tf_op jit(solution)/shard_map/conv2/pallas_call | solution.py:626
  234.0 1.2 collective-permute-start.12
  235.2 2.1 collective-permute-start.13
  237.3 1.2 collective-permute-start.14
  238.5 0.2 broadcast_in_dim.6
  238.8 9.6 %collective-permute-done.12 = bf16[8,64,512]{2,1,0:T(8,128)(2,1)S(1)} collective-permute-done((bf16[8,64,512]{2,1,0:T(8,128)(2,1)}, bf16[8,64,512]{2,1,0:T(8,128)(2,1)S(1)}, u32[]{:S(2)}, u32[]{:S(2)}) %collective-permute-start.12) | collective-permute-done | bytes 524320 | tf_op jit(solution)/shard_map/ppermute | solution.py:501
  248.5 11.8 %collective-permute-done.13 = bf16[8,64,512]{2,1,0:T(8,128)(2,1)S(1)} collective-permute-done((bf16[8,64,512]{2,1,0:T(8,128)(2,1)}, bf16[8,64,512]{2,1,0:T(8,128)(2,1)S(1)}, u32[]{:S(2)}, u32[]{:S(2)}) %collective-permute-start.13) | collective-permute-done | bytes 524320 | tf_op jit(solution)/shard_map/ppermute | solution.py:501
  260.3 0.0 copy-start.6
  260.4 1.3 copy-done.6
  261.7 0.8 constant_dynamic-update-slice_fusion
  (45 shorter events, 0.2 us)
Async XLA Ops:
  6.5 99.4 %all-gather.3.cloned.1.call-start = ((), (), s32[]{:S(2)}) async-start(), calls=%async_computation.2 | async-start | bytes 3440640 | tf_op jit(solution)/shard_map/all_gather | solution.py:535
  10.1 17.2 %copy-start = (bf16[32,64,512]{2,1,0:T(8,128)(2,1)S(1)}, bf16[32,64,512]{2,1,0:T(8,128)(2,1)}, u32[]{:S(2)}) copy-start(bf16[32,64,512]{2,1,0:T(8,128)(2,1)} %feats.1) | copy-start | bytes 6291460
  17.9 28.5 %all-to-all-start = ((bf16[160,32,128]{2,1,0:T(8,128)(2,1)}), bf16[160,32,128]{2,1,0:T(8,128)(2,1)S(1)}, u32[]{:S(2)}, u32[]{:S(2)}) async-start(bf16[160,32,128]{2,1,0:T(8,128)(2,1)} %get-tuple-element.27), calls=%async_computation | async-start | bytes 2621440 | tf_op jit(solution)/shard_map/all_to_all | solution.py:506
  27.4 2.8 %copy-start.19 = (s32[32,6]{0,1:T(8,128)S(1)}, s32[32,6]{0,1:T(8,128)}, u32[]{:S(2)}) copy-start(s32[32,6]{0,1:T(8,128)} %param.18) | copy-start | bytes 2308
  27.4 3.5 %copy-start.22 = (s32[1,32,2]{1,2,0:T(2,128)S(1)}, s32[1,32,2]{1,2,0:T(2,128)}, u32[]{:S(2)}) copy-start(s32[1,32,2]{1,2,0:T(2,128)} %param.21) | copy-start | bytes 772
  27.4 4.3 %copy-start.20 = (f32[3,64]{1,0:T(4,128)S(1)}, f32[3,64]{1,0:T(4,128)}, u32[]{:S(2)}) copy-start(f32[3,64]{1,0:T(4,128)} %param.15) | copy-start | bytes 2308
  27.4 4.3 %copy-start.21 = (f32[3,64]{1,0:T(4,128)S(1)}, f32[3,64]{1,0:T(4,128)}, u32[]{:S(2)}) copy-start(f32[3,64]{1,0:T(4,128)} %param.16) | copy-start | bytes 2308
  27.4 4.2 %copy-start.23 = (f32[64]{0:T(128)S(1)}, f32[64]{0:T(128)}, u32[]{:S(2)}) copy-start(f32[64]{0:T(128)} %param.17) | copy-start | bytes 772
  28.9 33.1 %collective-permute-start = (bf16[8,64,512]{2,1,0:T(8,128)(2,1)}, bf16[8,64,512]{2,1,0:T(8,128)(2,1)S(1)}, u32[]{:S(2)}, u32[]{:S(2)}) collective-permute-start(bf16[8,64,512]{2,1,0:T(8,128)(2,1)} %get-tuple-element.49), channel_id=1, source_target_pairs={{0,1},{1,2},{2,3},{3,0},{4,5},{5,6},{6,7},{7,4},{8,9},{9,10},{10,1... | collective-permute-start | bytes 1572872 | tf_op jit(solution)/shard_map/ppermute | solution.py:501
  46.4 1.1 copy-start.2
  46.4 15.5 %copy-start.15 = (bf16[8,64,512]{2,1,0:T(8,128)(2,1)S(1)}, bf16[8,64,512]{2,1,0:T(8,128)(2,1)}, u32[]{:S(2)}) copy-start(bf16[8,64,512]{2,1,0:T(8,128)(2,1)} %get-tuple-element.48) | copy-start | bytes 1572868
  46.4 15.6 %copy-start.14 = (bf16[8,64,512]{2,1,0:T(8,128)(2,1)S(1)}, bf16[8,64,512]{2,1,0:T(8,128)(2,1)}, u32[]{:S(2)}) copy-start(bf16[8,64,512]{2,1,0:T(8,128)(2,1)} %get-tuple-element.47) | copy-start | bytes 1572868
  56.9 48.9 %collective-permute-start.3 = (bf16[65,32,128]{2,1,0:T(8,128)(2,1)}, bf16[65,32,128]{2,1,0:T(8,128)(2,1)S(1)}, u32[]{:S(2)}, u32[]{:S(2)}) collective-permute-start(bf16[65,32,128]{2,1,0:T(8,128)(2,1)} %get-tuple-element.29), channel_id=1, source_target_pairs={{0,1},{1,2},{2,3},{3,0},{4,5},{5,6},{6,7},{7,4},{8,9},{9,10},{10,1... | collective-permute-start | bytes 1597448 | tf_op jit(solution)/shard_map/ppermute | solution.py:501
  58.2 47.7 %collective-permute-start.4 = (bf16[65,32,128]{2,1,0:T(8,128)(2,1)}, bf16[65,32,128]{2,1,0:T(8,128)(2,1)S(1)}, u32[]{:S(2)}, u32[]{:S(2)}) collective-permute-start(bf16[65,32,128]{2,1,0:T(8,128)(2,1)} %get-tuple-element.30), channel_id=1, source_target_pairs={{0,2},{1,3},{2,0},{3,1},{4,6},{5,7},{6,4},{7,5},{8,10},{9,11},{10,... | collective-permute-start | bytes 1597448 | tf_op jit(solution)/shard_map/ppermute | solution.py:501
  60.8 45.1 %collective-permute-start.5 = (bf16[65,32,128]{2,1,0:T(8,128)(2,1)}, bf16[65,32,128]{2,1,0:T(8,128)(2,1)S(1)}, u32[]{:S(2)}, u32[]{:S(2)}) collective-permute-start(bf16[65,32,128]{2,1,0:T(8,128)(2,1)} %get-tuple-element.31), channel_id=1, source_target_pairs={{0,3},{1,0},{2,1},{3,2},{4,7},{5,4},{6,5},{7,6},{8,11},{9,8},{10,9... | collective-permute-start | bytes 1597448 | tf_op jit(solution)/shard_map/ppermute | solution.py:501
  61.9 32.0 %collective-permute-start.1 = (bf16[8,64,512]{2,1,0:T(8,128)(2,1)S(1)}, bf16[8,64,512]{2,1,0:T(8,128)(2,1)S(1)}, u32[]{:S(2)}, u32[]{:S(2)}) collective-permute-start(bf16[8,64,512]{2,1,0:T(8,128)(2,1)S(1)} %copy-done.15), channel_id=1, source_target_pairs={{0,2},{1,3},{2,0},{3,1},{4,6},{5,7},{6,4},{7,5},{8,10},{9,11},{10,... | collective-permute-start | bytes 1572872 | tf_op jit(solution)/shard_map/ppermute | solution.py:501
  62.0 43.9 %copy-start.3 = (bf16[8,64,512]{2,1,0:T(8,128)(2,1)}, bf16[8,64,512]{2,1,0:T(8,128)(2,1)S(1)}, u32[]{:S(2)}) copy-start(bf16[8,64,512]{2,1,0:T(8,128)(2,1)S(1)} %collective-permute-done.v1) | copy-start | bytes 1572868
  62.0 43.8 %collective-permute-start.2 = (bf16[8,64,512]{2,1,0:T(8,128)(2,1)S(1)}, bf16[8,64,512]{2,1,0:T(8,128)(2,1)S(1)}, u32[]{:S(2)}, u32[]{:S(2)}) collective-permute-start(bf16[8,64,512]{2,1,0:T(8,128)(2,1)S(1)} %copy-done.14), channel_id=1, source_target_pairs={{0,3},{1,0},{2,1},{3,2},{4,7},{5,4},{6,5},{7,6},{8,11},{9,8},{10,9... | collective-permute-start | bytes 1572872 | tf_op jit(solution)/shard_map/ppermute | solution.py:501
  93.9 12.1 %copy-start.4 = (bf16[8,64,512]{2,1,0:T(8,128)(2,1)}, bf16[8,64,512]{2,1,0:T(8,128)(2,1)S(1)}, u32[]{:S(2)}) copy-start(bf16[8,64,512]{2,1,0:T(8,128)(2,1)S(1)} %collective-permute-done.1.v2) | copy-start | bytes 1572868
  105.8 0.8 copy-start.5
  105.8 1.0 copy-start.7
  105.9 1.2 copy-start.8
  105.9 1.3 copy-start.9
  126.1 15.0 %collective-permute-start.6 = (bf16[65,32,128]{2,1,0:T(8,128)(2,1)}, bf16[65,32,128]{2,1,0:T(8,128)(2,1)S(1)}, u32[]{:S(2)}, u32[]{:S(2)}) collective-permute-start(bf16[65,32,128]{2,1,0:T(8,128)(2,1)} %get-tuple-element.34), channel_id=1, source_target_pairs={{0,1},{1,2},{2,3},{3,0},{4,5},{5,6},{6,7},{7,4},{8,9},{9,10},{10,1... | collective-permute-start | bytes 1597448 | tf_op jit(solution)/shard_map/ppermute | solution.py:501
  127.8 26.3 %collective-permute-start.7 = (bf16[65,32,128]{2,1,0:T(8,128)(2,1)}, bf16[65,32,128]{2,1,0:T(8,128)(2,1)S(1)}, u32[]{:S(2)}, u32[]{:S(2)}) collective-permute-start(bf16[65,32,128]{2,1,0:T(8,128)(2,1)} %get-tuple-element.35), channel_id=1, source_target_pairs={{0,2},{1,3},{2,0},{3,1},{4,6},{5,7},{6,4},{7,5},{8,10},{9,11},{10,... | collective-permute-start | bytes 1597448 | tf_op jit(solution)/shard_map/ppermute | solution.py:501
  130.8 23.3 %collective-permute-start.8 = (bf16[65,32,128]{2,1,0:T(8,128)(2,1)}, bf16[65,32,128]{2,1,0:T(8,128)(2,1)S(1)}, u32[]{:S(2)}, u32[]{:S(2)}) collective-permute-start(bf16[65,32,128]{2,1,0:T(8,128)(2,1)} %get-tuple-element.36), channel_id=1, source_target_pairs={{0,3},{1,0},{2,1},{3,2},{4,7},{5,4},{6,5},{7,6},{8,11},{9,8},{10,9... | collective-permute-start | bytes 1597448 | tf_op jit(solution)/shard_map/ppermute | solution.py:501
  141.1 13.0 %copy-start.10 = (bf16[65,32,128]{2,1,0:T(8,128)(2,1)}, bf16[65,32,128]{2,1,0:T(8,128)(2,1)S(1)}, u32[]{:S(2)}) copy-start(bf16[65,32,128]{2,1,0:T(8,128)(2,1)S(1)} %collective-permute-done.6.v1) | copy-start | bytes 1597444
  154.1 0.8 copy-start.11
  154.1 1.0 copy-start.12
  160.1 25.1 %all-to-all-start.1 = ((bf16[160,32,128]{2,1,0:T(8,128)(2,1)}), bf16[160,32,128]{2,1,0:T(8,128)(2,1)S(1)}, u32[]{:S(2)}, u32[]{:S(2)}) async-start(bf16[160,32,128]{2,1,0:T(8,128)(2,1)} %get-tuple-element.38), calls=%async_computation.1 | async-start | bytes 2621440 | tf_op jit(solution)/shard_map/all_to_all | solution.py:506
  185.2 1.1 copy-start.1
  195.7 12.0 %collective-permute-start.10 = (bf16[57,32,128]{2,1,0:T(8,128)(2,1)}, bf16[57,32,128]{2,1,0:T(8,128)(2,1)S(1)}, u32[]{:S(2)}, u32[]{:S(2)}) collective-permute-start(bf16[57,32,128]{2,1,0:T(8,128)(2,1)} %get-tuple-element.41), channel_id=1, source_target_pairs={{0,2},{1,3},{2,0},{3,1},{4,6},{5,7},{6,4},{7,5},{8,10},{9,11},{10,... | collective-permute-start | bytes 1400840 | tf_op jit(solution)/shard_map/ppermute | solution.py:501
  198.1 20.6 %collective-permute-start.11 = (bf16[57,32,128]{2,1,0:T(8,128)(2,1)}, bf16[57,32,128]{2,1,0:T(8,128)(2,1)S(1)}, u32[]{:S(2)}, u32[]{:S(2)}) collective-permute-start(bf16[57,32,128]{2,1,0:T(8,128)(2,1)} %get-tuple-element.42), channel_id=1, source_target_pairs={{0,3},{1,0},{2,1},{3,2},{4,7},{5,4},{6,5},{7,6},{8,11},{9,8},{10,9... | collective-permute-start | bytes 1400840 | tf_op jit(solution)/shard_map/ppermute | solution.py:501
  199.2 20.9 %collective-permute-start.9 = (bf16[57,32,128]{2,1,0:T(8,128)(2,1)}, bf16[57,32,128]{2,1,0:T(8,128)(2,1)S(1)}, u32[]{:S(2)}, u32[]{:S(2)}) collective-permute-start(bf16[57,32,128]{2,1,0:T(8,128)(2,1)} %get-tuple-element.40), channel_id=1, source_target_pairs={{0,1},{1,2},{2,3},{3,0},{4,5},{5,6},{6,7},{7,4},{8,9},{9,10},{10,1... | collective-permute-start | bytes 1400840 | tf_op jit(solution)/shard_map/ppermute | solution.py:501
  207.7 12.3 %copy-start.16 = (bf16[57,32,128]{2,1,0:T(8,128)(2,1)}, bf16[57,32,128]{2,1,0:T(8,128)(2,1)S(1)}, u32[]{:S(2)}) copy-start(bf16[57,32,128]{2,1,0:T(8,128)(2,1)S(1)} %collective-permute-done.10.u2) | copy-start | bytes 1400836
  218.7 1.4 copy-start.17
  220.1 0.8 copy-start.18
  234.0 4.8 %copy-start.13 = (bf16[8,64,512]{2,1,0:T(8,128)(2,1)S(1)}, bf16[8,64,512]{2,1,0:T(8,128)(2,1)}, u32[]{:S(2)}) copy-start(bf16[8,64,512]{2,1,0:T(8,128)(2,1)} %get-tuple-element.43) | copy-start | bytes 1572868
  234.0 14.5 %collective-permute-start.12 = (bf16[8,64,512]{2,1,0:T(8,128)(2,1)}, bf16[8,64,512]{2,1,0:T(8,128)(2,1)S(1)}, u32[]{:S(2)}, u32[]{:S(2)}) collective-permute-start(bf16[8,64,512]{2,1,0:T(8,128)(2,1)} %get-tuple-element.44), channel_id=1, source_target_pairs={{0,1},{1,2},{2,3},{3,0},{4,5},{5,6},{6,7},{7,4},{8,9},{9,10},{10,1... | collective-permute-start | bytes 1572872 | tf_op jit(solution)/shard_map/ppermute | solution.py:501
  235.2 25.1 %collective-permute-start.13 = (bf16[8,64,512]{2,1,0:T(8,128)(2,1)}, bf16[8,64,512]{2,1,0:T(8,128)(2,1)S(1)}, u32[]{:S(2)}, u32[]{:S(2)}) collective-permute-start(bf16[8,64,512]{2,1,0:T(8,128)(2,1)} %get-tuple-element.45), channel_id=1, source_target_pairs={{0,2},{1,3},{2,0},{3,1},{4,6},{5,7},{6,4},{7,5},{8,10},{9,11},{10,... | collective-permute-start | bytes 1572872 | tf_op jit(solution)/shard_map/ppermute | solution.py:501
  237.3 23.0 %collective-permute-start.14 = (bf16[8,64,512]{2,1,0:T(8,128)(2,1)}, bf16[8,64,512]{2,1,0:T(8,128)(2,1)S(1)}, u32[]{:S(2)}, u32[]{:S(2)}) collective-permute-start(bf16[8,64,512]{2,1,0:T(8,128)(2,1)} %get-tuple-element.46), channel_id=1, source_target_pairs={{0,3},{1,0},{2,1},{3,2},{4,7},{5,4},{6,5},{7,6},{8,11},{9,8},{10,9... | collective-permute-start | bytes 1572872 | tf_op jit(solution)/shard_map/ppermute | solution.py:501
  260.3 1.3 copy-start.6
Sparse Core Ops, SparseCore 0:
  9.0 50.6 all-gather.2

commit v2 on v0

v2 whole, which is shorter than its diff:
```python
import functools

import jax
import jax.numpy as jnp
import numpy as np
from jax import lax
from jax.experimental import pallas as pl
from jax.experimental.pallas import tpu as pltpu
from jax.sharding import PartitionSpec as P

GROUP = 8
SIDE = 8
VOX = 512
SLOTS = 32
DEVS = 32
QUART = 8
TILES = 2
FACES = 6 * SLOTS
CODES = 64
EPS = 1e-05
F32 = jnp.float32
BF16 = jnp.bfloat16
HIGH = lax.Precision.HIGHEST
NT = (((1,), (1,)), ((), ()))
NN = (((1,), (0,)), ((), ()))
VMEM = pl.BlockSpec(memory_space=pltpu.VMEM)
ANY = pl.BlockSpec(memory_space=pl.ANY)
HBM = pl.BlockSpec(memory_space=pltpu.HBM)
SMEM = pl.BlockSpec(memory_space=pltpu.SMEM)
MIB = 1024 * 1024
ROWS = 144


def tables():
    places = np.arange(VOX)
    coords = (places // 64, places // 8 % 8, places % 8)
    extract = np.zeros((7 * 64, VOX), np.float32)
    for face in range(6):
        along = face // 2
        others = [coords[k] for k in range(3) if k != along]
        chosen = coords[along] == (0 if face % 2 == 0 else SIDE - 1)
        extract[face * 64 + (8 * others[0] + others[1])[chosen], places[chosen]] = 1.0
    x, y, z = coords
    extract[384 + x // 2 * 16 + y // 2 * 4 + z // 2, places] = 0.125
    return extract


def lanes(rows):
    return lax.broadcasted_iota(jnp.int32, (rows, 128), 1)


def terms(value):
    high = value.astype(BF16).astype(F32)
    rest = value - high
    middle = rest.astype(BF16).astype(F32)
    return high, middle, rest - middle


def joined(block, row):
    return (block[row + 2 : row + 3] + block[row + 1 : row + 2]) + block[row : row + 1]


def put_terms(ref, row, value):
    for k, part in enumerate(terms(value)):
        ref[row + k : row + k + 1, :] = part


def silu(u):
    half = 0.5 * u
    return half + half * jnp.tanh(half)


def group_matrix(period):
    row = lax.broadcasted_iota(jnp.int32, (128, 128), 0) % period // GROUP
    col = lax.broadcasted_iota(jnp.int32, (128, 128), 1) % period // GROUP
    return (row == col).astype(F32)


def group_sum(row, groups=None):
    wide = jnp.broadcast_to(row, (8, 128))
    groups = group_matrix(64) if groups is None else groups
    return lax.dot_general(wide, groups, NN, precision=HIGH, preferred_element_type=F32)[0:1]


def norm_rows(total, square, entries, gain):
    mean = total * (1.0 / entries)
    spread = square * (1.0 / entries) - mean * mean
    return mean, lax.rsqrt(spread + EPS) * gain


def unpack(parts):
    left = lanes(32) < 64
    low, high = [], []
    for a, b in ((parts[0], parts[1]), (parts[2], parts[3])):
        low.append(jnp.where(left, a, pltpu.roll(b, 64, 1)))
        high.append(jnp.where(left, pltpu.roll(a, 64, 1), b))
    return jnp.concatenate(
        [jnp.concatenate(low, axis=1), jnp.concatenate(high, axis=1)], axis=0
    )


def pack(cells):
    left = lanes(32) < 64
    parts = []
    for half in range(2):
        low = cells[0:32, 128 * half : 128 * half + 128]
        high = cells[32:64, 128 * half : 128 * half + 128]
        parts.append(jnp.where(left, low, pltpu.roll(high, 64, 1)))
        parts.append(jnp.where(left, pltpu.roll(low, 64, 1), high))
    return parts


def spread_row(row):
    left = lanes(1) < 64
    parts = []
    for half in range(2):
        part = row[:, 128 * half : 128 * half + 128]
        turned = pltpu.roll(jnp.broadcast_to(part, (8, 128)), 64, 1)[0:1]
        parts.append(jnp.where(left, part, turned))
        parts.append(jnp.where(left, turned, part))
    return parts


def gather_row(rows):
    left = lanes(1) < 64
    return jnp.concatenate(
        [jnp.where(left, rows[0], rows[1]), jnp.where(left, rows[2], rows[3])], axis=1
    )


def extract_kernel(links, csend, feats, table, faces, out, held, pooled, acc, stat, send_buf, sem):
    step = pl.program_id(0)
    left = lanes(32) < 64

    @pl.when(step == 0)
    def _():
        acc[...] = jnp.zeros((192, 128), F32)

    rows = []
    s = jnp.zeros((64, 128), F32)
    q = jnp.zeros((64, 128), F32)
    ps = jnp.zeros((32, 128), F32)
    pq = jnp.zeros((32, 128), F32)
    for k in range(4):
        x = feats[k]
        rows += [x, x]
        wide = x.astype(F32)
        for v in range(4):
            piece = wide[:, 128 * v : 128 * v + 128]
            s = s + piece
            q = q + piece * piece
    layers = lax.dot_general(
        table[...], jnp.concatenate(rows, axis=0), NT, preferred_element_type=F32
    )
    for k in range(4):
        for f in range(7):
            low = layers[64 * f : 64 * f + 32, 128 * k : 128 * k + 128]
            high = layers[64 * f + 32 : 64 * f + 64, 128 * k : 128 * k + 128]
            unit = jnp.where(left, low, high).astype(BF16)
            if f < 6:
                held[(4 * step + k) * 6 + f] = unit
            else:
                pooled[4 * step + k] = unit
                wide = unit.astype(F32)
                ps = ps + wide
                pq = pq + wide * wide
    acc[0:64, :] += s
    acc[64:128, :] += q
    acc[128:160, :] += ps
    acc[160:192, :] += pq

    @pl.when(step == pl.num_programs(0) - 1)
    def _():
        keep = pltpu.make_async_copy(held, faces, sem.at[0])
        keep.start()
        ones = jnp.ones((8, 128), F32)

        def by_lane(sums):
            twice = jnp.concatenate([sums, sums], axis=0)
            return lax.dot_general(ones, twice, NT, precision=HIGH, preferred_element_type=F32)[0:1]

        stat[...] = jnp.zeros((16, 128), F32)
        put_terms(stat, 0, by_lane(acc[0:64, :]))
        put_terms(stat, 3, by_lane(acc[64:128, :]))
        put_terms(stat, 6, jnp.sum(acc[128:160, :], axis=0, keepdims=True))
        put_terms(stat, 9, jnp.sum(acc[160:192, :], axis=0, keepdims=True))
        sums = stat[...].astype(BF16)

        def send(p, _):
            for k in range(2):
                send_buf[p, 32 * k : 32 * k + 32] = held[jnp.minimum(links[k, p], FACES - 1)]
                send_buf[p, 64 + 32 * k : 96 + 32 * k] = pooled[
                    jnp.minimum(csend[k, p], SLOTS - 1)
                ]
            send_buf[p, 128:144] = sums
            return 0

        lax.fori_loop(0, DEVS, send, 0, unroll=4)
        give = pltpu.make_async_copy(send_buf, out, sem.at[1])
        give.start()
        keep.wait()
        give.wait()


def plan_kernel(nbr, links, csend, crecv, sel, tsel, ssel):
    def slot_of(n, _):
        for f in range(6):
            near = nbr[f, n]
            sel[n * 6 + f] = jnp.where(near < SLOTS, near * 6 + (f ^ 1), FACES + 2 * DEVS)
        return 0

    lax.fori_loop(0, SLOTS, slot_of, 0)

    def empty(i, _):
        tsel[i] = 2 * DEVS
        return 0

    lax.fori_loop(0, CODES, empty, 0)

    def mark(p, _):
        for k in range(2):
            code = links[k, p]

            @pl.when(code < FACES)
            def _():
                sel[code] = FACES + 2 * p + k

            place = crecv[k, p]

            @pl.when(place < CODES)
            def _():
                tsel[place] = 2 * p + k

            slot = csend[k, p]

            @pl.when(slot < SLOTS)
            def _():
                ssel[slot] = 2 * p + k

        return 0

    lax.fori_loop(0, DEVS, mark, 0)


def octant1_kernel(tsel, me, recv, par, x1, x2, x3, o0, o1, o2, o3, own, buf, stat, sem):
    y = me[0]

    def add(s, total):
        return total + recv[s, 128:144].astype(F32)

    sums = lax.fori_loop(0, DEVS, add, jnp.zeros((16, 128), F32), unroll=8)
    fine = float(DEVS * SLOTS * VOX * GROUP)
    rough = float(DEVS * SLOTS * 64 * GROUP)
    mean1, scale1 = norm_rows(
        group_sum(joined(sums, 0)) * 0.5, group_sum(joined(sums, 3)) * 0.5, fine, par[0:1]
    )
    mean3, scale3 = norm_rows(
        group_sum(joined(sums, 6)), group_sum(joined(sums, 9)), rough, par[2:3]
    )
    bias1, bias3 = par[1:2], par[3:4]
    own[0:1, :] = mean1
    own[1:2, :] = scale1
    own[2:3, :] = bias1
    stat[...] = jnp.zeros((32, 128), F32)
    put_terms(stat, 0, mean1)
    put_terms(stat, 3, scale1)
    put_terms(stat, 6, bias1)
    put_terms(stat, 9, par[4:5])
    put_terms(stat, 12, par[5:6])
    put_terms(stat, 15, par[6:7])
    told = stat[...].astype(BF16)
    copies = []
    for r, o in enumerate((o0, o1, o2, o3)):
        q = (y + r) & 3
        buf[r, 16] = told

        def octant(i, _):
            for k in range(4):
                far = tsel[q * 16 + i * 4 + k]
                link = jnp.minimum(far, 2 * DEVS - 1)
                at = pl.multiple_of(64 + 32 * (link & 1), 32)
                u = recv[link >> 1, pl.ds(at, 32)].astype(F32)
                v = silu((u - mean3) * scale3 + bias3)
                buf[r, i * 4 + k] = (v * (far < 2 * DEVS).astype(F32)).astype(BF16)
            return 0

        lax.fori_loop(0, 4, octant, 0)
        copies.append(pltpu.make_async_copy(buf.at[r], o, sem.at[r]))
        copies[-1].start()
    for copy in copies:
        copy.wait()


def border1_kernel(sel, me, own, faces, recv, o0, o1, o2, o3, src, buf, sem, load):
    y = me[0]
    fetch = pltpu.make_async_copy(faces, src.at[pl.ds(0, FACES)], load)
    fetch.start()

    def place(s, _):
        src[FACES + 2 * s] = recv[s, 0:32]
        src[FACES + 2 * s + 1] = recv[s, 32:64]
        return 0

    lax.fori_loop(0, DEVS, place, 0, unroll=4)
    src[FACES + 2 * DEVS] = jnp.zeros((32, 128), BF16)
    mean, scale, bias = own[0:1], own[1:2], own[2:3]
    fetch.wait()
    copies = []
    for r, o in enumerate((o0, o1, o2, o3)):
        q = (y + r) & 3

        def face(i, _):
            for f in range(6):
                at = sel[q * 48 + i * 6 + f]
                u = src[at].astype(F32)
                v = silu((u - mean) * scale + bias)
                buf[r, i * 6 + f] = (v * (at < FACES + 2 * DEVS).astype(F32)).astype(BF16)
            return 0

        lax.fori_loop(0, QUART, face, 0)
        copies.append(pltpu.make_async_copy(buf.at[r], o, sem.at[r]))
        copies[-1].start()
    for copy in copies:
        copy.wait()


def interior_taps(act, taps):
    wide = act.astype(F32)
    cube = wide.reshape(8, 8, 8, 256)
    none = jnp.zeros((64, 256), BF16)
    wall = jnp.zeros((8, 1, 8, 256), F32)
    taps[:, 0:256] = act
    taps[0:64, 256:512] = none
    taps[64:512, 256:512] = act[0:448]
    taps[0:448, 512:768] = act[64:512]
    taps[448:512, 512:768] = none
    low = jnp.concatenate([wall, cube[:, 0:7]], axis=1)
    taps[:, 768:1024] = low.reshape(512, 256).astype(BF16)
    high = jnp.concatenate([cube[:, 1:8], wall], axis=1)
    taps[:, 1024:1280] = high.reshape(512, 256).astype(BF16)
    depth = lax.broadcasted_iota(jnp.int32, (512, 256), 0) % 8
    low = jnp.where(depth == 0, 0.0, pltpu.roll(wide, 1, 0))
    taps[:, 1280:1536] = low.astype(BF16)
    high = jnp.where(depth == 7, 0.0, pltpu.roll(wide, 511, 0))
    taps[:, 1536:1792] = high.astype(BF16)


def halves(first, second, core, which):
    def pieces(c, t):
        for side, part in enumerate((first, second)):
            yield pl.multiple_of(64 * c + 32 * (core ^ side), 32), part[c, which, t]

    return pieces


def fill_weights(dst, pieces):
    for c in range(4):
        for t in range(7):
            for at, rows in pieces(c, t):
                dst[pl.ds(at, rows.shape[0]), 256 * t : 256 * t + 256] = rows


def fill_tap_weights(dst, pieces):
    for c in range(4):
        for f in range(6):
            for at, rows in pieces(c, 1 + f):
                dst[f, pl.ds(at, rows.shape[0]), :] = rows


def fill_cube(cube, volumes, y):
    for r, v in enumerate(volumes):
        at = pl.multiple_of(((y - r) & 3) * 64, 64)
        cube[pl.ds(at, 64), :] = v[0].astype(F32)


def place_rows(rows, told, y, stat):
    rows[...] = jnp.zeros((8, 256), F32)
    for r, t in enumerate(told):
        stat[(y - r) & 3] = t[0].astype(F32)
    for k in range(6):
        rows[k : k + 1, :] = gather_row([joined(stat[c], 3 * k) for c in range(4)])


def inner1_kernel(
    me, t0, t1, t2, t3, v0, v1, v2, v3, wa, wb, part, rows, weights, stat, taps, cube
):
    y = me[0]

    @pl.when(pl.program_id(0) == 0)
    def _():
        place_rows(rows, (t0, t1, t2, t3), y, stat)
        fill_weights(weights, halves(wa, wb, me[1], 0))

    fill_cube(cube, (v0, v1, v2, v3), y)
    x = cube[...].T
    act = silu((x - rows[0:1]) * rows[1:2] + rows[2:3]).astype(BF16)
    interior_taps(act, taps)
    part[0] = lax.dot_general(taps[...], weights[...], NT, preferred_element_type=F32)


def inner2_kernel(me, rows, hid, wa, wb, part, weights, taps, cells, sem):
    step = pl.program_id(0)

    def fetch_cells(n):
        return pltpu.make_async_copy(hid.at[n], cells.at[n], sem.at[n])

    @pl.when(step == 0)
    def _():
        for n in range(QUART):
            fetch_cells(n).start()
        fill_weights(weights, halves(wa, wb, me[1], 1))

    fetch_cells(step).wait()
    act = silu((cells[step] - rows[0:1]) * rows[1:2] + rows[2:3]).astype(BF16)
    interior_taps(act, taps)
    part[0] = lax.dot_general(taps[...], weights[...], NT, preferred_element_type=F32)


def border_terms(units, tap_weights, parts, y, across):
    for r, u in enumerate(parts):
        units[(y - r) & 3] = u[...]
    for f in range(6):
        layer = jnp.concatenate(
            [
                unpack([units[c, 6 * n + f].astype(F32) for c in range(4)]).astype(BF16)
                for n in range(QUART)
            ],
            axis=0,
        )
        across[f] = lax.dot_general(layer, tap_weights[f], NT, preferred_element_type=F32)


def add_borders(h, across, step, shift):
    at = pl.multiple_of(step * 64, 64)
    h = jnp.concatenate(
        [h[0:64] + across[0, pl.ds(at, 64), :], h[64:448], h[448:512] + across[1, pl.ds(at, 64), :]],
        axis=0,
    )
    deep = h.reshape(8, 8, 8, 256)
    low = across[2, pl.ds(at, 64), :].reshape(8, 1, 8, 256)
    high = across[3, pl.ds(at, 64), :].reshape(8, 1, 8, 256)
    h = jnp.concatenate([deep[:, 0:1] + low, deep[:, 1:7], deep[:, 7:8] + high], axis=1)
    h = h.reshape(512, 256)
    halves, edges = [], [[], []]
    for half in range(2):
        cut = slice(128 * half, 128 * half + 128)
        shift[half] = h[:, cut]
        for side in range(2):
            layer = shift[half, pl.ds(7 * side, 64, stride=8), :]
            layer = layer + across[4 + side, pl.ds(at, 64), cut]
            shift[half, pl.ds(7 * side, 64, stride=8), :] = layer
            edges[side].append(layer)
        halves.append(shift[half])
    h = jnp.concatenate(halves, axis=1)
    return h, [jnp.concatenate(pair, axis=1) for pair in edges]


def outer1_kernel(
    me, rows, part, u0, u1, u2, u3, tiles, wa, wb,
    hid, o0, o1, o2, o3,
    units, outs, weights, across, shift, stat, sums, cells, sem,
):
    step = pl.program_id(0)
    y = me[0]

    def keep_cells(n):
        return pltpu.make_async_copy(cells.at[n], hid.at[n], sem.at[n])

    @pl.when(step == 0)
    def _():
        fill_tap_weights(weights, halves(wa, wb, me[1], 0))
        border_terms(units, weights, (u0, u1, u2, u3), y, across)
        sums[...] = jnp.zeros((8, 256), F32)
        stat[...] = jnp.zeros((4, 32, 128), F32)

    h, edges = add_borders(part[0] + rows[3:4], across, step, shift)
    cells[step] = h
    keep_cells(step).start()
    total = jnp.sum(h, axis=0, keepdims=True)
    sums[0:1] += total
    sums[1:2] += jnp.sum(h * h, axis=0, keepdims=True)
    centre = (total * (1.0 / VOX)).astype(BF16).astype(F32)
    for c, row in enumerate(spread_row(centre)):
        stat[c, pl.ds(step, 1), :] = row
    deep = h.reshape(8, 8, 8, 256)
    for f in range(6):
        if f < 2:
            layer = h[448 * f : 448 * f + 64]
        elif f < 4:
            layer = deep[:, 7 * (f - 2)].reshape(64, 256)
        else:
            layer = edges[f - 4]
        for c, unit in enumerate(pack(layer - centre)):
            outs[c, step * 6 + f] = unit.astype(BF16)

    @pl.when(step == QUART - 1)
    def _():
        at = 8
        for k in range(2):
            for half in range(2):
                for row in terms(sums[k : k + 1, 128 * half : 128 * half + 128]):
                    for c in range(4):
                        stat[c, at : at + 1, :] = row
                    at += 1
        for c in range(4):
            outs[c, 48] = stat[c].astype(BF16)
        for r, o in enumerate((o0, o1, o2, o3)):
            o[0:49] = outs[(y + r) & 3]
            o[49:65] = tiles[(y + r) & 3]
        for n in range(QUART):
            keep_cells(n).wait()


def placement(rows, columns, code):
    row = lax.broadcasted_iota(jnp.int32, (rows, columns), 0)
    column = lax.broadcasted_iota(jnp.int32, (rows, columns), 1)
    return (code(row) == column).astype(F32).astype(BF16)


def octant_code(v):
    x, y, z = v >> 6, (v >> 3) & 7, v & 7
    octant = (x >> 2) * 4 + (y >> 2) * 2 + (z >> 2)
    return octant * 64 + (x & 3) * 16 + (y & 3) * 4 + (z & 3)


def voxel_code(w):
    octant, x, y, z = w >> 6, (w >> 4) & 3, (w >> 2) & 3, w & 3
    x, y, z = x + 4 * (octant >> 2), y + 4 * ((octant >> 1) & 1), z + 4 * (octant & 1)
    return x * 64 + y * 8 + z


def coarse_code(v):
    return ((v >> 7) & 3) * 16 + ((v >> 4) & 3) * 4 + ((v >> 1) & 3)


def tile_kernel(me, u0, u1, u2, u3, wa, wb, out, units, weights, taps, place, place_t):
    t = pl.program_id(0)
    y = me[0]

    @pl.when(t == 0)
    def _():
        place[...] = placement(VOX, VOX, octant_code)
        place_t[...] = placement(VOX, VOX, voxel_code)
        fill_weights(weights, halves(wa, wb, me[1], 2))

    for r, u in enumerate((u0, u1, u2, u3)):
        units[(y - r) & 3] = u[...]
    octants = jnp.concatenate(
        [unpack([units[c, o].astype(F32) for c in range(4)]).astype(BF16) for o in range(8)], axis=0
    )
    act = lax.dot_general(place[...], octants, NN, preferred_element_type=F32).astype(BF16)
    interior_taps(act, taps)
    h = lax.dot_general(taps[...], weights[...], NT, preferred_element_type=F32).astype(BF16)
    pieces = lax.dot_general(place_t[...], h, NN, preferred_element_type=F32)
    for o in range(8):
        for c, unit in enumerate(pack(pieces[64 * o : 64 * o + 64])):
            out[c, o] = unit.astype(BF16)


def route2_kernel(
    links, crecv, me, v0, v1, v2, v3, keep, out, held, cen, stat, send_buf, sem
):
    y = me[0]
    for r, v in enumerate((v0, v1, v2, v3)):
        held[(y - r) & 3] = v[...]
    kept = pltpu.make_async_copy(held, keep, sem.at[0])
    kept.start()
    total = jnp.zeros((32, 128), F32)
    for q in range(4):
        told = held[q, 48].astype(F32)
        cen[8 * q : 8 * q + 8, :] = told[0:8]
        total = total + told
    stat[...] = jnp.zeros((16, 128), F32)
    for k in range(4):
        put_terms(stat, 2 + 3 * k, joined(total, 8 + 3 * k))

    def send(p, _):
        for k in range(2):
            code = jnp.minimum(links[k, p], FACES - 1)
            slot = lax.div(code, 6)
            q = slot >> 3
            send_buf[p, 32 * k : 32 * k + 32] = held[q, code - 48 * q]
            stat[k : k + 1, :] = cen[pl.ds(slot, 1), :]
            place = jnp.minimum(crecv[k, p], CODES - 1)
            send_buf[p, 64 + 32 * k : 96 + 32 * k] = held[place >> 4, 49 + (place & 15)]
        send_buf[p, 128:144] = stat[...].astype(BF16)
        return 0

    lax.fori_loop(0, DEVS, send, 0, unroll=4)
    give = pltpu.make_async_copy(send_buf, out, sem.at[1])
    give.start()
    kept.wait()
    give.wait()


def own_row(row, y):
    wide = jnp.broadcast_to(jnp.where(y >= 2, row[:, 128:256], row[:, 0:128]), (8, 128))
    turned = pltpu.roll(wide, 64, 1)
    left = lanes(8) < 64
    odd = (y & 1) == 1
    return jnp.where(left, jnp.where(odd, turned, wide), jnp.where(odd, wide, turned))[0:1]


def border2_kernel(
    sel, ssel, me, rows, held, recv, o0, o1, o2, o3, norm, src, cen, buf, sem, load
):
    y = me[0]
    fetches = []
    for q in range(4):
        fetches.append(
            pltpu.make_async_copy(held.at[q, pl.ds(0, 48)], src.at[pl.ds(48 * q, 48)], load.at[q])
        )
        fetches.append(pltpu.make_async_copy(held.at[q, 48], buf.at[q, 0], load.at[4 + q]))
    for fetch in fetches:
        fetch.start()

    def add(s, total):
        src[FACES + 2 * s] = recv[s, 0:32]
        src[FACES + 2 * s + 1] = recv[s, 32:64]
        told = recv[s, 128:144].astype(F32)
        cen[pl.ds(SLOTS + 2 * s, 2), :] = told[0:2]
        return total + told

    sums = lax.fori_loop(0, DEVS, add, jnp.zeros((16, 128), F32), unroll=8)
    src[FACES + 2 * DEVS] = jnp.zeros((32, 128), BF16)
    cen[pl.ds(SLOTS + 2 * DEVS, 8), :] = jnp.zeros((8, 128), F32)
    fine = float(DEVS * SLOTS * VOX * GROUP)
    groups = group_matrix(128)
    norm[...] = jnp.zeros((8, 256), F32)
    for half in range(2):
        cut = slice(128 * half, 128 * half + 128)
        mean, scale = norm_rows(
            group_sum(joined(sums, 2 + 3 * half), groups),
            group_sum(joined(sums, 8 + 3 * half), groups),
            fine,
            rows[4:5, cut],
        )
        norm[0:1, cut] = mean
        norm[1:2, cut] = scale
        norm[2:3, cut] = rows[5:6, cut]
    mean, scale, bias = (own_row(norm[k : k + 1, :], y) for k in range(3))
    for fetch in fetches:
        fetch.wait()
    for q in range(4):
        cen[8 * q : 8 * q + 8, :] = buf[q, 0].astype(F32)[0:8]
    copies = []
    for r, o in enumerate((o0, o1, o2, o3)):
        q = (y + r) & 3

        def face(i, _):
            for f in range(6):
                at = sel[q * 48 + i * 6 + f]
                owner = jnp.where(at < FACES, lax.div(at, 6), at - (FACES - SLOTS))
                u = src[at].astype(F32) + (cen[pl.ds(owner, 1), :] - mean)
                v = silu(u * scale + bias)
                buf[r, i * 6 + f] = (v * (at < FACES + 2 * DEVS).astype(F32)).astype(BF16)
            link = ssel[q * 8 + i]
            at = pl.multiple_of(64 + 32 * (link & 1), 32)
            buf[r, 48 + i] = recv[link >> 1, pl.ds(at, 32)]
            return 0

        lax.fori_loop(0, QUART, face, 0)
        copies.append(pltpu.make_async_copy(buf.at[r], o, sem.at[r]))
        copies[-1].start()
    for copy in copies:
        copy.wait()


def outer2_kernel(
    me, part, v0, v1, v2, v3, u0, u1, u2, u3, wa, wb,
    o0, o1, o2, o3,
    units, weights, across, shift, cube, lift,
):
    step = pl.program_id(0)
    y = me[0]

    @pl.when(step == 0)
    def _():
        lift[...] = placement(VOX, 64, coarse_code)
        fill_tap_weights(weights, halves(wa, wb, me[1], 1))
        border_terms(units, weights, (u0, u1, u2, u3), y, across)

    raised = unpack([units[c, 48 + step].astype(F32) for c in range(4)]).astype(BF16)
    lifted = lax.dot_general(lift[...], raised, NN, preferred_element_type=F32)
    h, _ = add_borders(part[0] + lifted, across, step, shift)
    fill_cube(cube, (v0, v1, v2, v3), y)
    cube[...] += h.T
    for r, o in enumerate((o0, o1, o2, o3)):
        at = pl.multiple_of(((y + r) & 3) * 64, 64)
        o[0] = cube[pl.ds(at, 64), :].astype(BF16)


def gather_kernel(me, p0, p1, p2, p3, out, sem):
    y = me[0]
    copies = []
    for r, p in enumerate((p0, p1, p2, p3)):
        at = pl.multiple_of(((y - r) & 3) * QUART, QUART)
        copies.append(pltpu.make_async_copy(p, out.at[pl.ds(at, QUART)], sem.at[r]))
        copies[-1].start()
    for copy in copies:
        copy.wait()


def shape(*dims, dtype=BF16):
    return jax.ShapeDtypeStruct(dims, dtype)


def call(kernel, name, mib, micros=1, **more):
    return pl.pallas_call(
        kernel,
        cost_estimate=pl.CostEstimate(
            flops=micros * 10**9, bytes_accessed=micros * 3 * 10**6, transcendentals=0
        ),
        compiler_params=pltpu.CompilerParams(vmem_limit_bytes=mib * MIB),
        name=name,
        **more,
    )


def exchange(parts, order=(0, 1, 2, 3)):
    got = {
        r: lax.ppermute(parts[r], "chan", [(i, (i + r) % 4) for i in order]) for r in (2, 1, 3)
    }
    return [parts[0], got[1], got[2], got[3]]


def over_blocks(units):
    return lax.all_to_all(units, "blocks", split_axis=0, concat_axis=0, tiled=True)


def local(
    feats,
    conv_weights,
    norm_gain,
    norm_bias,
    time_bias,
    local_nbr,
    face_links,
    coarse_send,
    coarse_recv,
):
    extract_np = tables()
    y = lax.axis_index("chan").astype(jnp.int32)
    core = (lax.axis_index("blocks") % 2).astype(jnp.int32)
    me = jnp.stack([y, core])
    nbr = local_nbr.T
    links = face_links[0].T
    csend = coarse_send[0].T
    crecv = coarse_recv[0].T

    def twice(rows):
        block = jnp.stack(rows)
        block = jnp.concatenate([block, block], axis=1)
        return jnp.pad(block, ((0, 8 - block.shape[0]), (0, 0)))

    par = twice(
        [norm_gain[0], norm_bias[0], norm_gain[2], norm_bias[2], time_bias]
        + [norm_gain[1], norm_bias[1]]
    )
    half = lax.dynamic_slice_in_dim(conv_weights, 32 * core, 32, axis=2)
    wa = lax.all_gather(half, "chan", axis=0, tiled=False)

    faces, outgoing = call(
        extract_kernel,
        "extract",
        60,
        grid=(8,),
        out_shape=(shape(FACES, 32, 128), shape(DEVS, ROWS, 128)),
        in_specs=[SMEM, SMEM, pl.BlockSpec((4, 64, VOX), lambda i: (i, 0, 0)), VMEM],
        out_specs=(HBM, HBM),
        scratch_shapes=[
            pltpu.VMEM((FACES, 32, 128), BF16),
            pltpu.VMEM((SLOTS, 32, 128), BF16),
            pltpu.VMEM((192, 128), F32),
            pltpu.VMEM((16, 128), F32),
            pltpu.VMEM((DEVS, ROWS, 128), BF16),
            pltpu.SemaphoreType.DMA((2,)),
        ],
    )(links, csend, feats, jnp.asarray(extract_np, BF16))
    arrived = over_blocks(outgoing)
    volumes = exchange(
        [
            lax.dynamic_slice_in_dim(feats, QUART * ((y + r) % 4), QUART, axis=0)
            for r in range(4)
        ]
    )
    sel, tsel, ssel = call(
        plan_kernel,
        "plan",
        4,
        20,
        out_shape=(
            shape(FACES, dtype=jnp.int32),
            shape(CODES, dtype=jnp.int32),
            shape(SLOTS, dtype=jnp.int32),
        ),
        in_specs=[SMEM] * 4,
        out_specs=(SMEM,) * 3,
    )(nbr, links, csend, crecv)

    *parts, own = call(
        octant1_kernel,
        "octant1",
        8,
        out_shape=(shape(17, 32, 128),) * 4 + (shape(8, 128, dtype=F32),),
        in_specs=[SMEM] * 2 + [VMEM] * 2 + [HBM] * 3,
        out_specs=(ANY,) * 4 + (VMEM,),
        scratch_shapes=[
            pltpu.VMEM((4, 17, 32, 128), BF16),
            pltpu.VMEM((32, 128), F32),
            pltpu.SemaphoreType.DMA((4,)),
        ],
    )(tsel, me, arrived, par, *volumes[1:])
    tiles1 = exchange(parts, (3, 2, 1, 0))
    wa, _ = lax.optimization_barrier((wa, own))
    wb = lax.ppermute(wa, "blocks", [(i, i ^ 1) for i in range(DEVS)])
    parts = call(
        border1_kernel,
        "border1",
        12,
        out_shape=(shape(48, 32, 128),) * 4,
        in_specs=[SMEM] * 2 + [VMEM, HBM, VMEM],
        out_specs=(ANY,) * 4,
        scratch_shapes=[
            pltpu.VMEM((FACES + 2 * DEVS + 1, 32, 128), BF16),
            pltpu.VMEM((4, 48, 32, 128), BF16),
            pltpu.SemaphoreType.DMA((4,)),
            pltpu.SemaphoreType.DMA,
        ],
    )(sel, me, own, faces, arrived)
    units1 = exchange(parts)

    slots = pl.BlockSpec((1, 64, VOX), lambda i: (i, 0, 0))
    cells = pl.BlockSpec((1, VOX, 256), lambda i: (i, 0, 0))
    last = pl.BlockSpec((1, 32, 128), lambda i: (16, 0, 0))
    part1, rows = call(
        inner1_kernel,
        "inner1",
        24,
        8,
        grid=(QUART,),
        out_shape=(shape(QUART, VOX, 256, dtype=F32), shape(8, 256, dtype=F32)),
        in_specs=[SMEM] + [last] * 4 + [slots] * 4 + [VMEM] * 2,
        out_specs=(cells, VMEM),
        scratch_shapes=[
            pltpu.VMEM((256, 1792), BF16),
            pltpu.VMEM((4, 32, 128), F32),
            pltpu.VMEM((VOX, 1792), BF16),
            pltpu.VMEM((256, VOX), F32),
        ],
    )(me, *tiles1, *volumes, wa, wb)
    eight = pl.BlockSpec((8, 32, 128), lambda t: (t, 0, 0))
    coarse = call(
        tile_kernel,
        "tiles",
        24,
        4,
        grid=(TILES,),
        out_shape=shape(4, 16, 32, 128),
        in_specs=[SMEM] + [eight] * 4 + [VMEM] * 2,
        out_specs=pl.BlockSpec((4, 8, 32, 128), lambda t: (0, t, 0, 0)),
        scratch_shapes=[
            pltpu.VMEM((4, 8, 32, 128), BF16),
            pltpu.VMEM((256, 1792), BF16),
            pltpu.VMEM((VOX, 1792), BF16),
            pltpu.VMEM((VOX, VOX), BF16),
            pltpu.VMEM((VOX, VOX), BF16),
        ],
    )(me, *tiles1, wa, wb)
    hidden, *parts = call(
        outer1_kernel,
        "outer1",
        32,
        5,
        grid=(QUART,),
        out_shape=(shape(QUART, VOX, 256, dtype=F32),) + (shape(65, 32, 128),) * 4,
        in_specs=[SMEM, VMEM, cells] + [VMEM] * 7,
        out_specs=(HBM,) + (VMEM,) * 4,
        scratch_shapes=[
            pltpu.VMEM((4, 48, 32, 128), BF16),
            pltpu.VMEM((4, 49, 32, 128), BF16),
            pltpu.VMEM((6, 256, 256), BF16),
            pltpu.VMEM((6, VOX, 256), F32),
            pltpu.VMEM((2, VOX, 128), F32),
            pltpu.VMEM((4, 32, 128), F32),
            pltpu.VMEM((8, 256), F32),
            pltpu.VMEM((QUART, VOX, 256), F32),
            pltpu.SemaphoreType.DMA((QUART,)),
        ],
    )(me, rows, part1, *units1, coarse, wa, wb)
    units = exchange(parts)

    held, outgoing = call(
        route2_kernel,
        "route2",
        12,
        out_shape=(shape(4, 65, 32, 128), shape(DEVS, ROWS, 128)),
        in_specs=[SMEM] * 3 + [VMEM] * 4,
        out_specs=(HBM, HBM),
        scratch_shapes=[
            pltpu.VMEM((4, 65, 32, 128), BF16),
            pltpu.VMEM((SLOTS, 128), F32),
            pltpu.VMEM((16, 128), F32),
            pltpu.VMEM((DEVS, ROWS, 128), BF16),
            pltpu.SemaphoreType.DMA((2,)),
        ],
    )(links, crecv, me, *units)
    arrived = over_blocks(outgoing)

    *parts, norm = call(
        border2_kernel,
        "border2",
        12,
        out_shape=(shape(56, 32, 128),) * 4 + (shape(8, 256, dtype=F32),),
        in_specs=[SMEM] * 3 + [VMEM, HBM, VMEM],
        out_specs=(ANY,) * 4 + (VMEM,),
        scratch_shapes=[
            pltpu.VMEM((FACES + 2 * DEVS + 1, 32, 128), BF16),
            pltpu.VMEM((SLOTS + 2 * DEVS + 8, 128), F32),
            pltpu.VMEM((4, 56, 32, 128), BF16),
            pltpu.SemaphoreType.DMA((4,)),
            pltpu.SemaphoreType.DMA((8,)),
        ],
    )(sel, ssel, me, rows, held, arrived)
    units2 = exchange(parts)
    part2 = call(
        inner2_kernel,
        "inner2",
        24,
        8,
        grid=(QUART,),
        out_shape=shape(QUART, VOX, 256, dtype=F32),
        in_specs=[SMEM, VMEM, HBM, VMEM, VMEM],
        out_specs=cells,
        scratch_shapes=[
            pltpu.VMEM((256, 1792), BF16),
            pltpu.VMEM((VOX, 1792), BF16),
            pltpu.VMEM((QUART, VOX, 256), F32),
            pltpu.SemaphoreType.DMA((QUART,)),
        ],
    )(me, norm, hidden, wa, wb)
    parts = call(
        outer2_kernel,
        "outer2",
        32,
        5,
        grid=(QUART,),
        out_shape=(shape(QUART, 64, VOX),) * 4,
        in_specs=[SMEM, cells] + [slots] * 4 + [VMEM] * 6,
        out_specs=(slots,) * 4,
        scratch_shapes=[
            pltpu.VMEM((4, 56, 32, 128), BF16),
            pltpu.VMEM((6, 256, 256), BF16),
            pltpu.VMEM((6, VOX, 256), F32),
            pltpu.VMEM((2, VOX, 128), F32),
            pltpu.VMEM((256, VOX), F32),
            pltpu.VMEM((VOX, 64), BF16),
        ],
    )(me, part2, *volumes, *units2, wa, wb)
    parts = exchange(parts)
    return call(
        gather_kernel,
        "gather",
        4,
        out_shape=shape(SLOTS, 64, VOX),
        in_specs=[SMEM] + [ANY] * 4,
        out_specs=HBM,
        scratch_shapes=[pltpu.SemaphoreType.DMA((4,))],
    )(me, *parts)


def solution(mesh):
    in_specs = (
        P("blocks", "chan", None),
        P(None, None, "chan", None),
        P(None, "chan"),
        P(None, "chan"),
        P("chan"),
        P("blocks", None),
        P("blocks", None, None),
        P("blocks", None, None),
        P("blocks", None, None),
    )
    out_specs = P("blocks", "chan", None)
    return jax.shard_map(local, mesh=mesh, in_specs=in_specs, out_specs=out_specs, check_vma=False)
```

time: 781 us -> 220 us (0.28); the launches traced: 772 us -> 219 us
  matrix products: 187 us -> 0 us
  local copies, waits for them, and re-layouts: 172 us -> 8.69 us
  blocking collectives: 167 us -> 25.3 us
  waiting for transfers between devices: 176 us -> 78.9 us
  Pallas kernels: 0 us -> 56.3 us
  other arithmetic: 46.2 us -> 0.15 us
  starting transfers between devices: 8.75 us -> 36 us
    dot_general x22 -> x0, matrix products: 187 us -> none  [the longest x12 98 us: add_taps(): jnp.einsum('bcu,vu->bcv', border[:, which_face], table, preferred_element...]
    all_gather x5 -> x1, waiting for transfers between devices: 166 us -> 0.01 us  [local(): wa = lax.all_gather(half, 'chan', axis=0, tiled=False)]
    psum x2 -> x0, blocking collectives: 128 us -> none  [global_sums(): return lax.psum(stacked, 'blocks')]
    ppermute x0 -> x19, waiting for transfers between devices: none -> 75.8 us  [the longest x18 75.8 us: exchange(): lax.ppermute(parts[r], 'chan', [(i, (i + r) % 4) for i in order])]
    pallas_call x0 -> x12, Pallas kernels: none -> 56.3 us  [the longest x1 8.04 us: local(): call(extract_kernel, 'extract', 60, grid=(8,), out_shape=(shape(FACES, 32...]
    slice x9 -> x1, local copies, waits for them, and re-layouts: 53.4 us -> 0.01 us  [local(): norm_bias[1]]
    gather x14 -> x0, local copies, waits for them, and re-layouts: 47.3 us -> none  [the longest x2 21.5 us: build_border(): nearby = jnp.concatenate([layers, blank], axis=0)[local_src]]
    ppermute x0 -> x19, starting transfers between devices: none -> 26.4 us  [the longest x18 24.9 us: exchange(): lax.ppermute(parts[r], 'chan', [(i, (i + r) % 4) for i in order])]
  transfers between devices with their start and end apart: 7 -> 21, of which waited for: 5 -> 11; matrix products, arithmetic and copies ran while one was open for 12% -> 1% of each run, Pallas kernels for 0% -> 16%
where the time goes in v2:
time: 220 us; the launch traced here: 219 us
  waiting for transfers between devices  78.9 us (36%)
  Pallas kernels  56.3 us (26%)
  starting transfers between devices  36 us (16%)
  blocking collectives  25.3 us (12%)
  between operations  13.7 us (6%)
  local copies, waits for them, and re-layouts  8.69 us (4%)
    ppermute x18, waiting for transfers between devices, exchange(): lax.ppermute(parts[r], 'chan', [(i, (i + r) % 4) for i in order])  75.8 us
    all_to_all x1, blocking collectives, over_blocks(): lax.all_to_all(units, 'blocks', split_axis=0, concat_axis=0, tiled=True)  25.3 us
    ppermute x18, starting transfers between devices, exchange(): lax.ppermute(parts[r], 'chan', [(i, (i + r) % 4) for i in order])  24.9 us
    all_to_all x1, starting transfers between devices, over_blocks(): lax.all_to_all(units, 'blocks', split_axis=0, concat_axis=0, tiled=True)  9.56 us
    pallas_call x1, Pallas kernels, local(): call(extract_kernel, 'extract', 60, grid=(8,), out_shape=(shape(FACES, 32...  8.04 us
    pallas_call x1, Pallas kernels, local(): call(outer2_kernel, 'outer2', 32, 5, grid=(QUART,), out_shape=(shape(QUAR...  7.85 us
    pallas_call x1, Pallas kernels, local(): call(inner1_kernel, 'inner1', 24, 8, grid=(QUART,), out_shape=(shape(QUAR...  7.53 us
    pallas_call x1, Pallas kernels, local(): call(inner2_kernel, 'inner2', 24, 8, grid=(QUART,), out_shape=shape(QUART...  6.73 us
  transfers between devices with their start and end apart: 21, of which 11 were waited for; matrix products, arithmetic and copies ran while one was open for 1% of the time, Pallas kernels for 16%

profile of v2, /device:TPU:1, one launch (start us, length us, event | category | flops | bytes accessed | tf_op | source)
XLA Modules:
  0.0 219.1 jit_solution(71046589299189213)
XLA Ops:
  6.5 1.1 copy-done
  7.6 0.8 constant_dynamic-slice_fusion
  8.4 0.0 all-gather.3.cloned.1.call-update
  8.5 2.7 %constant_dynamic-slice_fusion.1 = (bf16[8,64,512]{2,1,0:T(8,128)(2,1)S(1)}, bf16[8,64,512]{2,1,0:T(8,128)(2,1)}, bf16[8,64,512]{2,1,0:T(8,128)(2,1)}, bf16[8,64,512]{2,1,0:T(8,128)(2,1)}) fusion(bf16[32,64,512]{2,1,0:T(8,128)(2,1)} %feats.1, s32[]{:T(128)S(6)} %select_n.46, s32[]{:T(128)S(6)} %select_n.42, s32[]{:T(128)S(6)} %select_n.40, s32[]{:T(128)S(6)} %select_n.44), kind=kLoop, calls=%fused_computation.3 | loop fusion | bytes 4194320 | tf_op jit(solution)/shard_map/dynamic_slice | solution.py:783
  11.2 3.7 %collective-permute-start.1 = (bf16[8,64,512]{2,1,0:T(8,128)(2,1)}, bf16[8,64,512]{2,1,0:T(8,128)(2,1)S(1)}, u32[]{:S(2)}, u32[]{:S(2)}) collective-permute-start(bf16[8,64,512]{2,1,0:T(8,128)(2,1)} %get-tuple-element.72), channel_id=1, source_target_pairs={{0,2},{1,3},{2,0},{3,1},{4,6},{5,7},{6,4},{7,5},{8,10},{9,11},{10,... | collective-permute-start | bytes 1572872 | tf_op jit(solution)/shard_map/ppermute | solution.py:722
  15.0 0.4 collective-permute-start
  15.4 2.3 %collective-permute-start.2 = (bf16[8,64,512]{2,1,0:T(8,128)(2,1)}, bf16[8,64,512]{2,1,0:T(8,128)(2,1)}, u32[]{:S(2)}, u32[]{:S(2)}) collective-permute-start(bf16[8,64,512]{2,1,0:T(8,128)(2,1)} %get-tuple-element.74), channel_id=1, source_target_pairs={{0,3},{1,0},{2,1},{3,2},{4,7},{5,4},{6,5},{7,6},{8,11},{9,8},{10,9... | collective-permute-start | bytes 1572872 | tf_op jit(solution)/shard_map/ppermute | solution.py:722
  17.6 8.0 %extract.1 = (bf16[192,32,128]{2,1,0:T(8,128)(2,1)}, bf16[32,144,128]{2,1,0:T(8,128)(2,1)}) custom-call(s32[2,32]{1,0:T(2,128)} %bitcast.23, s32[2,32]{1,0:T(2,128)} %bitcast.21, bf16[32,64,512]{2,1,0:T(8,128)(2,1)} %feats.1, bf16[448,512]{1,0:T(8,128)(2,1)} %constant.57.clone.table), custom_call_target="tpu_custom_call" | custom-call | flops 1000000000 | bytes 3000000 | tf_op jit(solution)/shard_map/extract/pallas_call | solution.py:763
  25.7 0.0 copy-start.5
  25.7 0.0 copy-start.6
  25.7 0.0 copy-start.7
  25.7 0.0 copy-start.8
  25.7 9.6 %all-to-all-start = ((bf16[32,144,128]{2,1,0:T(8,128)(2,1)}), bf16[32,144,128]{2,1,0:T(8,128)(2,1)S(1)}, u32[]{:S(2)}, u32[]{:S(2)}) async-start(bf16[32,144,128]{2,1,0:T(8,128)(2,1)} %get-tuple-element.41), calls=%async_computation | async-start | bytes 2359296 | tf_op jit(solution)/shard_map/all_to_all | solution.py:728
  35.4 0.0 copy-start.12
  35.4 0.0 copy-start.13
  35.4 0.0 copy-start.14
  35.4 2.7 %plan.1 = (s32[192]{0:T(256)S(1)}, s32[64]{0:T(128)S(1)}, s32[32]{0:T(128)S(1)}) custom-call(s32[6,32]{1,0:T(8,128)S(1)} %bitcast.20, s32[2,32]{1,0:T(2,128)S(1)} %bitcast.24, s32[2,32]{1,0:T(2,128)S(1)} %bitcast.22, s32[2,32]{1,0:T(2,128)S(1)} %bitcast.26), custom_call_target="tpu_custom_call" | custom-call | flops 20000000000 | bytes 60000000 | tf_op jit(solution)/shard_map/plan/pallas_call | solution.py:787
  38.1 0.1 pad_add_fusion.me
  38.2 0.1 select_maximum_fusion.par
  38.3 11.6 %collective-permute-done.x1.v1 = bf16[8,64,512]{2,1,0:T(8,128)(2,1)S(1)} collective-permute-done((bf16[8,64,512]{2,1,0:T(8,128)(2,1)}, bf16[8,64,512]{2,1,0:T(8,128)(2,1)S(1)}, u32[]{:S(2)}, u32[]{:S(2)}) %collective-permute-start) | collective-permute-done | bytes 524320 | tf_op jit(solution)/shard_map/ppermute | solution.py:722
  49.9 3.1 %all-to-all-done.recv = bf16[32,144,128]{2,1,0:T(8,128)(2,1)S(1)} async-done(((bf16[32,144,128]{2,1,0:T(8,128)(2,1)}), bf16[32,144,128]{2,1,0:T(8,128)(2,1)S(1)}, u32[]{:S(2)}, u32[]{:S(2)}) %all-to-all-start) | async-done | bytes 1179680 | tf_op jit(solution)/shard_map/all_to_all | solution.py:728
  53.0 2.3 %octant1.1 = (bf16[17,32,128]{2,1,0:T(8,128)(2,1)S(1)}, bf16[17,32,128]{2,1,0:T(8,128)(2,1)S(1)}, bf16[17,32,128]{2,1,0:T(8,128)(2,1)S(1)}, bf16[17,32,128]{2,1,0:T(8,128)(2,1)S(1)}, f32[8,128]{1,0:T(8,128)S(1)}) custom-call(s32[64]{0:T(128)S(1)} %get-tuple-element.40.tsel, s32[2]{0:T(128)S(1)} %pad_add_fusion.me, ...), custom_call_target="tpu_custom_call" | custom-call | flops 1000000000 | bytes 3000000 | tf_op jit(solution)/shard_map/octant1/pallas_call | solution.py:801
  55.4 0.6 copy-done.2
  56.0 0.7 copy-done.3
  56.7 0.6 copy-done.4
  57.3 0.6 copy-done.10
  58.0 1.6 collective-permute-start.6
  59.5 0.0 collective-permute-start.3
  59.5 0.9 collective-permute-start.4
  60.4 1.8 collective-permute-start.5
  62.2 1.4 copy-done.9
  63.6 3.0 %border1.1 = (bf16[48,32,128]{2,1,0:T(8,128)(2,1)S(1)}, bf16[48,32,128]{2,1,0:T(8,128)(2,1)S(1)}, bf16[48,32,128]{2,1,0:T(8,128)(2,1)S(1)}, bf16[48,32,128]{2,1,0:T(8,128)(2,1)S(1)}) custom-call(s32[192]{0:T(256)S(1)} %get-tuple-element.38.sel, s32[2]{0:T(128)S(1)} %pad_add_fusion.me, f32[8,128]{1,0:T(8,128)S(1)} %get-tuple-element.46.own, ...), custom_call_target="tpu_custom_call" | custom-call | flops 1000000000 | bytes 3000000 | tf_op jit(solution)/shard_map/border1/pallas_call | solution.py:817
  66.6 0.6 collective-permute-start.7
  67.2 2.0 collective-permute-done.3.t1.u1
  69.2 1.9 collective-permute-start.9
  71.1 0.0 collective-permute-done.5.t3.u3
  71.1 0.0 collective-permute-done.6.wb
  71.1 7.5 %inner1.1 = (f32[8,512,256]{2,1,0:T(8,128)S(1)}, f32[8,256]{1,0:T(8,128)S(1)}) custom-call(s32[2]{0:T(128)S(1)} %pad_add_fusion.me, bf16[17,32,128]{2,1,0:T(8,128)(2,1)S(1)} %copy-done.11, bf16[17,32,128]{2,1,0:T(8,128)(2,1)S(1)} %collective-permute-done.3.t1.u1, bf16[17,32,128]{2,1,0:T(8,128)(2,1)S(1)} %collective-permute-done.4.t2.u2, ...), custom_call_target="tpu_custom_call" | custom-call | flops 8000000000 | bytes 24000000 | tf_op jit(solution)/shard_map/inner1/pallas_call | solution.py:836
  78.7 4.3 %tiles.1 = bf16[4,16,32,128]{3,2,1,0:T(8,128)(2,1)S(1)} custom-call(s32[2]{0:T(128)S(1)} %pad_add_fusion.me, bf16[17,32,128]{2,1,0:T(8,128)(2,1)S(1)} %copy-done.11, bf16[17,32,128]{2,1,0:T(8,128)(2,1)S(1)} %collective-permute-done.3.t1.u1, bf16[17,32,128]{2,1,0:T(8,128)(2,1)S(1)} %collective-permute-done.4.t2.u2, ...), custom_call_target="tpu_custom_call" | custom-call | flops 4000000000 | bytes 12000000 | tf_op jit(solution)/shard_map/tiles/pallas_call | solution.py:853
  83.0 3.1 %collective-permute-done.8.u2 = bf16[48,32,128]{2,1,0:T(8,128)(2,1)S(1)} collective-permute-done((bf16[48,32,128]{2,1,0:T(8,128)(2,1)S(1)}, bf16[48,32,128]{2,1,0:T(8,128)(2,1)S(1)}, u32[]{:S(2)}, u32[]{:S(2)}) %collective-permute-start.8) | collective-permute-done | bytes 393248 | tf_op jit(solution)/shard_map/ppermute | solution.py:722
  86.2 0.8 collective-permute-done.9.u3
  86.9 5.3 %outer1.1 = (f32[8,512,256]{2,1,0:T(8,128)S(1)}, bf16[65,32,128]{2,1,0:T(8,128)(2,1)S(1)}, bf16[65,32,128]{2,1,0:T(8,128)(2,1)S(1)}, bf16[65,32,128]{2,1,0:T(8,128)(2,1)S(1)}, bf16[65,32,128]{2,1,0:T(8,128)(2,1)S(1)}) custom-call(s32[2]{0:T(128)S(1)} %pad_add_fusion.me, f32[8,256]{1,0:T(8,128)S(1)} %get-tuple-element.48.rows, ...), custom_call_target="tpu_custom_call" | custom-call | flops 5000000000 | bytes 15000000 | tf_op jit(solution)/shard_map/outer1/pallas_call | solution.py:870
  92.2 2.8 %collective-permute-start.10 = (bf16[65,32,128]{2,1,0:T(8,128)(2,1)S(1)}, bf16[65,32,128]{2,1,0:T(8,128)(2,1)S(1)}, u32[]{:S(2)}, u32[]{:S(2)}) collective-permute-start(bf16[65,32,128]{2,1,0:T(8,128)(2,1)S(1)} %get-tuple-element.56), channel_id=1, source_target_pairs={{0,1},{1,2},{2,3},{3,0},{4,5},{5,6},{6,7},{7,4},{8,9},{9,10},{10,1... | collective-permute-start | bytes 1597448 | tf_op jit(solution)/shard_map/ppermute | solution.py:722
  95.1 1.8 collective-permute-start.11
  96.9 0.7 collective-permute-start.12
  97.5 9.5 %collective-permute-done.10.v1 = bf16[65,32,128]{2,1,0:T(8,128)(2,1)S(1)} collective-permute-done((bf16[65,32,128]{2,1,0:T(8,128)(2,1)S(1)}, bf16[65,32,128]{2,1,0:T(8,128)(2,1)S(1)}, u32[]{:S(2)}, u32[]{:S(2)}) %collective-permute-start.10) | collective-permute-done | bytes 532512 | tf_op jit(solution)/shard_map/ppermute | solution.py:722
  107.0 13.0 %collective-permute-done.11.v2 = bf16[65,32,128]{2,1,0:T(8,128)(2,1)S(1)} collective-permute-done((bf16[65,32,128]{2,1,0:T(8,128)(2,1)S(1)}, bf16[65,32,128]{2,1,0:T(8,128)(2,1)S(1)}, u32[]{:S(2)}, u32[]{:S(2)}) %collective-permute-start.11) | collective-permute-done | bytes 532512 | tf_op jit(solution)/shard_map/ppermute | solution.py:722
  120.0 0.0 collective-permute-done.12.v3
  120.0 1.8 route2.1
  121.8 25.3 %all_to_all.10.recv = bf16[32,144,128]{2,1,0:T(8,128)(2,1)S(1)} all-to-all(bf16[32,144,128]{2,1,0:T(8,128)(2,1)S(1)} %get-tuple-element.60), channel_id=1, replica_groups=mesh['blocks'=32,'chan'=4] {'blocks'}, dimensions={0} | all-to-all | bytes 2359296 | tf_op jit(solution)/shard_map/all_to_all | solution.py:728
  147.1 4.8 %border2.1 = (bf16[56,32,128]{2,1,0:T(8,128)(2,1)S(1)}, bf16[56,32,128]{2,1,0:T(8,128)(2,1)S(1)}, bf16[56,32,128]{2,1,0:T(8,128)(2,1)S(1)}, bf16[56,32,128]{2,1,0:T(8,128)(2,1)S(1)}, f32[8,256]{1,0:T(8,128)S(1)}) custom-call(s32[192]{0:T(256)S(1)} %get-tuple-element.38.sel, s32[32]{0:T(128)S(1)} %get-tuple-element.39.ssel, s32[2]{0:T(128)S(1)} %pad_add_fusion.me, ...), custom_call_target="tpu_custom_call" | custom-call | flops 1000000000 | bytes 3000000 | tf_op jit(solution)/shard_map/border2/pallas_call | solution.py:910
  152.0 0.7 collective-permute-start.13
  152.6 2.5 %collective-permute-start.14 = (bf16[56,32,128]{2,1,0:T(8,128)(2,1)S(1)}, bf16[56,32,128]{2,1,0:T(8,128)(2,1)S(1)}, u32[]{:S(2)}, u32[]{:S(2)}) collective-permute-start(bf16[56,32,128]{2,1,0:T(8,128)(2,1)S(1)} %get-tuple-element.65), channel_id=1, source_target_pairs={{0,2},{1,3},{2,0},{3,1},{4,6},{5,7},{6,4},{7,5},{8,10},{9,11},{10,... | collective-permute-start | bytes 1376264 | tf_op jit(solution)/shard_map/ppermute | solution.py:722
  155.1 0.2 collective-permute-start.15
  155.4 6.7 %inner2.1.part = f32[8,512,256]{2,1,0:T(8,128)S(1)} custom-call(s32[2]{0:T(128)S(1)} %pad_add_fusion.me, f32[8,256]{1,0:T(8,128)S(1)} %get-tuple-element.61.rows, f32[8,512,256]{2,1,0:T(8,128)S(1)} %get-tuple-element.62.hid, bf16[4,3,7,32,256]{4,3,2,1,0:T(8,128)(2,1)S(1)} %bitcast.18, bf16[4,3,7,32,256]{4,3,2,1,0:T(8,128)(2,1)S(1)} %collective-permute-done.6.wb), custom_call_target="tpu_custom_call" | custom-call | flops 8000000000 | bytes 24000000 | tf_op jit(solution)/shard_map/inner2/pallas_call | solution.py:926
  162.1 2.9 %collective-permute-done.13.u1 = bf16[56,32,128]{2,1,0:T(8,128)(2,1)S(1)} collective-permute-done((bf16[56,32,128]{2,1,0:T(8,128)(2,1)S(1)}, bf16[56,32,128]{2,1,0:T(8,128)(2,1)S(1)}, u32[]{:S(2)}, u32[]{:S(2)}) %collective-permute-start.13) | collective-permute-done | bytes 458784 | tf_op jit(solution)/shard_map/ppermute | solution.py:722
  165.0 10.2 %collective-permute-done.14.u2 = bf16[56,32,128]{2,1,0:T(8,128)(2,1)S(1)} collective-permute-done((bf16[56,32,128]{2,1,0:T(8,128)(2,1)S(1)}, bf16[56,32,128]{2,1,0:T(8,128)(2,1)S(1)}, u32[]{:S(2)}, u32[]{:S(2)}) %collective-permute-start.14) | collective-permute-done | bytes 458784 | tf_op jit(solution)/shard_map/ppermute | solution.py:722
  175.2 7.8 %outer2.1 = (bf16[8,64,512]{2,1,0:T(8,128)(2,1)S(1)}, bf16[8,64,512]{2,1,0:T(8,128)(2,1)S(1)}, bf16[8,64,512]{2,1,0:T(8,128)(2,1)S(1)}, bf16[8,64,512]{2,1,0:T(8,128)(2,1)S(1)}) custom-call(s32[2]{0:T(128)S(1)} %pad_add_fusion.me, f32[8,512,256]{2,1,0:T(8,128)S(1)} %inner2.1.part, bf16[8,64,512]{2,1,0:T(8,128)(2,1)S(1)} %get-tuple-element.71.v0, ...), custom_call_target="tpu_custom_call" | custom-call | flops 5000000000 | bytes 15000000 | tf_op jit(solution)/shard_map/outer2/pallas_call | solution.py:942
  183.0 1.6 collective-permute-start.16
  184.6 3.0 %collective-permute-start.17 = (bf16[8,64,512]{2,1,0:T(8,128)(2,1)S(1)}, bf16[8,64,512]{2,1,0:T(8,128)(2,1)S(1)}, u32[]{:S(2)}, u32[]{:S(2)}) collective-permute-start(bf16[8,64,512]{2,1,0:T(8,128)(2,1)S(1)} %get-tuple-element.69), channel_id=1, source_target_pairs={{0,2},{1,3},{2,0},{3,1},{4,6},{5,7},{6,4},{7,5},{8,10},{9,11},{10,... | collective-permute-start | bytes 1572872 | tf_op jit(solution)/shard_map/ppermute | solution.py:722
  187.6 0.0 collective-permute-start.18
  187.6 10.0 %collective-permute-done.16.p1 = bf16[8,64,512]{2,1,0:T(8,128)(2,1)S(1)} collective-permute-done((bf16[8,64,512]{2,1,0:T(8,128)(2,1)S(1)}, bf16[8,64,512]{2,1,0:T(8,128)(2,1)S(1)}, u32[]{:S(2)}, u32[]{:S(2)}) %collective-permute-start.16) | collective-permute-done | bytes 524320 | tf_op jit(solution)/shard_map/ppermute | solution.py:722
  197.6 12.8 %collective-permute-done.17.p2 = bf16[8,64,512]{2,1,0:T(8,128)(2,1)S(1)} collective-permute-done((bf16[8,64,512]{2,1,0:T(8,128)(2,1)S(1)}, bf16[8,64,512]{2,1,0:T(8,128)(2,1)S(1)}, u32[]{:S(2)}, u32[]{:S(2)}) %collective-permute-start.17) | collective-permute-done | bytes 524320 | tf_op jit(solution)/shard_map/ppermute | solution.py:722
  210.4 1.9 gather.1
  (28 shorter events, 0.1 us)
Async XLA Ops:
  6.5 1.1 copy-start
  6.5 51.4 %all-gather.3.cloned.1.call-start = ((), (), s32[]{:S(2)}) async-start(), calls=%async_computation.2 | async-start | bytes 1720320 | tf_op jit(solution)/shard_map/all_gather | solution.py:761
  11.2 27.1 %collective-permute-start.1 = (bf16[8,64,512]{2,1,0:T(8,128)(2,1)}, bf16[8,64,512]{2,1,0:T(8,128)(2,1)S(1)}, u32[]{:S(2)}, u32[]{:S(2)}) collective-permute-start(bf16[8,64,512]{2,1,0:T(8,128)(2,1)} %get-tuple-element.72), channel_id=1, source_target_pairs={{0,2},{1,3},{2,0},{3,1},{4,6},{5,7},{6,4},{7,5},{8,10},{9,11},{10,... | collective-permute-start | bytes 1572872 | tf_op jit(solution)/shard_map/ppermute | solution.py:722
  15.0 35.0 %collective-permute-start = (bf16[8,64,512]{2,1,0:T(8,128)(2,1)}, bf16[8,64,512]{2,1,0:T(8,128)(2,1)S(1)}, u32[]{:S(2)}, u32[]{:S(2)}) collective-permute-start(bf16[8,64,512]{2,1,0:T(8,128)(2,1)} %get-tuple-element.73), channel_id=1, source_target_pairs={{0,1},{1,2},{2,3},{3,0},{4,5},{5,6},{6,7},{7,4},{8,9},{9,10},{10,1... | collective-permute-start | bytes 1572872 | tf_op jit(solution)/shard_map/ppermute | solution.py:722
  15.4 34.6 %collective-permute-start.2 = (bf16[8,64,512]{2,1,0:T(8,128)(2,1)}, bf16[8,64,512]{2,1,0:T(8,128)(2,1)}, u32[]{:S(2)}, u32[]{:S(2)}) collective-permute-start(bf16[8,64,512]{2,1,0:T(8,128)(2,1)} %get-tuple-element.74), channel_id=1, source_target_pairs={{0,3},{1,0},{2,1},{3,2},{4,7},{5,4},{6,5},{7,6},{8,11},{9,8},{10,9... | collective-permute-start | bytes 1572872 | tf_op jit(solution)/shard_map/ppermute | solution.py:722
  25.7 9.6 %copy-start.5 = (s32[32,6]{0,1:T(8,128)S(1)}, s32[32,6]{0,1:T(8,128)}, u32[]{:S(2)}) copy-start(s32[32,6]{0,1:T(8,128)} %param.15) | copy-start | bytes 2308
  25.7 9.6 %copy-start.6 = (s32[1,32,2]{1,2,0:T(2,128)S(1)}, s32[1,32,2]{1,2,0:T(2,128)}, u32[]{:S(2)}) copy-start(s32[1,32,2]{1,2,0:T(2,128)} %param.17) | copy-start | bytes 772
  25.7 9.6 %copy-start.7 = (s32[1,32,2]{1,2,0:T(2,128)S(1)}, s32[1,32,2]{1,2,0:T(2,128)}, u32[]{:S(2)}) copy-start(s32[1,32,2]{1,2,0:T(2,128)} %param.16) | copy-start | bytes 772
  25.7 9.6 %copy-start.8 = (s32[1,32,2]{1,2,0:T(2,128)S(1)}, s32[1,32,2]{1,2,0:T(2,128)}, u32[]{:S(2)}) copy-start(s32[1,32,2]{1,2,0:T(2,128)} %param.18) | copy-start | bytes 772
  25.7 27.3 %all-to-all-start = ((bf16[32,144,128]{2,1,0:T(8,128)(2,1)}), bf16[32,144,128]{2,1,0:T(8,128)(2,1)S(1)}, u32[]{:S(2)}, u32[]{:S(2)}) async-start(bf16[32,144,128]{2,1,0:T(8,128)(2,1)} %get-tuple-element.41), calls=%async_computation | async-start | bytes 2359296 | tf_op jit(solution)/shard_map/all_to_all | solution.py:728
  35.4 2.7 %copy-start.12 = (f32[3,64]{1,0:T(4,128)S(1)}, f32[3,64]{1,0:T(4,128)}, u32[]{:S(2)}) copy-start(f32[3,64]{1,0:T(4,128)} %param.13) | copy-start | bytes 2308
  35.4 2.7 %copy-start.13 = (f32[3,64]{1,0:T(4,128)S(1)}, f32[3,64]{1,0:T(4,128)}, u32[]{:S(2)}) copy-start(f32[3,64]{1,0:T(4,128)} %param.12) | copy-start | bytes 2308
  35.4 2.7 %copy-start.14 = (f32[64]{0:T(128)S(1)}, f32[64]{0:T(128)}, u32[]{:S(2)}) copy-start(f32[64]{0:T(128)} %param.14) | copy-start | bytes 772
  55.3 0.7 copy-start.2
  56.0 0.7 copy-start.3
  56.7 0.6 copy-start.4
  57.3 0.6 copy-start.10
  58.0 13.2 %copy-start.1 = (bf16[12,7,32,256]{3,2,1,0:T(8,128)(2,1)S(1)}, bf16[12,7,32,256]{3,2,1,0:T(8,128)(2,1)}, u32[]{:S(2)}) copy-start(bf16[12,7,32,256]{3,2,1,0:T(8,128)(2,1)} %all-gather.3.cloned.1.call-done) | copy-start | bytes 4128772
  58.0 13.2 %collective-permute-start.6 = (bf16[4,3,7,32,256]{4,3,2,1,0:T(8,128)(2,1)}, bf16[4,3,7,32,256]{4,3,2,1,0:T(8,128)(2,1)S(1)}, u32[]{:S(2)}, u32[]{:S(2)}) collective-permute-start(bf16[4,3,7,32,256]{4,3,2,1,0:T(8,128)(2,1)} %bitcast.14), channel_id=1, source_target_pairs={{0,4},{4,0},{8,12},{12,8},{16,20},{20,16},{24,28},{28,24},{32,36},... | collective-permute-start | bytes 4128776 | tf_op jit(solution)/shard_map/ppermute | solution.py:816
  59.5 9.7 %collective-permute-start.3 = (bf16[17,32,128]{2,1,0:T(8,128)(2,1)}, bf16[17,32,128]{2,1,0:T(8,128)(2,1)S(1)}, u32[]{:S(2)}, u32[]{:S(2)}) collective-permute-start(bf16[17,32,128]{2,1,0:T(8,128)(2,1)} %copy-done.4), channel_id=1, source_target_pairs={{3,0},{2,3},{1,2},{0,1},{7,4},{6,7},{5,6},{4,5},{11,8},{10,11},{9,... | collective-permute-start | bytes 417800 | tf_op jit(solution)/shard_map/ppermute | solution.py:722
  59.5 9.7 %collective-permute-start.4 = (bf16[17,32,128]{2,1,0:T(8,128)(2,1)}, bf16[17,32,128]{2,1,0:T(8,128)(2,1)S(1)}, u32[]{:S(2)}, u32[]{:S(2)}) collective-permute-start(bf16[17,32,128]{2,1,0:T(8,128)(2,1)} %copy-done.3), channel_id=1, source_target_pairs={{3,1},{2,0},{1,3},{0,2},{7,5},{6,4},{5,7},{4,6},{11,9},{10,8},{9,1... | collective-permute-start | bytes 417800 | tf_op jit(solution)/shard_map/ppermute | solution.py:722
  60.4 10.7 %collective-permute-start.5 = (bf16[17,32,128]{2,1,0:T(8,128)(2,1)}, bf16[17,32,128]{2,1,0:T(8,128)(2,1)S(1)}, u32[]{:S(2)}, u32[]{:S(2)}) collective-permute-start(bf16[17,32,128]{2,1,0:T(8,128)(2,1)} %copy-done.2), channel_id=1, source_target_pairs={{3,2},{2,1},{1,0},{0,3},{7,6},{6,5},{5,4},{4,7},{11,10},{10,9},{9,... | collective-permute-start | bytes 417800 | tf_op jit(solution)/shard_map/ppermute | solution.py:722
  62.2 1.4 copy-start.9
  63.6 7.5 %copy-start.11 = (bf16[17,32,128]{2,1,0:T(8,128)(2,1)S(1)}, bf16[17,32,128]{2,1,0:T(8,128)(2,1)}, u32[]{:S(2)}) copy-start(bf16[17,32,128]{2,1,0:T(8,128)(2,1)} %copy-done.10) | copy-start | bytes 417796
  66.6 16.4 %collective-permute-start.7 = (bf16[48,32,128]{2,1,0:T(8,128)(2,1)S(1)}, bf16[48,32,128]{2,1,0:T(8,128)(2,1)S(1)}, u32[]{:S(2)}, u32[]{:S(2)}) collective-permute-start(bf16[48,32,128]{2,1,0:T(8,128)(2,1)S(1)} %get-tuple-element.52), channel_id=1, source_target_pairs={{0,1},{1,2},{2,3},{3,0},{4,5},{5,6},{6,7},{7,4},{8,9},{9,10},{10,1... | collective-permute-start | bytes 1179656 | tf_op jit(solution)/shard_map/ppermute | solution.py:722
  69.2 16.9 %collective-permute-start.8 = (bf16[48,32,128]{2,1,0:T(8,128)(2,1)S(1)}, bf16[48,32,128]{2,1,0:T(8,128)(2,1)S(1)}, u32[]{:S(2)}, u32[]{:S(2)}) collective-permute-start(bf16[48,32,128]{2,1,0:T(8,128)(2,1)S(1)} %get-tuple-element.53), channel_id=1, source_target_pairs={{0,2},{1,3},{2,0},{3,1},{4,6},{5,7},{6,4},{7,5},{8,10},{9,11},{10,... | collective-permute-start | bytes 1179656 | tf_op jit(solution)/shard_map/ppermute | solution.py:722
  69.2 17.7 %collective-permute-start.9 = (bf16[48,32,128]{2,1,0:T(8,128)(2,1)S(1)}, bf16[48,32,128]{2,1,0:T(8,128)(2,1)S(1)}, u32[]{:S(2)}, u32[]{:S(2)}) collective-permute-start(bf16[48,32,128]{2,1,0:T(8,128)(2,1)S(1)} %get-tuple-element.54), channel_id=1, source_target_pairs={{0,3},{1,0},{2,1},{3,2},{4,7},{5,4},{6,5},{7,6},{8,11},{9,8},{10,9... | collective-permute-start | bytes 1179656 | tf_op jit(solution)/shard_map/ppermute | solution.py:722
  92.2 14.8 %collective-permute-start.10 = (bf16[65,32,128]{2,1,0:T(8,128)(2,1)S(1)}, bf16[65,32,128]{2,1,0:T(8,128)(2,1)S(1)}, u32[]{:S(2)}, u32[]{:S(2)}) collective-permute-start(bf16[65,32,128]{2,1,0:T(8,128)(2,1)S(1)} %get-tuple-element.56), channel_id=1, source_target_pairs={{0,1},{1,2},{2,3},{3,0},{4,5},{5,6},{6,7},{7,4},{8,9},{9,10},{10,1... | collective-permute-start | bytes 1597448 | tf_op jit(solution)/shard_map/ppermute | solution.py:722
  95.1 24.9 %collective-permute-start.11 = (bf16[65,32,128]{2,1,0:T(8,128)(2,1)S(1)}, bf16[65,32,128]{2,1,0:T(8,128)(2,1)S(1)}, u32[]{:S(2)}, u32[]{:S(2)}) collective-permute-start(bf16[65,32,128]{2,1,0:T(8,128)(2,1)S(1)} %get-tuple-element.57), channel_id=1, source_target_pairs={{0,2},{1,3},{2,0},{3,1},{4,6},{5,7},{6,4},{7,5},{8,10},{9,11},{10,... | collective-permute-start | bytes 1597448 | tf_op jit(solution)/shard_map/ppermute | solution.py:722
  96.9 23.1 %collective-permute-start.12 = (bf16[65,32,128]{2,1,0:T(8,128)(2,1)S(1)}, bf16[65,32,128]{2,1,0:T(8,128)(2,1)S(1)}, u32[]{:S(2)}, u32[]{:S(2)}) collective-permute-start(bf16[65,32,128]{2,1,0:T(8,128)(2,1)S(1)} %get-tuple-element.58), channel_id=1, source_target_pairs={{0,3},{1,0},{2,1},{3,2},{4,7},{5,4},{6,5},{7,6},{8,11},{9,8},{10,9... | collective-permute-start | bytes 1597448 | tf_op jit(solution)/shard_map/ppermute | solution.py:722
  152.0 13.0 %collective-permute-start.13 = (bf16[56,32,128]{2,1,0:T(8,128)(2,1)S(1)}, bf16[56,32,128]{2,1,0:T(8,128)(2,1)S(1)}, u32[]{:S(2)}, u32[]{:S(2)}) collective-permute-start(bf16[56,32,128]{2,1,0:T(8,128)(2,1)S(1)} %get-tuple-element.64), channel_id=1, source_target_pairs={{0,1},{1,2},{2,3},{3,0},{4,5},{5,6},{6,7},{7,4},{8,9},{9,10},{10,1... | collective-permute-start | bytes 1376264 | tf_op jit(solution)/shard_map/ppermute | solution.py:722
  152.6 22.5 %collective-permute-start.14 = (bf16[56,32,128]{2,1,0:T(8,128)(2,1)S(1)}, bf16[56,32,128]{2,1,0:T(8,128)(2,1)S(1)}, u32[]{:S(2)}, u32[]{:S(2)}) collective-permute-start(bf16[56,32,128]{2,1,0:T(8,128)(2,1)S(1)} %get-tuple-element.65), channel_id=1, source_target_pairs={{0,2},{1,3},{2,0},{3,1},{4,6},{5,7},{6,4},{7,5},{8,10},{9,11},{10,... | collective-permute-start | bytes 1376264 | tf_op jit(solution)/shard_map/ppermute | solution.py:722
  155.1 20.1 %collective-permute-start.15 = (bf16[56,32,128]{2,1,0:T(8,128)(2,1)S(1)}, bf16[56,32,128]{2,1,0:T(8,128)(2,1)S(1)}, u32[]{:S(2)}, u32[]{:S(2)}) collective-permute-start(bf16[56,32,128]{2,1,0:T(8,128)(2,1)S(1)} %get-tuple-element.66), channel_id=1, source_target_pairs={{0,3},{1,0},{2,1},{3,2},{4,7},{5,4},{6,5},{7,6},{8,11},{9,8},{10,9... | collective-permute-start | bytes 1376264 | tf_op jit(solution)/shard_map/ppermute | solution.py:722
  183.0 14.5 %collective-permute-start.16 = (bf16[8,64,512]{2,1,0:T(8,128)(2,1)S(1)}, bf16[8,64,512]{2,1,0:T(8,128)(2,1)S(1)}, u32[]{:S(2)}, u32[]{:S(2)}) collective-permute-start(bf16[8,64,512]{2,1,0:T(8,128)(2,1)S(1)} %get-tuple-element.68), channel_id=1, source_target_pairs={{0,1},{1,2},{2,3},{3,0},{4,5},{5,6},{6,7},{7,4},{8,9},{9,10},{10,1... | collective-permute-start | bytes 1572872 | tf_op jit(solution)/shard_map/ppermute | solution.py:722
  184.6 25.7 %collective-permute-start.17 = (bf16[8,64,512]{2,1,0:T(8,128)(2,1)S(1)}, bf16[8,64,512]{2,1,0:T(8,128)(2,1)S(1)}, u32[]{:S(2)}, u32[]{:S(2)}) collective-permute-start(bf16[8,64,512]{2,1,0:T(8,128)(2,1)S(1)} %get-tuple-element.69), channel_id=1, source_target_pairs={{0,2},{1,3},{2,0},{3,1},{4,6},{5,7},{6,4},{7,5},{8,10},{9,11},{10,... | collective-permute-start | bytes 1572872 | tf_op jit(solution)/shard_map/ppermute | solution.py:722
  187.6 22.8 %collective-permute-start.18 = (bf16[8,64,512]{2,1,0:T(8,128)(2,1)S(1)}, bf16[8,64,512]{2,1,0:T(8,128)(2,1)S(1)}, u32[]{:S(2)}, u32[]{:S(2)}) collective-permute-start(bf16[8,64,512]{2,1,0:T(8,128)(2,1)S(1)} %get-tuple-element.70), channel_id=1, source_target_pairs={{0,3},{1,0},{2,1},{3,2},{4,7},{5,4},{6,5},{7,6},{8,11},{9,8},{10,9... | collective-permute-start | bytes 1572872 | tf_op jit(solution)/shard_map/ppermute | solution.py:722
Sparse Core Ops, SparseCore 0:
  9.0 41.1 all-gather.2

commit v3 on v2

--- a/solution.py
+++ b/solution.py
@@ -14,10 +14,12 @@
 SLOTS = 32
 DEVS = 32
 QUART = 8
+HALF = 4
 TILES = 2
 FACES = 6 * SLOTS
 CODES = 64
 EPS = 1e-05
+ORDER = (0, 2, 1, 3)
 F32 = jnp.float32
 BF16 = jnp.bfloat16
 HIGH = lax.Precision.HIGHEST
@@ -128,78 +130,91 @@
     )
 
 
-def extract_kernel(links, csend, feats, table, faces, out, held, pooled, acc, stat, send_buf, sem):
-    step = pl.program_id(0)
+def extract_kernel(
+    links, csend, feats, table, faces, out,
+    slots, codes, held, pooled, stat, send_buf, sem, load,
+):
     left = lanes(32) < 64
 
-    @pl.when(step == 0)
-    def _():
-        acc[...] = jnp.zeros((192, 128), F32)
-
-    rows = []
-    s = jnp.zeros((64, 128), F32)
-    q = jnp.zeros((64, 128), F32)
-    ps = jnp.zeros((32, 128), F32)
-    pq = jnp.zeros((32, 128), F32)
-    for k in range(4):
-        x = feats[k]
-        rows += [x, x]
+    def fetch(n):
+        here = pl.ds(4 * n, 4)
+        return pltpu.make_async_copy(feats.at[here], slots.at[here], load.at[n])
+
+    def keep(n):
+        here = pl.ds(12 * n, 12)
+        return pltpu.make_async_copy(held.at[here], faces.at[here], sem.at[n])
+
+    get_codes = pltpu.make_async_copy(table, codes, load.at[8])
+    fetch(0).start()
+    get_codes.start()
+    for n in range(1, 8):
+        fetch(n).start()
+    get_codes.wait()
+
+    def step(n, carry):
+        s, q, ps, pq = carry
+        fetch(n).wait()
+        x = slots[pl.ds(4 * n, 4)]
+        layers = lax.dot_general(
+            codes[...], x.reshape(256, VOX), NT, preferred_element_type=F32
+        )
         wide = x.astype(F32)
-        for v in range(4):
-            piece = wide[:, 128 * v : 128 * v + 128]
-            s = s + piece
-            q = q + piece * piece
-    layers = lax.dot_general(
-        table[...], jnp.concatenate(rows, axis=0), NT, preferred_element_type=F32
-    )
-    for k in range(4):
-        for f in range(7):
-            low = layers[64 * f : 64 * f + 32, 128 * k : 128 * k + 128]
-            high = layers[64 * f + 32 : 64 * f + 64, 128 * k : 128 * k + 128]
-            unit = jnp.where(left, low, high).astype(BF16)
-            if f < 6:
-                held[(4 * step + k) * 6 + f] = unit
-            else:
-                pooled[4 * step + k] = unit
-                wide = unit.astype(F32)
-                ps = ps + wide
-                pq = pq + wide * wide
-    acc[0:64, :] += s
-    acc[64:128, :] += q
-    acc[128:160, :] += ps
-    acc[160:192, :] += pq
-
-    @pl.when(step == pl.num_programs(0) - 1)
-    def _():
-        keep = pltpu.make_async_copy(held, faces, sem.at[0])
-        keep.start()
-        ones = jnp.ones((8, 128), F32)
-
-        def by_lane(sums):
-            twice = jnp.concatenate([sums, sums], axis=0)
-            return lax.dot_general(ones, twice, NT, precision=HIGH, preferred_element_type=F32)[0:1]
-
-        stat[...] = jnp.zeros((16, 128), F32)
-        put_terms(stat, 0, by_lane(acc[0:64, :]))
-        put_terms(stat, 3, by_lane(acc[64:128, :]))
-        put_terms(stat, 6, jnp.sum(acc[128:160, :], axis=0, keepdims=True))
-        put_terms(stat, 9, jnp.sum(acc[160:192, :], axis=0, keepdims=True))
-        sums = stat[...].astype(BF16)
-
-        def send(p, _):
-            for k in range(2):
-                send_buf[p, 32 * k : 32 * k + 32] = held[jnp.minimum(links[k, p], FACES - 1)]
-                send_buf[p, 64 + 32 * k : 96 + 32 * k] = pooled[
-                    jnp.minimum(csend[k, p], SLOTS - 1)
-                ]
-            send_buf[p, 128:144] = sums
-            return 0
-
-        lax.fori_loop(0, DEVS, send, 0, unroll=4)
-        give = pltpu.make_async_copy(send_buf, out, sem.at[1])
-        give.start()
-        keep.wait()
-        give.wait()
+        for k in range(4):
+            for v in range(4):
+                piece = wide[k, :, 128 * v : 128 * v + 128]
+                s = s + piece
+                q = q + piece * piece
+        for j in range(2):
+            for f in range(7):
+                low = layers[64 * f : 64 * f + 32, 128 * j : 128 * j + 128]
+                high = layers[64 * f + 32 : 64 * f + 64, 128 * j : 128 * j + 128]
+                pair = (
+                    jnp.where(left, low, pltpu.roll(high, 64, 1)),
+                    jnp.where(left, pltpu.roll(low, 64, 1), high),
+                )
+                for k in range(2):
+                    unit = pair[k].astype(BF16)
+                    slot = 4 * n + 2 * j + k
+                    if f < 6:
+                        held[slot * 3 + f // 2, 32 * (f % 2) : 32 * (f % 2) + 32] = unit
+                    else:
+                        pooled[slot] = unit
+                        wide = unit.astype(F32)
+                        ps = ps + wide
+                        pq = pq + wide * wide
+        keep(n).start()
+        return s, q, ps, pq
+
+    zero = jnp.zeros((64, 128), F32)
+    small = jnp.zeros((32, 128), F32)
+    s, q, ps, pq = lax.fori_loop(0, 8, step, (zero, zero, small, small), unroll=2)
+    ones = jnp.ones((8, 128), F32)
+    both = jnp.concatenate([s, q], axis=0)
+    rows = lax.dot_general(ones, both, NT, precision=HIGH, preferred_element_type=F32)
+    turned = pltpu.roll(rows, 64, 1)
+    first = lanes(8) < 64
+    stat[...] = jnp.zeros((16, 128), F32)
+    put_terms(stat, 0, jnp.where(first, rows, turned)[0:1])
+    put_terms(stat, 3, jnp.where(first, turned, rows)[0:1])
+    put_terms(stat, 6, jnp.sum(ps, axis=0, keepdims=True))
+    put_terms(stat, 9, jnp.sum(pq, axis=0, keepdims=True))
+    sums = stat[...].astype(BF16)
+
+    def send(p, _):
+        for k in range(2):
+            code = jnp.minimum(links[k, p], FACES - 1)
+            at = pl.multiple_of(32 * (code & 1), 32)
+            send_buf[p, 32 * k : 32 * k + 32] = held[code >> 1, pl.ds(at, 32)]
+            send_buf[p, 64 + 32 * k : 96 + 32 * k] = pooled[jnp.minimum(csend[k, p], SLOTS - 1)]
+        send_buf[p, 128:144] = sums
+        return 0
+
+    lax.fori_loop(0, DEVS, send, 0, unroll=8)
+    give = pltpu.make_async_copy(send_buf, out, sem.at[8])
+    give.start()
+    for n in range(8):
+        keep(n).wait()
+    give.wait()
 
 
 def plan_kernel(nbr, links, csend, crecv, sel, tsel, ssel):
@@ -242,78 +257,73 @@
     lax.fori_loop(0, DEVS, mark, 0)
 
 
-def octant1_kernel(tsel, me, recv, par, x1, x2, x3, o0, o1, o2, o3, own, buf, stat, sem):
+def border1_kernel(
+    sel, tsel, me, par, faces, recv, x1, x2, x3,
+    p0, p1, p2, p3, o0, o1, o2, o3,
+    told_in, rough_in, src, first, buf, stat, psem, sem, load,
+):
     y = me[0]
+    fetches = [
+        pltpu.make_async_copy(recv.at[:, pl.ds(128, 16)], told_in, load.at[0]),
+        pltpu.make_async_copy(recv.at[:, pl.ds(64, 64)], rough_in, load.at[1]),
+        pltpu.make_async_copy(recv.at[:, pl.ds(0, 64)], src.at[pl.ds(96, DEVS)], load.at[2]),
+        pltpu.make_async_copy(faces, src.at[pl.ds(0, 96)], load.at[3]),
+    ]
+    for fetch in fetches:
+        fetch.start()
+    src[96 + DEVS] = jnp.zeros((64, 128), BF16)
+    fetches[0].wait()
 
     def add(s, total):
-        return total + recv[s, 128:144].astype(F32)
+        return total + told_in[s].astype(F32)
 
     sums = lax.fori_loop(0, DEVS, add, jnp.zeros((16, 128), F32), unroll=8)
     fine = float(DEVS * SLOTS * VOX * GROUP)
     rough = float(DEVS * SLOTS * 64 * GROUP)
+    groups = group_matrix(64)
     mean1, scale1 = norm_rows(
-        group_sum(joined(sums, 0)) * 0.5, group_sum(joined(sums, 3)) * 0.5, fine, par[0:1]
+        group_sum(joined(sums, 0), groups) * 0.5,
+        group_sum(joined(sums, 3), groups) * 0.5,
+        fine,
+        par[0:1],
     )
     mean3, scale3 = norm_rows(
-        group_sum(joined(sums, 6)), group_sum(joined(sums, 9)), rough, par[2:3]
+        group_sum(joined(sums, 6), groups), group_sum(joined(sums, 9), groups), rough, par[2:3]
     )
     bias1, bias3 = par[1:2], par[3:4]
-    own[0:1, :] = mean1
-    own[1:2, :] = scale1
-    own[2:3, :] = bias1
     stat[...] = jnp.zeros((32, 128), F32)
-    put_terms(stat, 0, mean1)
-    put_terms(stat, 3, scale1)
-    put_terms(stat, 6, bias1)
-    put_terms(stat, 9, par[4:5])
-    put_terms(stat, 12, par[5:6])
-    put_terms(stat, 15, par[6:7])
+    for k, row in enumerate((mean1, scale1, bias1, par[4:5], par[5:6], par[6:7])):
+        put_terms(stat, 3 * k, row)
     told = stat[...].astype(BF16)
+    fetches[1].wait()
     copies = []
-    for r, o in enumerate((o0, o1, o2, o3)):
+    for r, p in enumerate((p0, p1, p2, p3)):
         q = (y + r) & 3
-        buf[r, 16] = told
+        first[r, 16] = told
 
         def octant(i, _):
-            for k in range(4):
-                far = tsel[q * 16 + i * 4 + k]
+            for k in range(8):
+                far = tsel[q * 16 + i * 8 + k]
                 link = jnp.minimum(far, 2 * DEVS - 1)
-                at = pl.multiple_of(64 + 32 * (link & 1), 32)
-                u = recv[link >> 1, pl.ds(at, 32)].astype(F32)
+                at = pl.multiple_of(32 * (link & 1), 32)
+                u = rough_in[link >> 1, pl.ds(at, 32)].astype(F32)
                 v = silu((u - mean3) * scale3 + bias3)
-                buf[r, i * 4 + k] = (v * (far < 2 * DEVS).astype(F32)).astype(BF16)
+                first[r, i * 8 + k] = (v * (far < 2 * DEVS).astype(F32)).astype(BF16)
             return 0
 
-        lax.fori_loop(0, 4, octant, 0)
-        copies.append(pltpu.make_async_copy(buf.at[r], o, sem.at[r]))
+        lax.fori_loop(0, 2, octant, 0)
+        copies.append(pltpu.make_async_copy(first.at[r], p, psem.at[r]))
         copies[-1].start()
-    for copy in copies:
-        copy.wait()
-
-
-def border1_kernel(sel, me, own, faces, recv, o0, o1, o2, o3, src, buf, sem, load):
-    y = me[0]
-    fetch = pltpu.make_async_copy(faces, src.at[pl.ds(0, FACES)], load)
-    fetch.start()
-
-    def place(s, _):
-        src[FACES + 2 * s] = recv[s, 0:32]
-        src[FACES + 2 * s + 1] = recv[s, 32:64]
-        return 0
-
-    lax.fori_loop(0, DEVS, place, 0, unroll=4)
-    src[FACES + 2 * DEVS] = jnp.zeros((32, 128), BF16)
-    mean, scale, bias = own[0:1], own[1:2], own[2:3]
-    fetch.wait()
-    copies = []
+    for fetch in fetches[2:]:
+        fetch.wait()
     for r, o in enumerate((o0, o1, o2, o3)):
         q = (y + r) & 3
 
         def face(i, _):
             for f in range(6):
                 at = sel[q * 48 + i * 6 + f]
-                u = src[at].astype(F32)
-                v = silu((u - mean) * scale + bias)
+                u = src[at >> 1, pl.ds(pl.multiple_of(32 * (at & 1), 32), 32)].astype(F32)
+                v = silu((u - mean1) * scale1 + bias1)
                 buf[r, i * 6 + f] = (v * (at < FACES + 2 * DEVS).astype(F32)).astype(BF16)
             return 0
 
@@ -345,37 +355,31 @@
     taps[:, 1536:1792] = high.astype(BF16)
 
 
-def halves(first, second, core, which):
-    def pieces(c, t):
+def fill_weights(dst, first, second, core, which):
+    for c in range(4):
         for side, part in enumerate((first, second)):
-            yield pl.multiple_of(64 * c + 32 * (core ^ side), 32), part[c, which, t]
-
-    return pieces
-
-
-def fill_weights(dst, pieces):
+            at = pl.multiple_of(64 * c + 32 * (core ^ side), 32)
+            for t in range(7):
+                dst[pl.ds(at, 32), 256 * t : 256 * t + 256] = part[c, which, t]
+
+
+def fill_tap_weights(dst, first, second, core, which):
     for c in range(4):
-        for t in range(7):
-            for at, rows in pieces(c, t):
-                dst[pl.ds(at, rows.shape[0]), 256 * t : 256 * t + 256] = rows
-
-
-def fill_tap_weights(dst, pieces):
-    for c in range(4):
-        for f in range(6):
-            for at, rows in pieces(c, 1 + f):
-                dst[f, pl.ds(at, rows.shape[0]), :] = rows
+        for side, part in enumerate((first, second)):
+            at = pl.multiple_of(64 * c + 32 * (core ^ side), 32)
+            for f in range(6):
+                dst[f, pl.ds(at, 32), :] = part[c, which, 1 + f]
 
 
 def fill_cube(cube, volumes, y):
-    for r, v in enumerate(volumes):
+    for r, v in zip(ORDER, volumes):
         at = pl.multiple_of(((y - r) & 3) * 64, 64)
         cube[pl.ds(at, 64), :] = v[0].astype(F32)
 
 
 def place_rows(rows, told, y, stat):
     rows[...] = jnp.zeros((8, 256), F32)
-    for r, t in enumerate(told):
+    for r, t in zip(ORDER, told):
         stat[(y - r) & 3] = t[0].astype(F32)
     for k in range(6):
         rows[k : k + 1, :] = gather_row([joined(stat[c], 3 * k) for c in range(4)])
@@ -389,7 +393,7 @@
     @pl.when(pl.program_id(0) == 0)
     def _():
         place_rows(rows, (t0, t1, t2, t3), y, stat)
-        fill_weights(weights, halves(wa, wb, me[1], 0))
+        fill_weights(weights, wa, wb, me[1], 0)
 
     fill_cube(cube, (v0, v1, v2, v3), y)
     x = cube[...].T
@@ -408,7 +412,7 @@
     def _():
         for n in range(QUART):
             fetch_cells(n).start()
-        fill_weights(weights, halves(wa, wb, me[1], 1))
+        fill_weights(weights, wa, wb, me[1], 1)
 
     fetch_cells(step).wait()
     act = silu((cells[step] - rows[0:1]) * rows[1:2] + rows[2:3]).astype(BF16)
@@ -416,14 +420,14 @@
     part[0] = lax.dot_general(taps[...], weights[...], NT, preferred_element_type=F32)
 
 
-def border_terms(units, tap_weights, parts, y, across):
-    for r, u in enumerate(parts):
+def border_terms(units, tap_weights, parts, y, across, start, count):
+    for r, u in zip(ORDER, parts):
         units[(y - r) & 3] = u[...]
     for f in range(6):
         layer = jnp.concatenate(
             [
                 unpack([units[c, 6 * n + f].astype(F32) for c in range(4)]).astype(BF16)
-                for n in range(QUART)
+                for n in range(start, start + count)
             ],
             axis=0,
         )
@@ -458,57 +462,54 @@
 def outer1_kernel(
     me, rows, part, u0, u1, u2, u3, tiles, wa, wb,
     hid, o0, o1, o2, o3,
-    units, outs, weights, across, shift, stat, sums, cells, sem,
+    units, outs, weights, across, shift, stat, cells, sem,
 ):
-    step = pl.program_id(0)
     y = me[0]
+    fill_tap_weights(weights, wa, wb, me[1], 0)
+    border_terms(units, weights, (u0, u1, u2, u3), y, across, 0, QUART)
+    stat[...] = jnp.zeros((4, 32, 128), F32)
 
     def keep_cells(n):
         return pltpu.make_async_copy(cells.at[n], hid.at[n], sem.at[n])
 
-    @pl.when(step == 0)
-    def _():
-        fill_tap_weights(weights, halves(wa, wb, me[1], 0))
-        border_terms(units, weights, (u0, u1, u2, u3), y, across)
-        sums[...] = jnp.zeros((8, 256), F32)
-        stat[...] = jnp.zeros((4, 32, 128), F32)
-
-    h, edges = add_borders(part[0] + rows[3:4], across, step, shift)
-    cells[step] = h
-    keep_cells(step).start()
-    total = jnp.sum(h, axis=0, keepdims=True)
-    sums[0:1] += total
-    sums[1:2] += jnp.sum(h * h, axis=0, keepdims=True)
-    centre = (total * (1.0 / VOX)).astype(BF16).astype(F32)
-    for c, row in enumerate(spread_row(centre)):
-        stat[c, pl.ds(step, 1), :] = row
-    deep = h.reshape(8, 8, 8, 256)
-    for f in range(6):
-        if f < 2:
-            layer = h[448 * f : 448 * f + 64]
-        elif f < 4:
-            layer = deep[:, 7 * (f - 2)].reshape(64, 256)
-        else:
-            layer = edges[f - 4]
-        for c, unit in enumerate(pack(layer - centre)):
-            outs[c, step * 6 + f] = unit.astype(BF16)
-
-    @pl.when(step == QUART - 1)
-    def _():
-        at = 8
-        for k in range(2):
-            for half in range(2):
-                for row in terms(sums[k : k + 1, 128 * half : 128 * half + 128]):
-                    for c in range(4):
-                        stat[c, at : at + 1, :] = row
-                    at += 1
-        for c in range(4):
-            outs[c, 48] = stat[c].astype(BF16)
-        for r, o in enumerate((o0, o1, o2, o3)):
-            o[0:49] = outs[(y + r) & 3]
-            o[49:65] = tiles[(y + r) & 3]
-        for n in range(QUART):
-            keep_cells(n).wait()
+    def slot(n, carry):
+        all_total, all_square = carry
+        h, edges = add_borders(part[n] + rows[3:4], across, n, shift)
+        cells[n] = h
+        keep_cells(n).start()
+        total = jnp.sum(h, axis=0, keepdims=True)
+        square = jnp.sum(h * h, axis=0, keepdims=True)
+        centre = (total * (1.0 / VOX)).astype(BF16).astype(F32)
+        for c, row in enumerate(spread_row(centre)):
+            stat[c, pl.ds(n, 1), :] = row
+        deep = h.reshape(8, 8, 8, 256)
+        for f in range(6):
+            if f < 2:
+                layer = h[448 * f : 448 * f + 64]
+            elif f < 4:
+                layer = deep[:, 7 * (f - 2)].reshape(64, 256)
+            else:
+                layer = edges[f - 4]
+            for c, unit in enumerate(pack(layer - centre)):
+                outs[c, n * 6 + f] = unit.astype(BF16)
+        return all_total + total, all_square + square
+
+    nothing = jnp.zeros((1, 256), F32)
+    sums = lax.fori_loop(0, QUART, slot, (nothing, nothing))
+    at = 8
+    for k in range(2):
+        for half in range(2):
+            for row in terms(sums[k][:, 128 * half : 128 * half + 128]):
+                for c in range(4):
+                    stat[c, at : at + 1, :] = row
+                at += 1
+    for c in range(4):
+        outs[c, 48] = stat[c].astype(BF16)
+    for r, o in enumerate((o0, o1, o2, o3)):
+        o[0:49] = outs[(y + r) & 3]
+        o[49:65] = tiles[(y + r) & 3]
+    for n in range(QUART):
+        keep_cells(n).wait()
 
 
 def placement(rows, columns, code):
@@ -541,9 +542,9 @@
     def _():
         place[...] = placement(VOX, VOX, octant_code)
         place_t[...] = placement(VOX, VOX, voxel_code)
-        fill_weights(weights, halves(wa, wb, me[1], 2))
-
-    for r, u in enumerate((u0, u1, u2, u3)):
+        fill_weights(weights, wa, wb, me[1], 2)
+
+    for r, u in zip(ORDER, (u0, u1, u2, u3)):
         units[(y - r) & 3] = u[...]
     octants = jnp.concatenate(
         [unpack([units[c, o].astype(F32) for c in range(4)]).astype(BF16) for o in range(8)], axis=0
@@ -561,7 +562,7 @@
     links, crecv, me, v0, v1, v2, v3, keep, out, held, cen, stat, send_buf, sem
 ):
     y = me[0]
-    for r, v in enumerate((v0, v1, v2, v3)):
+    for r, v in zip(ORDER, (v0, v1, v2, v3)):
         held[(y - r) & 3] = v[...]
     kept = pltpu.make_async_copy(held, keep, sem.at[0])
     kept.start()
@@ -670,32 +671,37 @@
     me, part, v0, v1, v2, v3, u0, u1, u2, u3, wa, wb,
     o0, o1, o2, o3,
     units, weights, across, shift, cube, lift,
+    *, start,
 ):
-    step = pl.program_id(0)
     y = me[0]
-
-    @pl.when(step == 0)
-    def _():
-        lift[...] = placement(VOX, 64, coarse_code)
-        fill_tap_weights(weights, halves(wa, wb, me[1], 1))
-        border_terms(units, weights, (u0, u1, u2, u3), y, across)
-
-    raised = unpack([units[c, 48 + step].astype(F32) for c in range(4)]).astype(BF16)
-    lifted = lax.dot_general(lift[...], raised, NN, preferred_element_type=F32)
-    h, _ = add_borders(part[0] + lifted, across, step, shift)
-    fill_cube(cube, (v0, v1, v2, v3), y)
-    cube[...] += h.T
-    for r, o in enumerate((o0, o1, o2, o3)):
-        at = pl.multiple_of(((y + r) & 3) * 64, 64)
-        o[0] = cube[pl.ds(at, 64), :].astype(BF16)
-
-
-def gather_kernel(me, p0, p1, p2, p3, out, sem):
+    lift[...] = placement(VOX, 64, coarse_code)
+    fill_tap_weights(weights, wa, wb, me[1], 1)
+    border_terms(units, weights, (u0, u1, u2, u3), y, across, start, HALF)
+
+    def slot(n, _):
+        m = start + n
+        raised = unpack([units[c, 48 + m].astype(F32) for c in range(4)]).astype(BF16)
+        lifted = lax.dot_general(lift[...], raised, NN, preferred_element_type=F32)
+        h, _ = add_borders(part[m] + lifted, across, n, shift)
+        for r, v in zip(ORDER, (v0, v1, v2, v3)):
+            at = pl.multiple_of(((y - r) & 3) * 64, 64)
+            cube[pl.ds(at, 64), :] = v[QUART * y + m if r == 0 else m].astype(F32)
+        cube[...] += h.T
+        for r, o in enumerate((o0, o1, o2, o3)):
+            at = pl.multiple_of(((y + r) & 3) * 64, 64)
+            o[n] = cube[pl.ds(at, 64), :].astype(BF16)
+        return 0
+
+    lax.fori_loop(0, HALF, slot, 0)
+
+
+def gather_kernel(me, *refs):
+    *parts, out, sem = refs
     y = me[0]
     copies = []
-    for r, p in enumerate((p0, p1, p2, p3)):
-        at = pl.multiple_of(((y - r) & 3) * QUART, QUART)
-        copies.append(pltpu.make_async_copy(p, out.at[pl.ds(at, QUART)], sem.at[r]))
+    for k, p in enumerate(parts):
+        at = ((y - ORDER[k % 4]) & 3) * QUART + HALF * (k // 4)
+        copies.append(pltpu.make_async_copy(p, out.at[pl.ds(at, HALF)], sem.at[k]))
         copies[-1].start()
     for copy in copies:
         copy.wait()
@@ -719,9 +725,9 @@
 
 def exchange(parts, order=(0, 1, 2, 3)):
     got = {
-        r: lax.ppermute(parts[r], "chan", [(i, (i + r) % 4) for i in order]) for r in (2, 1, 3)
+        r: lax.ppermute(parts[r], "chan", [(i, (i + r) % 4) for i in order]) for r in ORDER[1:]
     }
-    return [parts[0], got[1], got[2], got[3]]
+    return [parts[0]] + [got[r] for r in ORDER[1:]]
 
 
 def over_blocks(units):
@@ -757,31 +763,32 @@
         [norm_gain[0], norm_bias[0], norm_gain[2], norm_bias[2], time_bias]
         + [norm_gain[1], norm_bias[1]]
     )
-    half = lax.dynamic_slice_in_dim(conv_weights, 32 * core, 32, axis=2)
-    wa = lax.all_gather(half, "chan", axis=0, tiled=False)
-
     faces, outgoing = call(
         extract_kernel,
         "extract",
         60,
-        grid=(8,),
-        out_shape=(shape(FACES, 32, 128), shape(DEVS, ROWS, 128)),
-        in_specs=[SMEM, SMEM, pl.BlockSpec((4, 64, VOX), lambda i: (i, 0, 0)), VMEM],
-        out_specs=(HBM, HBM),
+        out_shape=(shape(FACES // 2, 64, 128), shape(DEVS, ROWS, 128)),
+        in_specs=[SMEM] * 2 + [HBM] * 2,
+        out_specs=(HBM,) * 2,
         scratch_shapes=[
-            pltpu.VMEM((FACES, 32, 128), BF16),
+            pltpu.VMEM((SLOTS, 64, VOX), BF16),
+            pltpu.VMEM((448, VOX), BF16),
+            pltpu.VMEM((FACES // 2, 64, 128), BF16),
             pltpu.VMEM((SLOTS, 32, 128), BF16),
-            pltpu.VMEM((192, 128), F32),
             pltpu.VMEM((16, 128), F32),
             pltpu.VMEM((DEVS, ROWS, 128), BF16),
-            pltpu.SemaphoreType.DMA((2,)),
+            pltpu.SemaphoreType.DMA((9,)),
+            pltpu.SemaphoreType.DMA((9,)),
         ],
     )(links, csend, feats, jnp.asarray(extract_np, BF16))
     arrived = over_blocks(outgoing)
+    half = lax.dynamic_slice_in_dim(conv_weights, 32 * core, 32, axis=2)
+    wa = lax.all_gather(half, "chan", axis=0, tiled=False)
     volumes = exchange(
-        [
+        [feats]
+        + [
             lax.dynamic_slice_in_dim(feats, QUART * ((y + r) % 4), QUART, axis=0)
-            for r in range(4)
+            for r in range(1, 4)
         ]
     )
     sel, tsel, ssel = call(
@@ -798,56 +805,66 @@
         out_specs=(SMEM,) * 3,
     )(nbr, links, csend, crecv)
 
-    *parts, own = call(
-        octant1_kernel,
-        "octant1",
-        8,
-        out_shape=(shape(17, 32, 128),) * 4 + (shape(8, 128, dtype=F32),),
-        in_specs=[SMEM] * 2 + [VMEM] * 2 + [HBM] * 3,
-        out_specs=(ANY,) * 4 + (VMEM,),
-        scratch_shapes=[
-            pltpu.VMEM((4, 17, 32, 128), BF16),
-            pltpu.VMEM((32, 128), F32),
-            pltpu.SemaphoreType.DMA((4,)),
-        ],
-    )(tsel, me, arrived, par, *volumes[1:])
-    tiles1 = exchange(parts, (3, 2, 1, 0))
-    wa, _ = lax.optimization_barrier((wa, own))
-    wb = lax.ppermute(wa, "blocks", [(i, i ^ 1) for i in range(DEVS)])
     parts = call(
         border1_kernel,
         "border1",
-        12,
-        out_shape=(shape(48, 32, 128),) * 4,
-        in_specs=[SMEM] * 2 + [VMEM, HBM, VMEM],
-        out_specs=(ANY,) * 4,
+        60,
+        out_shape=(shape(17, 32, 128),) * 4 + (shape(48, 32, 128),) * 4,
+        in_specs=[SMEM] * 3 + [VMEM] + [HBM] * 5,
+        out_specs=(HBM,) * 8,
         scratch_shapes=[
-            pltpu.VMEM((FACES + 2 * DEVS + 1, 32, 128), BF16),
+            pltpu.VMEM((DEVS, 16, 128), BF16),
+            pltpu.VMEM((DEVS, 64, 128), BF16),
+            pltpu.VMEM((FACES // 2 + DEVS + 1, 64, 128), BF16),
+            pltpu.VMEM((4, 17, 32, 128), BF16),
             pltpu.VMEM((4, 48, 32, 128), BF16),
+            pltpu.VMEM((32, 128), F32),
             pltpu.SemaphoreType.DMA((4,)),
-            pltpu.SemaphoreType.DMA,
+            pltpu.SemaphoreType.DMA((4,)),
+            pltpu.SemaphoreType.DMA((4,)),
         ],
-    )(sel, me, own, faces, arrived)
-    units1 = exchange(parts)
-
-    slots = pl.BlockSpec((1, 64, VOX), lambda i: (i, 0, 0))
+    )(sel, tsel, me, par, faces, arrived, *volumes[1:])
+    tiles1 = exchange(parts[:4], (3, 2, 1, 0))
+    units1 = exchange(parts[4:])
+    wa, _ = lax.optimization_barrier((wa, parts[0]))
+    wb = lax.ppermute(wa, "blocks", [(i, i ^ 1) for i in range(DEVS)])
+
     cells = pl.BlockSpec((1, VOX, 256), lambda i: (i, 0, 0))
-    last = pl.BlockSpec((1, 32, 128), lambda i: (16, 0, 0))
+
+    def prefetched(count, in_specs, out_specs, scratch_shapes):
+        return pltpu.PrefetchScalarGridSpec(
+            num_scalar_prefetch=1,
+            grid=(count,),
+            in_specs=in_specs,
+            out_specs=out_specs,
+            scratch_shapes=scratch_shapes,
+        )
+
+    def slot_specs(start):
+        first = pl.BlockSpec((1, 64, VOX), lambda i, me: (QUART * me[0] + start + i, 0, 0))
+        return [first] + [pl.BlockSpec((1, 64, VOX), lambda i, me: (start + i, 0, 0))] * 3
+
+    def cell_spec(start):
+        return pl.BlockSpec((1, VOX, 256), lambda i, me: (start + i, 0, 0))
+
+    last = pl.BlockSpec((1, 32, 128), lambda i, me: (16, 0, 0))
     part1, rows = call(
         inner1_kernel,
         "inner1",
         24,
         8,
-        grid=(QUART,),
+        grid_spec=prefetched(
+            QUART,
+            [last] * 4 + slot_specs(0) + [VMEM] * 2,
+            (cell_spec(0), VMEM),
+            [
+                pltpu.VMEM((256, 1792), BF16),
+                pltpu.VMEM((4, 32, 128), F32),
+                pltpu.VMEM((VOX, 1792), BF16),
+                pltpu.VMEM((256, VOX), F32),
+            ],
+        ),
         out_shape=(shape(QUART, VOX, 256, dtype=F32), shape(8, 256, dtype=F32)),
-        in_specs=[SMEM] + [last] * 4 + [slots] * 4 + [VMEM] * 2,
-        out_specs=(cells, VMEM),
-        scratch_shapes=[
-            pltpu.VMEM((256, 1792), BF16),
-            pltpu.VMEM((4, 32, 128), F32),
-            pltpu.VMEM((VOX, 1792), BF16),
-            pltpu.VMEM((256, VOX), F32),
-        ],
     )(me, *tiles1, *volumes, wa, wb)
     eight = pl.BlockSpec((8, 32, 128), lambda t: (t, 0, 0))
     coarse = call(
@@ -872,9 +889,8 @@
         "outer1",
         32,
         5,
-        grid=(QUART,),
         out_shape=(shape(QUART, VOX, 256, dtype=F32),) + (shape(65, 32, 128),) * 4,
-        in_specs=[SMEM, VMEM, cells] + [VMEM] * 7,
+        in_specs=[SMEM] + [VMEM] * 9,
         out_specs=(HBM,) + (VMEM,) * 4,
         scratch_shapes=[
             pltpu.VMEM((4, 48, 32, 128), BF16),
@@ -883,7 +899,6 @@
             pltpu.VMEM((6, VOX, 256), F32),
             pltpu.VMEM((2, VOX, 128), F32),
             pltpu.VMEM((4, 32, 128), F32),
-            pltpu.VMEM((8, 256), F32),
             pltpu.VMEM((QUART, VOX, 256), F32),
             pltpu.SemaphoreType.DMA((QUART,)),
         ],
@@ -939,34 +954,35 @@
             pltpu.SemaphoreType.DMA((QUART,)),
         ],
     )(me, norm, hidden, wa, wb)
-    parts = call(
-        outer2_kernel,
-        "outer2",
-        32,
-        5,
-        grid=(QUART,),
-        out_shape=(shape(QUART, 64, VOX),) * 4,
-        in_specs=[SMEM, cells] + [slots] * 4 + [VMEM] * 6,
-        out_specs=(slots,) * 4,
-        scratch_shapes=[
-            pltpu.VMEM((4, 56, 32, 128), BF16),
-            pltpu.VMEM((6, 256, 256), BF16),
-            pltpu.VMEM((6, VOX, 256), F32),
-            pltpu.VMEM((2, VOX, 128), F32),
-            pltpu.VMEM((256, VOX), F32),
-            pltpu.VMEM((VOX, 64), BF16),
-        ],
-    )(me, part2, *volumes, *units2, wa, wb)
-    parts = exchange(parts)
+    pieces = []
+    for start in (0, HALF):
+        parts = call(
+            functools.partial(outer2_kernel, start=start),
+            "outer2",
+            32,
+            5,
+            in_specs=[SMEM] + [VMEM] * 11,
+            out_specs=(VMEM,) * 4,
+            scratch_shapes=[
+                pltpu.VMEM((4, 56, 32, 128), BF16),
+                pltpu.VMEM((6, 256, 256), BF16),
+                pltpu.VMEM((6, 64 * HALF, 256), F32),
+                pltpu.VMEM((2, VOX, 128), F32),
+                pltpu.VMEM((256, VOX), F32),
+                pltpu.VMEM((VOX, 64), BF16),
+            ],
+            out_shape=(shape(HALF, 64, VOX),) * 4,
+        )(me, part2, *volumes, *units2, wa, wb)
+        pieces += exchange(parts, (0, 1, 2, 3) if start == 0 else (3, 2, 1, 0))
     return call(
         gather_kernel,
         "gather",
         4,
         out_shape=shape(SLOTS, 64, VOX),
-        in_specs=[SMEM] + [ANY] * 4,
+        in_specs=[SMEM] + [ANY] * 8,
         out_specs=HBM,
-        scratch_shapes=[pltpu.SemaphoreType.DMA((4,))],
-    )(me, *parts)
+        scratch_shapes=[pltpu.SemaphoreType.DMA((8,))],
+    )(me, *pieces)
 
 
 def solution(mesh):

time: 220 us -> 215 us (0.977)
  waiting for transfers between devices: 78.9 us -> 66.4 us
  starting transfers between devices: 36 us -> 40.2 us
  local copies, waits for them, and re-layouts: 8.69 us -> 11.1 us
    ppermute x18 -> x21, waiting for transfers between devices: 75.8 us -> 64.8 us  [exchange(): lax.ppermute(parts[r], 'chan', [(i, (i + r) % 4) for i in order])]
    ppermute x18 -> x21, starting transfers between devices: 24.9 us -> 28.9 us  [exchange(): lax.ppermute(parts[r], 'chan', [(i, (i + r) % 4) for i in order])]
    unnamed x30 -> x52, local copies, waits for them, and re-layouts: 5.15 us -> 7.72 us
  transfers between devices with their start and end apart: 21 -> 24, of which waited for: 11 -> 11; matrix products, arithmetic and copies ran while one was open for 1% -> 2% of each run, Pallas kernels for 16% -> 17%
where the time goes in v3:
time: 215 us
  waiting for transfers between devices  66.4 us (31%)
  Pallas kernels  55.1 us (26%)
  starting transfers between devices  40.2 us (19%)
  blocking collectives  26.8 us (12%)
  between operations  13.8 us (6%)
  local copies, waits for them, and re-layouts  11.1 us (5%)
    ppermute x21, waiting for transfers between devices, exchange(): lax.ppermute(parts[r], 'chan', [(i, (i + r) % 4) for i in order])  64.8 us
    ppermute x21, starting transfers between devices, exchange(): lax.ppermute(parts[r], 'chan', [(i, (i + r) % 4) for i in order])  28.9 us
    all_to_all x1, blocking collectives, over_blocks(): lax.all_to_all(units, 'blocks', split_axis=0, concat_axis=0, tiled=True)  26.8 us
    all_to_all x1, starting transfers between devices, over_blocks(): lax.all_to_all(units, 'blocks', split_axis=0, concat_axis=0, tiled=True)  9.63 us
    pallas_call x2, Pallas kernels, local(): call(functools.partial(outer2_kernel, start=start), 'outer2', 32, 5, in_s...  7.84 us
    unnamed x52, local copies, waits for them, and re-layouts  7.72 us
    pallas_call x1, Pallas kernels, local(): call(extract_kernel, 'extract', 60, out_shape=(shape(FACES // 2, 64, 128)...  7.64 us
    pallas_call x1, Pallas kernels, local(): call(inner1_kernel, 'inner1', 24, 8, grid_spec=prefetched(QUART, [last] *...  7.03 us
  transfers between devices with their start and end apart: 24, of which 11 were waited for; matrix products, arithmetic and copies ran while one was open for 2% of the time, Pallas kernels for 17%

profile of v3, /device:TPU:1, one launch (start us, length us, event | category | flops | bytes accessed | tf_op | source)
XLA Modules:
  0.0 214.7 jit_solution(11638161424689373559)
XLA Ops:
  6.5 1.1 copy-done
  7.6 0.8 constant_dynamic-slice_fusion
  8.4 0.0 all-gather.3.cloned.1.call-update
  8.5 2.5 %constant_dynamic-slice_fusion.1 = (bf16[8,64,512]{2,1,0:T(8,128)(2,1)}, bf16[8,64,512]{2,1,0:T(8,128)(2,1)}, bf16[8,64,512]{2,1,0:T(8,128)(2,1)S(1)}) fusion(bf16[32,64,512]{2,1,0:T(8,128)(2,1)} %v0.5, s32[]{:T(128)S(6)} %select_n.37, s32[]{:T(128)S(6)} %select_n.35, s32[]{:T(128)S(6)} %select_n.33), kind=kLoop, calls=%fused_computation.3 | loop fusion | bytes 3145740 | tf_op jit(solution)/shard_map/dynamic_slice | solution.py:790
  11.0 3.6 %collective-permute-start.2 = (bf16[8,64,512]{2,1,0:T(8,128)(2,1)}, bf16[8,64,512]{2,1,0:T(8,128)(2,1)S(1)}, u32[]{:S(2)}, u32[]{:S(2)}) collective-permute-start(bf16[8,64,512]{2,1,0:T(8,128)(2,1)} %get-tuple-element.77), channel_id=1, source_target_pairs={{0,3},{1,0},{2,1},{3,2},{4,7},{5,4},{6,5},{7,6},{8,11},{9,8},{10,9... | collective-permute-start | bytes 1572872 | tf_op jit(solution)/shard_map/ppermute | solution.py:728
  14.6 1.6 collective-permute-start
  16.2 7.6 %extract.1 = (bf16[96,64,128]{2,1,0:T(8,128)(2,1)}, bf16[32,144,128]{2,1,0:T(8,128)(2,1)}) custom-call(s32[2,32]{1,0:T(2,128)} %bitcast.24, s32[2,32]{1,0:T(2,128)} %bitcast.22, bf16[32,64,512]{2,1,0:T(8,128)(2,1)} %v0.5, bf16[448,512]{1,0:T(8,128)(2,1)} %constant.53.clone.table), custom_call_target="tpu_custom_call" | custom-call | flops 1000000000 | bytes 3000000 | tf_op jit(solution)/shard_map/extract/pallas_call | solution.py:766
  23.9 0.0 copy-start.19
  23.9 0.0 copy-start.20
  23.9 0.0 copy-start.22
  23.9 9.6 %all-to-all-start = ((bf16[32,144,128]{2,1,0:T(8,128)(2,1)}), bf16[32,144,128]{2,1,0:T(8,128)(2,1)}, u32[]{:S(2)}, u32[]{:S(2)}) async-start(bf16[32,144,128]{2,1,0:T(8,128)(2,1)} %get-tuple-element.45), calls=%async_computation | async-start | bytes 2359296 | tf_op jit(solution)/shard_map/all_to_all | solution.py:734
  33.6 0.0 copy-start.23
  33.6 2.7 %plan.1 = (s32[192]{0:T(256)S(1)}, s32[64]{0:T(128)S(1)}, s32[32]{0:T(128)S(1)}) custom-call(s32[6,32]{1,0:T(8,128)S(1)} %bitcast.21, s32[2,32]{1,0:T(2,128)S(1)} %bitcast.25, s32[2,32]{1,0:T(2,128)S(1)} %bitcast.23, s32[2,32]{1,0:T(2,128)S(1)} %bitcast.27), custom_call_target="tpu_custom_call" | custom-call | flops 20000000000 | bytes 60000000 | tf_op jit(solution)/shard_map/plan/pallas_call | solution.py:794
  36.3 0.6 copy-done.12
  36.9 0.6 copy-done.14
  37.5 0.7 pad_add_fusion.me
  38.2 0.7 select_maximum_fusion.par
  38.9 10.9 %collective-permute-done.x1.v1 = bf16[8,64,512]{2,1,0:T(8,128)(2,1)S(1)} collective-permute-done((bf16[8,64,512]{2,1,0:T(8,128)(2,1)S(1)}, bf16[8,64,512]{2,1,0:T(8,128)(2,1)S(1)}, u32[]{:S(2)}, u32[]{:S(2)}) %collective-permute-start) | collective-permute-done | bytes 524320 | tf_op jit(solution)/shard_map/ppermute | solution.py:728
  49.7 1.6 all-to-all-done.recv
  51.3 0.0 copy-start.1
  51.3 5.1 %border1.1 = (bf16[17,32,128]{2,1,0:T(8,128)(2,1)}, bf16[17,32,128]{2,1,0:T(8,128)(2,1)}, bf16[17,32,128]{2,1,0:T(8,128)(2,1)}, bf16[17,32,128]{2,1,0:T(8,128)(2...) custom-call(s32[192]{0:T(256)} %copy-done.12, ...), custom_call_target="tpu_custom_call" | custom-call | flops 1000000000 | bytes 3000000 | tf_op jit(solution)/shard_map/border1/pallas_call | solution.py:808
  56.4 0.0 all-gather.3.cloned.1.call-done
  56.4 1.6 collective-permute-start.6
  58.1 1.1 collective-permute-start.3
  59.2 0.6 collective-permute-start.4
  59.7 2.4 %collective-permute-start.5 = (bf16[17,32,128]{2,1,0:T(8,128)(2,1)}, bf16[17,32,128]{2,1,0:T(8,128)(2,1)S(1)}, u32[]{:S(2)}, u32[]{:S(2)}) collective-permute-start(bf16[17,32,128]{2,1,0:T(8,128)(2,1)} %get-tuple-element.49), channel_id=1, source_target_pairs={{3,2},{2,1},{1,0},{0,3},{7,6},{6,5},{5,4},{4,7},{11,10},{10,9},{9,... | collective-permute-start | bytes 417800 | tf_op jit(solution)/shard_map/ppermute | solution.py:728
  62.1 1.2 collective-permute-start.7
  63.3 1.7 collective-permute-done.3.t1.u1
  65.0 1.7 collective-permute-start.8
  66.7 2.2 %collective-permute-done.4.t2.u2 = bf16[17,32,128]{2,1,0:T(8,128)(2,1)S(1)} collective-permute-done((bf16[17,32,128]{2,1,0:T(8,128)(2,1)}, bf16[17,32,128]{2,1,0:T(8,128)(2,1)S(1)}, u32[]{:S(2)}, u32[]{:S(2)}) %collective-permute-start.4) | collective-permute-done | bytes 139296 | tf_op jit(solution)/shard_map/ppermute | solution.py:728
  68.9 1.0 copy-done.3
  69.9 1.0 copy-done.6
  71.0 1.0 copy-done.9
  72.0 1.3 copy-done.15
  73.4 0.9 copy-done.18
  74.3 7.0 %inner1.1 = (f32[8,512,256]{2,1,0:T(8,128)S(1)}, f32[8,256]{1,0:T(8,128)S(1)}) custom-call(s32[2]{0:T(128)S(1)} %copy-done.11, bf16[17,32,128]{2,1,0:T(8,128)(2,1)S(1)} %copy-done.18, bf16[17,32,128]{2,1,0:T(8,128)(2,1)S(1)} %collective-permute-done.3.t1.u1, bf16[17,32,128]{2,1,0:T(8,128)(2,1)S(1)} %collective-permute-done.4.t2.u2, ...), custom_call_target="tpu_custom_call" | custom-call | flops 8000000000 | bytes 24000000 | tf_op jit(solution)/shard_map/inner1/pallas_call | solution.py:851
  81.3 4.3 %tiles.1 = bf16[4,16,32,128]{3,2,1,0:T(8,128)(2,1)S(1)} custom-call(s32[2]{0:T(128)S(1)} %copy-done.11, bf16[17,32,128]{2,1,0:T(8,128)(2,1)S(1)} %copy-done.18, bf16[17,32,128]{2,1,0:T(8,128)(2,1)S(1)} %collective-permute-done.3.t1.u1, bf16[17,32,128]{2,1,0:T(8,128)(2,1)S(1)} %collective-permute-done.4.t2.u2, ...), custom_call_target="tpu_custom_call" | custom-call | flops 4000000000 | bytes 12000000 | tf_op jit(solution)/shard_map/tiles/pallas_call | solution.py:870
  85.7 5.2 %outer1.1 = (f32[8,512,256]{2,1,0:T(8,128)S(1)}, bf16[65,32,128]{2,1,0:T(8,128)(2,1)S(1)}, bf16[65,32,128]{2,1,0:T(8,128)(2,1)S(1)}, bf16[65,32,128]{2,1,0:T(8,128)(2,1)S(1)}, bf16[65,32,128]{2,1,0:T(8,128)(2,1)S(1)}) custom-call(s32[2]{0:T(128)S(1)} %copy-done.11, f32[8,256]{1,0:T(8,128)S(1)} %get-tuple-element.51.rows, ...), custom_call_target="tpu_custom_call" | custom-call | flops 5000000000 | bytes 15000000 | tf_op jit(solution)/shard_map/outer1/pallas_call | solution.py:887
  90.9 1.5 collective-permute-start.10
  92.4 0.3 collective-permute-start.11
  92.8 2.3 %collective-permute-start.12 = (bf16[65,32,128]{2,1,0:T(8,128)(2,1)S(1)}, bf16[65,32,128]{2,1,0:T(8,128)(2,1)S(1)}, u32[]{:S(2)}, u32[]{:S(2)}) collective-permute-start(bf16[65,32,128]{2,1,0:T(8,128)(2,1)S(1)} %get-tuple-element.60), channel_id=1, source_target_pairs={{0,3},{1,0},{2,1},{3,2},{4,7},{5,4},{6,5},{7,6},{8,11},{9,8},{10,9... | collective-permute-start | bytes 1597448 | tf_op jit(solution)/shard_map/ppermute | solution.py:728
  95.1 10.0 %collective-permute-done.10.v1 = bf16[65,32,128]{2,1,0:T(8,128)(2,1)S(1)} collective-permute-done((bf16[65,32,128]{2,1,0:T(8,128)(2,1)S(1)}, bf16[65,32,128]{2,1,0:T(8,128)(2,1)S(1)}, u32[]{:S(2)}, u32[]{:S(2)}) %collective-permute-start.10) | collective-permute-done | bytes 532512 | tf_op jit(solution)/shard_map/ppermute | solution.py:728
  105.1 12.8 %collective-permute-done.11.v2 = bf16[65,32,128]{2,1,0:T(8,128)(2,1)S(1)} collective-permute-done((bf16[65,32,128]{2,1,0:T(8,128)(2,1)S(1)}, bf16[65,32,128]{2,1,0:T(8,128)(2,1)S(1)}, u32[]{:S(2)}, u32[]{:S(2)}) %collective-permute-start.11) | collective-permute-done | bytes 532512 | tf_op jit(solution)/shard_map/ppermute | solution.py:728
  117.9 1.8 route2.1
  119.8 26.8 %all_to_all.10.recv = bf16[32,144,128]{2,1,0:T(8,128)(2,1)S(1)} all-to-all(bf16[32,144,128]{2,1,0:T(8,128)(2,1)S(1)} %get-tuple-element.62), channel_id=1, replica_groups=mesh['blocks'=32,'chan'=4] {'blocks'}, dimensions={0} | all-to-all | bytes 2359296 | tf_op jit(solution)/shard_map/all_to_all | solution.py:734
  146.6 4.8 %border2.1 = (bf16[56,32,128]{2,1,0:T(8,128)(2,1)S(1)}, bf16[56,32,128]{2,1,0:T(8,128)(2,1)S(1)}, bf16[56,32,128]{2,1,0:T(8,128)(2,1)S(1)}, bf16[56,32,128]{2,1,0:T(8,128)(2,1)S(1)}, f32[8,256]{1,0:T(8,128)S(1)}) custom-call(s32[192]{0:T(256)S(1)} %copy-done.13, s32[32]{0:T(128)S(1)} %get-tuple-element.42.ssel, s32[2]{0:T(128)S(1)} %copy-done.11, ...), custom_call_target="tpu_custom_call" | custom-call | flops 1000000000 | bytes 3000000 | tf_op jit(solution)/shard_map/border2/pallas_call | solution.py:925
  151.4 2.2 %collective-permute-start.13 = (bf16[56,32,128]{2,1,0:T(8,128)(2,1)S(1)}, bf16[56,32,128]{2,1,0:T(8,128)(2,1)S(1)}, u32[]{:S(2)}, u32[]{:S(2)}) collective-permute-start(bf16[56,32,128]{2,1,0:T(8,128)(2,1)S(1)} %get-tuple-element.66), channel_id=1, source_target_pairs={{0,2},{1,3},{2,0},{3,1},{4,6},{5,7},{6,4},{7,5},{8,10},{9,11},{10,... | collective-permute-start | bytes 1376264 | tf_op jit(solution)/shard_map/ppermute | solution.py:728
  153.6 0.0 collective-permute-start.14
  153.6 2.7 %collective-permute-start.15 = (bf16[56,32,128]{2,1,0:T(8,128)(2,1)S(1)}, bf16[56,32,128]{2,1,0:T(8,128)(2,1)S(1)}, u32[]{:S(2)}, u32[]{:S(2)}) collective-permute-start(bf16[56,32,128]{2,1,0:T(8,128)(2,1)S(1)} %get-tuple-element.68), channel_id=1, source_target_pairs={{0,3},{1,0},{2,1},{3,2},{4,7},{5,4},{6,5},{7,6},{8,11},{9,8},{10,9... | collective-permute-start | bytes 1376264 | tf_op jit(solution)/shard_map/ppermute | solution.py:728
  156.2 6.7 %inner2.1.part = f32[8,512,256]{2,1,0:T(8,128)S(1)} custom-call(s32[2]{0:T(128)S(1)} %copy-done.11, f32[8,256]{1,0:T(8,128)S(1)} %get-tuple-element.63.rows, f32[8,512,256]{2,1,0:T(8,128)S(1)} %get-tuple-element.64.hid, bf16[4,3,7,32,256]{4,3,2,1,0:T(8,128)(2,1)S(1)} %bitcast.18, bf16[4,3,7,32,256]{4,3,2,1,0:T(8,128)(2,1)S(1)} %collective-permute-done.6.wb), custom_call_target="tpu_custom_call" | custom-call | flops 8000000000 | bytes 24000000 | tf_op jit(solution)/shard_map/inner2/pallas_call | solution.py:941
  163.0 1.7 collective-permute-done.13.u1
  164.7 10.5 %collective-permute-done.14.u2 = bf16[56,32,128]{2,1,0:T(8,128)(2,1)S(1)} collective-permute-done((bf16[56,32,128]{2,1,0:T(8,128)(2,1)S(1)}, bf16[56,32,128]{2,1,0:T(8,128)(2,1)S(1)}, u32[]{:S(2)}, u32[]{:S(2)}) %collective-permute-start.14) | collective-permute-done | bytes 458784 | tf_op jit(solution)/shard_map/ppermute | solution.py:728
  175.3 3.9 %outer2.3 = (bf16[4,64,512]{2,1,0:T(8,128)(2,1)S(1)}, bf16[4,64,512]{2,1,0:T(8,128)(2,1)S(1)}, bf16[4,64,512]{2,1,0:T(8,128)(2,1)S(1)}, bf16[4,64,512]{2,1,0:T(8,128)(2,1)S(1)}) custom-call(s32[2]{0:T(128)S(1)} %copy-done.11, f32[8,512,256]{2,1,0:T(8,128)S(1)} %inner2.1.part, bf16[32,64,512]{2,1,0:T(8,128)(2,1)S(1)} %copy-done.1, ...), custom_call_target="tpu_custom_call" | custom-call | flops 5000000000 | bytes 15000000 | tf_op jit(solution)/shard_map/outer2/pallas_call | solution.py:959
  179.2 1.4 collective-permute-start.19
  180.6 0.8 collective-permute-start.20
  181.4 1.9 collective-permute-start.21
  183.3 3.9 %outer2.2 = (bf16[4,64,512]{2,1,0:T(8,128)(2,1)S(1)}, bf16[4,64,512]{2,1,0:T(8,128)(2,1)S(1)}, bf16[4,64,512]{2,1,0:T(8,128)(2,1)S(1)}, bf16[4,64,512]{2,1,0:T(8,128)(2,1)S(1)}) custom-call(s32[2]{0:T(128)S(1)} %copy-done.11, f32[8,512,256]{2,1,0:T(8,128)S(1)} %inner2.1.part, bf16[32,64,512]{2,1,0:T(8,128)(2,1)S(1)} %copy-done.1, ...), custom_call_target="tpu_custom_call" | custom-call | flops 5000000000 | bytes 15000000 | tf_op jit(solution)/shard_map/outer2/pallas_call | solution.py:959
  187.2 1.1 collective-permute-start.16
  188.3 0.9 collective-permute-start.17
  189.2 1.8 collective-permute-start.18
  191.0 4.5 %collective-permute-done.20.refs_6_ = bf16[4,64,512]{2,1,0:T(8,128)(2,1)S(1)} collective-permute-done((bf16[4,64,512]{2,1,0:T(8,128)(2,1)S(1)}, bf16[4,64,512]{2,1,0:T(8,128)(2,1)S(1)}, u32[]{:S(2)}, u32[]{:S(2)}) %collective-permute-start.20) | collective-permute-done | bytes 262176 | tf_op jit(solution)/shard_map/ppermute | solution.py:728
  195.4 4.1 %collective-permute-done.16.refs_1_ = bf16[4,64,512]{2,1,0:T(8,128)(2,1)S(1)} collective-permute-done((bf16[4,64,512]{2,1,0:T(8,128)(2,1)S(1)}, bf16[4,64,512]{2,1,0:T(8,128)(2,1)S(1)}, u32[]{:S(2)}, u32[]{:S(2)}) %collective-permute-start.16) | collective-permute-done | bytes 262176 | tf_op jit(solution)/shard_map/ppermute | solution.py:728
  199.5 6.4 %collective-permute-done.17.refs_2_ = bf16[4,64,512]{2,1,0:T(8,128)(2,1)S(1)} collective-permute-done((bf16[4,64,512]{2,1,0:T(8,128)(2,1)S(1)}, bf16[4,64,512]{2,1,0:T(8,128)(2,1)S(1)}, u32[]{:S(2)}, u32[]{:S(2)}) %collective-permute-start.17) | collective-permute-done | bytes 262176 | tf_op jit(solution)/shard_map/ppermute | solution.py:728
  205.9 1.9 gather.1
  (56 shorter events, 0.2 us)
Async XLA Ops:
  6.5 1.1 copy-start
  6.5 49.9 %all-gather.3.cloned.1.call-start = ((), (), s32[]{:S(2)}) async-start(), calls=%async_computation.2 | async-start | bytes 1720320 | tf_op jit(solution)/shard_map/all_gather | solution.py:786
  11.0 27.9 %collective-permute-start.2 = (bf16[8,64,512]{2,1,0:T(8,128)(2,1)}, bf16[8,64,512]{2,1,0:T(8,128)(2,1)S(1)}, u32[]{:S(2)}, u32[]{:S(2)}) collective-permute-start(bf16[8,64,512]{2,1,0:T(8,128)(2,1)} %get-tuple-element.77), channel_id=1, source_target_pairs={{0,3},{1,0},{2,1},{3,2},{4,7},{5,4},{6,5},{7,6},{8,11},{9,8},{10,9... | collective-permute-start | bytes 1572872 | tf_op jit(solution)/shard_map/ppermute | solution.py:728
  14.6 24.3 %collective-permute-start.1 = (bf16[8,64,512]{2,1,0:T(8,128)(2,1)}, bf16[8,64,512]{2,1,0:T(8,128)(2,1)S(1)}, u32[]{:S(2)}, u32[]{:S(2)}) collective-permute-start(bf16[8,64,512]{2,1,0:T(8,128)(2,1)} %get-tuple-element.78), channel_id=1, source_target_pairs={{0,1},{1,2},{2,3},{3,0},{4,5},{5,6},{6,7},{7,4},{8,9},{9,10},{10,1... | collective-permute-start | bytes 1572872 | tf_op jit(solution)/shard_map/ppermute | solution.py:728
  14.6 35.2 %collective-permute-start = (bf16[8,64,512]{2,1,0:T(8,128)(2,1)S(1)}, bf16[8,64,512]{2,1,0:T(8,128)(2,1)S(1)}, u32[]{:S(2)}, u32[]{:S(2)}) collective-permute-start(bf16[8,64,512]{2,1,0:T(8,128)(2,1)S(1)} %get-tuple-element.79), channel_id=1, source_target_pairs={{0,2},{1,3},{2,0},{3,1},{4,6},{5,7},{6,4},{7,5},{8,10},{9,11},{10,... | collective-permute-start | bytes 1572872 | tf_op jit(solution)/shard_map/ppermute | solution.py:728
  23.9 9.7 %copy-start.19 = (s32[32,6]{0,1:T(8,128)S(1)}, s32[32,6]{0,1:T(8,128)}, u32[]{:S(2)}) copy-start(s32[32,6]{0,1:T(8,128)} %param.15) | copy-start | bytes 2308
  23.9 9.7 %copy-start.20 = (s32[1,32,2]{1,2,0:T(2,128)S(1)}, s32[1,32,2]{1,2,0:T(2,128)}, u32[]{:S(2)}) copy-start(s32[1,32,2]{1,2,0:T(2,128)} %param.17) | copy-start | bytes 772
  23.9 9.7 %copy-start.21 = (s32[1,32,2]{1,2,0:T(2,128)S(1)}, s32[1,32,2]{1,2,0:T(2,128)}, u32[]{:S(2)}) copy-start(s32[1,32,2]{1,2,0:T(2,128)} %param.16) | copy-start | bytes 772
  23.9 9.7 %copy-start.22 = (s32[1,32,2]{1,2,0:T(2,128)S(1)}, s32[1,32,2]{1,2,0:T(2,128)}, u32[]{:S(2)}) copy-start(s32[1,32,2]{1,2,0:T(2,128)} %param.18) | copy-start | bytes 772
  23.9 27.4 %all-to-all-start = ((bf16[32,144,128]{2,1,0:T(8,128)(2,1)}), bf16[32,144,128]{2,1,0:T(8,128)(2,1)}, u32[]{:S(2)}, u32[]{:S(2)}) async-start(bf16[32,144,128]{2,1,0:T(8,128)(2,1)} %get-tuple-element.45), calls=%async_computation | async-start | bytes 2359296 | tf_op jit(solution)/shard_map/all_to_all | solution.py:734
  33.6 3.9 %copy-start.23 = (f32[3,64]{1,0:T(4,128)S(1)}, f32[3,64]{1,0:T(4,128)}, u32[]{:S(2)}) copy-start(f32[3,64]{1,0:T(4,128)} %param.13) | copy-start | bytes 2308
  33.6 3.9 %copy-start.24 = (f32[3,64]{1,0:T(4,128)S(1)}, f32[3,64]{1,0:T(4,128)}, u32[]{:S(2)}) copy-start(f32[3,64]{1,0:T(4,128)} %param.12) | copy-start | bytes 2308
  33.6 3.9 %copy-start.25 = (f32[64]{0:T(128)S(1)}, f32[64]{0:T(128)}, u32[]{:S(2)}) copy-start(f32[64]{0:T(128)} %param.14) | copy-start | bytes 772
  36.3 0.6 copy-start.12
  36.9 0.6 copy-start.14
  38.9 12.4 %copy-start.2 = (bf16[8,64,512]{2,1,0:T(8,128)(2,1)}, bf16[8,64,512]{2,1,0:T(8,128)(2,1)S(1)}, u32[]{:S(2)}) copy-start(bf16[8,64,512]{2,1,0:T(8,128)(2,1)S(1)} %collective-permute-done.2.x3.v3) | copy-start | bytes 1572868
  38.9 12.4 %copy-start.5 = (bf16[8,64,512]{2,1,0:T(8,128)(2,1)}, bf16[8,64,512]{2,1,0:T(8,128)(2,1)S(1)}, u32[]{:S(2)}) copy-start(bf16[8,64,512]{2,1,0:T(8,128)(2,1)S(1)} %collective-permute-done.1.x2.v2) | copy-start | bytes 1572868
  49.7 1.6 copy-start.8
  51.3 17.6 %copy-start.1 = (bf16[32,64,512]{2,1,0:T(8,128)(2,1)S(1)}, bf16[32,64,512]{2,1,0:T(8,128)(2,1)}, u32[]{:S(2)}) copy-start(bf16[32,64,512]{2,1,0:T(8,128)(2,1)} %v0.5) | copy-start | bytes 6291460
  51.3 17.6 %copy-start.11 = (s32[2]{0:T(128)S(1)}, s32[2]{0:T(128)}, u32[]{:S(2)}) copy-start(s32[2]{0:T(128)} %pad_add_fusion.me) | copy-start | bytes 28
  56.4 12.4 %collective-permute-start.6 = (bf16[4,3,7,32,256]{4,3,2,1,0:T(8,128)(2,1)}, bf16[4,3,7,32,256]{4,3,2,1,0:T(8,128)(2,1)S(1)}, u32[]{:S(2)}, u32[]{:S(2)}) collective-permute-start(bf16[4,3,7,32,256]{4,3,2,1,0:T(8,128)(2,1)} %bitcast.14), channel_id=1, source_target_pairs={{0,4},{4,0},{8,12},{12,8},{16,20},{20,16},{24,28},{28,24},{32,36},... | collective-permute-start | bytes 4128776 | tf_op jit(solution)/shard_map/ppermute | solution.py:830
  58.1 6.9 %collective-permute-start.3 = (bf16[17,32,128]{2,1,0:T(8,128)(2,1)}, bf16[17,32,128]{2,1,0:T(8,128)(2,1)S(1)}, u32[]{:S(2)}, u32[]{:S(2)}) collective-permute-start(bf16[17,32,128]{2,1,0:T(8,128)(2,1)} %get-tuple-element.47), channel_id=1, source_target_pairs={{3,1},{2,0},{1,3},{0,2},{7,5},{6,4},{5,7},{4,6},{11,9},{10,8},{9,1... | collective-permute-start | bytes 417800 | tf_op jit(solution)/shard_map/ppermute | solution.py:728
  59.2 9.7 %collective-permute-start.4 = (bf16[17,32,128]{2,1,0:T(8,128)(2,1)}, bf16[17,32,128]{2,1,0:T(8,128)(2,1)S(1)}, u32[]{:S(2)}, u32[]{:S(2)}) collective-permute-start(bf16[17,32,128]{2,1,0:T(8,128)(2,1)} %get-tuple-element.48), channel_id=1, source_target_pairs={{3,0},{2,3},{1,2},{0,1},{7,4},{6,7},{5,6},{4,5},{11,8},{10,11},{9,... | collective-permute-start | bytes 417800 | tf_op jit(solution)/shard_map/ppermute | solution.py:728
  59.7 9.2 %collective-permute-start.5 = (bf16[17,32,128]{2,1,0:T(8,128)(2,1)}, bf16[17,32,128]{2,1,0:T(8,128)(2,1)S(1)}, u32[]{:S(2)}, u32[]{:S(2)}) collective-permute-start(bf16[17,32,128]{2,1,0:T(8,128)(2,1)} %get-tuple-element.49), channel_id=1, source_target_pairs={{3,2},{2,1},{1,0},{0,3},{7,6},{6,5},{5,4},{4,7},{11,10},{10,9},{9,... | collective-permute-start | bytes 417800 | tf_op jit(solution)/shard_map/ppermute | solution.py:728
  62.1 23.6 %collective-permute-start.7 = (bf16[48,32,128]{2,1,0:T(8,128)(2,1)}, bf16[48,32,128]{2,1,0:T(8,128)(2,1)S(1)}, u32[]{:S(2)}, u32[]{:S(2)}) collective-permute-start(bf16[48,32,128]{2,1,0:T(8,128)(2,1)} %get-tuple-element.54), channel_id=1, source_target_pairs={{0,2},{1,3},{2,0},{3,1},{4,6},{5,7},{6,4},{7,5},{8,10},{9,11},{10,... | collective-permute-start | bytes 1179656 | tf_op jit(solution)/shard_map/ppermute | solution.py:728
  65.0 20.7 %collective-permute-start.8 = (bf16[48,32,128]{2,1,0:T(8,128)(2,1)}, bf16[48,32,128]{2,1,0:T(8,128)(2,1)S(1)}, u32[]{:S(2)}, u32[]{:S(2)}) collective-permute-start(bf16[48,32,128]{2,1,0:T(8,128)(2,1)} %get-tuple-element.55), channel_id=1, source_target_pairs={{0,1},{1,2},{2,3},{3,0},{4,5},{5,6},{6,7},{7,4},{8,9},{9,10},{10,1... | collective-permute-start | bytes 1179656 | tf_op jit(solution)/shard_map/ppermute | solution.py:728
  68.9 16.8 %collective-permute-start.9 = (bf16[48,32,128]{2,1,0:T(8,128)(2,1)}, bf16[48,32,128]{2,1,0:T(8,128)(2,1)S(1)}, u32[]{:S(2)}, u32[]{:S(2)}) collective-permute-start(bf16[48,32,128]{2,1,0:T(8,128)(2,1)} %get-tuple-element.56), channel_id=1, source_target_pairs={{0,3},{1,0},{2,1},{3,2},{4,7},{5,4},{6,5},{7,6},{8,11},{9,8},{10,9... | collective-permute-start | bytes 1179656 | tf_op jit(solution)/shard_map/ppermute | solution.py:728
  68.9 1.0 copy-start.3
  69.9 1.0 copy-start.6
  71.0 1.0 copy-start.9
  72.0 1.3 copy-start.15
  73.4 0.9 copy-start.18
  81.3 4.4 %copy-start.16 = (bf16[12,7,32,256]{3,2,1,0:T(8,128)(2,1)S(1)}, bf16[12,7,32,256]{3,2,1,0:T(8,128)(2,1)}, u32[]{:S(2)}) copy-start(bf16[12,7,32,256]{3,2,1,0:T(8,128)(2,1)} %all-gather.3.cloned.1.call-done) | copy-start | bytes 4128772
  81.3 4.4 %copy-start.17 = (bf16[48,32,128]{2,1,0:T(8,128)(2,1)S(1)}, bf16[48,32,128]{2,1,0:T(8,128)(2,1)}, u32[]{:S(2)}) copy-start(bf16[48,32,128]{2,1,0:T(8,128)(2,1)} %get-tuple-element.53.u0) | copy-start | bytes 1179652
  90.9 14.2 %collective-permute-start.10 = (bf16[65,32,128]{2,1,0:T(8,128)(2,1)S(1)}, bf16[65,32,128]{2,1,0:T(8,128)(2,1)S(1)}, u32[]{:S(2)}, u32[]{:S(2)}) collective-permute-start(bf16[65,32,128]{2,1,0:T(8,128)(2,1)S(1)} %get-tuple-element.58), channel_id=1, source_target_pairs={{0,2},{1,3},{2,0},{3,1},{4,6},{5,7},{6,4},{7,5},{8,10},{9,11},{10,... | collective-permute-start | bytes 1597448 | tf_op jit(solution)/shard_map/ppermute | solution.py:728
  92.4 25.5 %collective-permute-start.11 = (bf16[65,32,128]{2,1,0:T(8,128)(2,1)S(1)}, bf16[65,32,128]{2,1,0:T(8,128)(2,1)S(1)}, u32[]{:S(2)}, u32[]{:S(2)}) collective-permute-start(bf16[65,32,128]{2,1,0:T(8,128)(2,1)S(1)} %get-tuple-element.59), channel_id=1, source_target_pairs={{0,1},{1,2},{2,3},{3,0},{4,5},{5,6},{6,7},{7,4},{8,9},{9,10},{10,1... | collective-permute-start | bytes 1597448 | tf_op jit(solution)/shard_map/ppermute | solution.py:728
  92.8 25.1 %collective-permute-start.12 = (bf16[65,32,128]{2,1,0:T(8,128)(2,1)S(1)}, bf16[65,32,128]{2,1,0:T(8,128)(2,1)S(1)}, u32[]{:S(2)}, u32[]{:S(2)}) collective-permute-start(bf16[65,32,128]{2,1,0:T(8,128)(2,1)S(1)} %get-tuple-element.60), channel_id=1, source_target_pairs={{0,3},{1,0},{2,1},{3,2},{4,7},{5,4},{6,5},{7,6},{8,11},{9,8},{10,9... | collective-permute-start | bytes 1597448 | tf_op jit(solution)/shard_map/ppermute | solution.py:728
  119.8 26.8 %copy-start.13 = (s32[192]{0:T(256)S(1)}, s32[192]{0:T(256)}, u32[]{:S(2)}) copy-start(s32[192]{0:T(256)} %copy-done.12) | copy-start | bytes 2308
  151.4 13.3 %collective-permute-start.13 = (bf16[56,32,128]{2,1,0:T(8,128)(2,1)S(1)}, bf16[56,32,128]{2,1,0:T(8,128)(2,1)S(1)}, u32[]{:S(2)}, u32[]{:S(2)}) collective-permute-start(bf16[56,32,128]{2,1,0:T(8,128)(2,1)S(1)} %get-tuple-element.66), channel_id=1, source_target_pairs={{0,2},{1,3},{2,0},{3,1},{4,6},{5,7},{6,4},{7,5},{8,10},{9,11},{10,... | collective-permute-start | bytes 1376264 | tf_op jit(solution)/shard_map/ppermute | solution.py:728
  153.6 21.7 %collective-permute-start.14 = (bf16[56,32,128]{2,1,0:T(8,128)(2,1)S(1)}, bf16[56,32,128]{2,1,0:T(8,128)(2,1)S(1)}, u32[]{:S(2)}, u32[]{:S(2)}) collective-permute-start(bf16[56,32,128]{2,1,0:T(8,128)(2,1)S(1)} %get-tuple-element.67), channel_id=1, source_target_pairs={{0,1},{1,2},{2,3},{3,0},{4,5},{5,6},{6,7},{7,4},{8,9},{9,10},{10,1... | collective-permute-start | bytes 1376264 | tf_op jit(solution)/shard_map/ppermute | solution.py:728
  153.6 21.7 %collective-permute-start.15 = (bf16[56,32,128]{2,1,0:T(8,128)(2,1)S(1)}, bf16[56,32,128]{2,1,0:T(8,128)(2,1)S(1)}, u32[]{:S(2)}, u32[]{:S(2)}) collective-permute-start(bf16[56,32,128]{2,1,0:T(8,128)(2,1)S(1)} %get-tuple-element.68), channel_id=1, source_target_pairs={{0,3},{1,0},{2,1},{3,2},{4,7},{5,4},{6,5},{7,6},{8,11},{9,8},{10,9... | collective-permute-start | bytes 1376264 | tf_op jit(solution)/shard_map/ppermute | solution.py:728
  156.2 19.0 %copy-start.4 = (bf16[8,64,512]{2,1,0:T(8,128)(2,1)S(1)}, bf16[8,64,512]{2,1,0:T(8,128)(2,1)}, u32[]{:S(2)}) copy-start(bf16[8,64,512]{2,1,0:T(8,128)(2,1)} %copy-done.2) | copy-start | bytes 1572868
  156.2 19.0 %copy-start.7 = (bf16[8,64,512]{2,1,0:T(8,128)(2,1)S(1)}, bf16[8,64,512]{2,1,0:T(8,128)(2,1)}, u32[]{:S(2)}) copy-start(bf16[8,64,512]{2,1,0:T(8,128)(2,1)} %copy-done.5) | copy-start | bytes 1572868
  156.2 19.0 %copy-start.10 = (bf16[8,64,512]{2,1,0:T(8,128)(2,1)S(1)}, bf16[8,64,512]{2,1,0:T(8,128)(2,1)}, u32[]{:S(2)}) copy-start(bf16[8,64,512]{2,1,0:T(8,128)(2,1)} %copy-done.8) | copy-start | bytes 1572868
  179.2 9.9 %collective-permute-start.19 = (bf16[4,64,512]{2,1,0:T(8,128)(2,1)S(1)}, bf16[4,64,512]{2,1,0:T(8,128)(2,1)S(1)}, u32[]{:S(2)}, u32[]{:S(2)}) collective-permute-start(bf16[4,64,512]{2,1,0:T(8,128)(2,1)S(1)} %get-tuple-element.74), channel_id=1, source_target_pairs={{3,1},{2,0},{1,3},{0,2},{7,5},{6,4},{5,7},{4,6},{11,9},{10,8},{9,1... | collective-permute-start | bytes 786440 | tf_op jit(solution)/shard_map/ppermute | solution.py:728
  180.6 14.8 %collective-permute-start.20 = (bf16[4,64,512]{2,1,0:T(8,128)(2,1)S(1)}, bf16[4,64,512]{2,1,0:T(8,128)(2,1)S(1)}, u32[]{:S(2)}, u32[]{:S(2)}) collective-permute-start(bf16[4,64,512]{2,1,0:T(8,128)(2,1)S(1)} %get-tuple-element.75), channel_id=1, source_target_pairs={{3,0},{2,3},{1,2},{0,1},{7,4},{6,7},{5,6},{4,5},{11,8},{10,11},{9,... | collective-permute-start | bytes 786440 | tf_op jit(solution)/shard_map/ppermute | solution.py:728
  181.4 14.1 %collective-permute-start.21 = (bf16[4,64,512]{2,1,0:T(8,128)(2,1)S(1)}, bf16[4,64,512]{2,1,0:T(8,128)(2,1)S(1)}, u32[]{:S(2)}, u32[]{:S(2)}) collective-permute-start(bf16[4,64,512]{2,1,0:T(8,128)(2,1)S(1)} %get-tuple-element.76), channel_id=1, source_target_pairs={{3,2},{2,1},{1,0},{0,3},{7,6},{6,5},{5,4},{4,7},{11,10},{10,9},{9,... | collective-permute-start | bytes 786440 | tf_op jit(solution)/shard_map/ppermute | solution.py:728
  187.2 12.3 %collective-permute-start.16 = (bf16[4,64,512]{2,1,0:T(8,128)(2,1)S(1)}, bf16[4,64,512]{2,1,0:T(8,128)(2,1)S(1)}, u32[]{:S(2)}, u32[]{:S(2)}) collective-permute-start(bf16[4,64,512]{2,1,0:T(8,128)(2,1)S(1)} %get-tuple-element.70), channel_id=1, source_target_pairs={{0,2},{1,3},{2,0},{3,1},{4,6},{5,7},{6,4},{7,5},{8,10},{9,11},{10,... | collective-permute-start | bytes 786440 | tf_op jit(solution)/shard_map/ppermute | solution.py:728
  188.3 17.6 %collective-permute-start.17 = (bf16[4,64,512]{2,1,0:T(8,128)(2,1)S(1)}, bf16[4,64,512]{2,1,0:T(8,128)(2,1)S(1)}, u32[]{:S(2)}, u32[]{:S(2)}) collective-permute-start(bf16[4,64,512]{2,1,0:T(8,128)(2,1)S(1)} %get-tuple-element.71), channel_id=1, source_target_pairs={{0,1},{1,2},{2,3},{3,0},{4,5},{5,6},{6,7},{7,4},{8,9},{9,10},{10,1... | collective-permute-start | bytes 786440 | tf_op jit(solution)/shard_map/ppermute | solution.py:728
  189.2 16.7 %collective-permute-start.18 = (bf16[4,64,512]{2,1,0:T(8,128)(2,1)S(1)}, bf16[4,64,512]{2,1,0:T(8,128)(2,1)S(1)}, u32[]{:S(2)}, u32[]{:S(2)}) collective-permute-start(bf16[4,64,512]{2,1,0:T(8,128)(2,1)S(1)} %get-tuple-element.72), channel_id=1, source_target_pairs={{0,3},{1,0},{2,1},{3,2},{4,7},{5,4},{6,5},{7,6},{8,11},{9,8},{10,9... | collective-permute-start | bytes 786440 | tf_op jit(solution)/shard_map/ppermute | solution.py:728
Sparse Core Ops, SparseCore 0:
  9.0 43.5 all-gather.2

commit v4 on v3

--- a/solution.py
+++ b/solution.py
@@ -131,10 +131,13 @@
 
 
 def extract_kernel(
-    links, csend, feats, table, faces, out,
-    slots, codes, held, pooled, stat, send_buf, sem, load,
+    links, csend, me, feats, table, kernels, faces, out, half,
+    slots, codes, held, pooled, stat, send_buf, cut, sem, load,
 ):
     left = lanes(32) < 64
+    at = pl.multiple_of(32 * me[1], 32)
+    cut_in = pltpu.make_async_copy(kernels.at[:, :, pl.ds(at, 32)], cut, load.at[9])
+    cut_out = pltpu.make_async_copy(cut, half, sem.at[9])
 
     def fetch(n):
         here = pl.ds(4 * n, 4)
@@ -149,6 +152,7 @@
     get_codes.start()
     for n in range(1, 8):
         fetch(n).start()
+    cut_in.start()
     get_codes.wait()
 
     def step(n, carry):
@@ -188,6 +192,8 @@
     zero = jnp.zeros((64, 128), F32)
     small = jnp.zeros((32, 128), F32)
     s, q, ps, pq = lax.fori_loop(0, 8, step, (zero, zero, small, small), unroll=2)
+    cut_in.wait()
+    cut_out.start()
     ones = jnp.ones((8, 128), F32)
     both = jnp.concatenate([s, q], axis=0)
     rows = lax.dot_general(ones, both, NT, precision=HIGH, preferred_element_type=F32)
@@ -214,14 +220,16 @@
     give.start()
     for n in range(8):
         keep(n).wait()
+    cut_out.wait()
     give.wait()
 
 
-def plan_kernel(nbr, links, csend, crecv, sel, tsel, ssel):
+def plan_kernel(nbr, links, csend, crecv, sel, tsel, ssel, owner, lslot):
     def slot_of(n, _):
         for f in range(6):
             near = nbr[f, n]
             sel[n * 6 + f] = jnp.where(near < SLOTS, near * 6 + (f ^ 1), FACES + 2 * DEVS)
+            owner[n * 6 + f] = jnp.where(near < SLOTS, near, SLOTS + 2 * DEVS)
         return 0
 
     lax.fori_loop(0, SLOTS, slot_of, 0)
@@ -235,10 +243,12 @@
     def mark(p, _):
         for k in range(2):
             code = links[k, p]
+            lslot[2 * p + k] = lax.div(jnp.minimum(code, FACES - 1), 6)
 
             @pl.when(code < FACES)
             def _():
                 sel[code] = FACES + 2 * p + k
+                owner[code] = SLOTS + 2 * p + k
 
             place = crecv[k, p]
 
@@ -363,14 +373,6 @@
                 dst[pl.ds(at, 32), 256 * t : 256 * t + 256] = part[c, which, t]
 
 
-def fill_tap_weights(dst, first, second, core, which):
-    for c in range(4):
-        for side, part in enumerate((first, second)):
-            at = pl.multiple_of(64 * c + 32 * (core ^ side), 32)
-            for f in range(6):
-                dst[f, pl.ds(at, 32), :] = part[c, which, 1 + f]
-
-
 def fill_cube(cube, volumes, y):
     for r, v in zip(ORDER, volumes):
         at = pl.multiple_of(((y - r) & 3) * 64, 64)
@@ -431,7 +433,12 @@
             ],
             axis=0,
         )
-        across[f] = lax.dot_general(layer, tap_weights[f], NT, preferred_element_type=F32)
+        across[f] = lax.dot_general(
+            layer,
+            tap_weights[:, 256 * (f + 1) : 256 * (f + 2)],
+            NT,
+            preferred_element_type=F32,
+        )
 
 
 def add_borders(h, across, step, shift):
@@ -460,12 +467,11 @@
 
 
 def outer1_kernel(
-    me, rows, part, u0, u1, u2, u3, tiles, wa, wb,
+    me, rows, part, u0, u1, u2, u3, tiles, weights,
     hid, o0, o1, o2, o3,
-    units, outs, weights, across, shift, stat, cells, sem,
+    units, outs, across, shift, stat, cells, sem,
 ):
     y = me[0]
-    fill_tap_weights(weights, wa, wb, me[1], 0)
     border_terms(units, weights, (u0, u1, u2, u3), y, across, 0, QUART)
     stat[...] = jnp.zeros((4, 32, 128), F32)
 
@@ -559,7 +565,7 @@
 
 
 def route2_kernel(
-    links, crecv, me, v0, v1, v2, v3, keep, out, held, cen, stat, send_buf, sem
+    links, lslot, crecv, me, v0, v1, v2, v3, keep, out, held, cen, stat, send_buf, sem
 ):
     y = me[0]
     for r, v in zip(ORDER, (v0, v1, v2, v3)):
@@ -578,7 +584,7 @@
     def send(p, _):
         for k in range(2):
             code = jnp.minimum(links[k, p], FACES - 1)
-            slot = lax.div(code, 6)
+            slot = lslot[2 * p + k]
             q = slot >> 3
             send_buf[p, 32 * k : 32 * k + 32] = held[q, code - 48 * q]
             stat[k : k + 1, :] = cen[pl.ds(slot, 1), :]
@@ -603,7 +609,7 @@
 
 
 def border2_kernel(
-    sel, ssel, me, rows, held, recv, o0, o1, o2, o3, norm, src, cen, buf, sem, load
+    sel, ssel, owner, me, rows, held, recv, o0, o1, o2, o3, norm, src, cen, buf, sem, load
 ):
     y = me[0]
     fetches = []
@@ -651,8 +657,8 @@
         def face(i, _):
             for f in range(6):
                 at = sel[q * 48 + i * 6 + f]
-                owner = jnp.where(at < FACES, lax.div(at, 6), at - (FACES - SLOTS))
-                u = src[at].astype(F32) + (cen[pl.ds(owner, 1), :] - mean)
+                whose = owner[q * 48 + i * 6 + f]
+                u = src[at].astype(F32) + (cen[pl.ds(whose, 1), :] - mean)
                 v = silu(u * scale + bias)
                 buf[r, i * 6 + f] = (v * (at < FACES + 2 * DEVS).astype(F32)).astype(BF16)
             link = ssel[q * 8 + i]
@@ -668,14 +674,13 @@
 
 
 def outer2_kernel(
-    me, part, v0, v1, v2, v3, u0, u1, u2, u3, wa, wb,
+    me, part, v0, v1, v2, v3, u0, u1, u2, u3, weights,
     o0, o1, o2, o3,
-    units, weights, across, shift, cube, lift,
+    units, across, shift, cube, lift,
     *, start,
 ):
     y = me[0]
     lift[...] = placement(VOX, 64, coarse_code)
-    fill_tap_weights(weights, wa, wb, me[1], 1)
     border_terms(units, weights, (u0, u1, u2, u3), y, across, start, HALF)
 
     def slot(n, _):
@@ -763,13 +768,17 @@
         [norm_gain[0], norm_bias[0], norm_gain[2], norm_bias[2], time_bias]
         + [norm_gain[1], norm_bias[1]]
     )
-    faces, outgoing = call(
+    faces, outgoing, half = call(
         extract_kernel,
         "extract",
         60,
-        out_shape=(shape(FACES // 2, 64, 128), shape(DEVS, ROWS, 128)),
-        in_specs=[SMEM] * 2 + [HBM] * 2,
-        out_specs=(HBM,) * 2,
+        out_shape=(
+            shape(FACES // 2, 64, 128),
+            shape(DEVS, ROWS, 128),
+            shape(3, 7, 32, 256),
+        ),
+        in_specs=[SMEM] * 3 + [HBM] * 3,
+        out_specs=(HBM,) * 3,
         scratch_shapes=[
             pltpu.VMEM((SLOTS, 64, VOX), BF16),
             pltpu.VMEM((448, VOX), BF16),
@@ -777,13 +786,13 @@
             pltpu.VMEM((SLOTS, 32, 128), BF16),
             pltpu.VMEM((16, 128), F32),
             pltpu.VMEM((DEVS, ROWS, 128), BF16),
-            pltpu.SemaphoreType.DMA((9,)),
-            pltpu.SemaphoreType.DMA((9,)),
+            pltpu.VMEM((3, 7, 32, 256), BF16),
+            pltpu.SemaphoreType.DMA((10,)),
+            pltpu.SemaphoreType.DMA((10,)),
         ],
-    )(links, csend, feats, jnp.asarray(extract_np, BF16))
+    )(links, csend, me, feats, jnp.asarray(extract_np, BF16), conv_weights)
+    wa = lax.all_gather(half, "chan", axis=0, tiled=False)
     arrived = over_blocks(outgoing)
-    half = lax.dynamic_slice_in_dim(conv_weights, 32 * core, 32, axis=2)
-    wa = lax.all_gather(half, "chan", axis=0, tiled=False)
     volumes = exchange(
         [feats]
         + [
@@ -791,7 +800,7 @@
             for r in range(1, 4)
         ]
     )
-    sel, tsel, ssel = call(
+    sel, tsel, ssel, owner, lslot = call(
         plan_kernel,
         "plan",
         4,
@@ -800,9 +809,11 @@
             shape(FACES, dtype=jnp.int32),
             shape(CODES, dtype=jnp.int32),
             shape(SLOTS, dtype=jnp.int32),
+            shape(FACES, dtype=jnp.int32),
+            shape(2 * DEVS, dtype=jnp.int32),
         ),
         in_specs=[SMEM] * 4,
-        out_specs=(SMEM,) * 3,
+        out_specs=(SMEM,) * 5,
     )(nbr, links, csend, crecv)
 
     parts = call(
@@ -848,7 +859,7 @@
         return pl.BlockSpec((1, VOX, 256), lambda i, me: (start + i, 0, 0))
 
     last = pl.BlockSpec((1, 32, 128), lambda i, me: (16, 0, 0))
-    part1, rows = call(
+    part1, rows, weights = call(
         inner1_kernel,
         "inner1",
         24,
@@ -856,15 +867,18 @@
         grid_spec=prefetched(
             QUART,
             [last] * 4 + slot_specs(0) + [VMEM] * 2,
-            (cell_spec(0), VMEM),
+            (cell_spec(0), VMEM, VMEM),
             [
-                pltpu.VMEM((256, 1792), BF16),
                 pltpu.VMEM((4, 32, 128), F32),
                 pltpu.VMEM((VOX, 1792), BF16),
                 pltpu.VMEM((256, VOX), F32),
             ],
         ),
-        out_shape=(shape(QUART, VOX, 256, dtype=F32), shape(8, 256, dtype=F32)),
+        out_shape=(
+            shape(QUART, VOX, 256, dtype=F32),
+            shape(8, 256, dtype=F32),
+            shape(256, 1792),
+        ),
     )(me, *tiles1, *volumes, wa, wb)
     eight = pl.BlockSpec((8, 32, 128), lambda t: (t, 0, 0))
     coarse = call(
@@ -890,19 +904,18 @@
         32,
         5,
         out_shape=(shape(QUART, VOX, 256, dtype=F32),) + (shape(65, 32, 128),) * 4,
-        in_specs=[SMEM] + [VMEM] * 9,
+        in_specs=[SMEM] + [VMEM] * 8,
         out_specs=(HBM,) + (VMEM,) * 4,
         scratch_shapes=[
             pltpu.VMEM((4, 48, 32, 128), BF16),
             pltpu.VMEM((4, 49, 32, 128), BF16),
-            pltpu.VMEM((6, 256, 256), BF16),
             pltpu.VMEM((6, VOX, 256), F32),
             pltpu.VMEM((2, VOX, 128), F32),
             pltpu.VMEM((4, 32, 128), F32),
             pltpu.VMEM((QUART, VOX, 256), F32),
             pltpu.SemaphoreType.DMA((QUART,)),
         ],
-    )(me, rows, part1, *units1, coarse, wa, wb)
+    )(me, rows, part1, *units1, coarse, weights)
     units = exchange(parts)
 
     held, outgoing = call(
@@ -910,7 +923,7 @@
         "route2",
         12,
         out_shape=(shape(4, 65, 32, 128), shape(DEVS, ROWS, 128)),
-        in_specs=[SMEM] * 3 + [VMEM] * 4,
+        in_specs=[SMEM] * 4 + [VMEM] * 4,
         out_specs=(HBM, HBM),
         scratch_shapes=[
             pltpu.VMEM((4, 65, 32, 128), BF16),
@@ -919,7 +932,7 @@
             pltpu.VMEM((DEVS, ROWS, 128), BF16),
             pltpu.SemaphoreType.DMA((2,)),
         ],
-    )(links, crecv, me, *units)
+    )(links, lslot, crecv, me, *units)
     arrived = over_blocks(outgoing)
 
     *parts, norm = call(
@@ -927,7 +940,7 @@
         "border2",
         12,
         out_shape=(shape(56, 32, 128),) * 4 + (shape(8, 256, dtype=F32),),
-        in_specs=[SMEM] * 3 + [VMEM, HBM, VMEM],
+        in_specs=[SMEM] * 4 + [VMEM, HBM, VMEM],
         out_specs=(ANY,) * 4 + (VMEM,),
         scratch_shapes=[
             pltpu.VMEM((FACES + 2 * DEVS + 1, 32, 128), BF16),
@@ -936,19 +949,18 @@
             pltpu.SemaphoreType.DMA((4,)),
             pltpu.SemaphoreType.DMA((8,)),
         ],
-    )(sel, ssel, me, rows, held, arrived)
+    )(sel, ssel, owner, me, rows, held, arrived)
     units2 = exchange(parts)
-    part2 = call(
+    part2, weights = call(
         inner2_kernel,
         "inner2",
         24,
         8,
         grid=(QUART,),
-        out_shape=shape(QUART, VOX, 256, dtype=F32),
+        out_shape=(shape(QUART, VOX, 256, dtype=F32), shape(256, 1792)),
         in_specs=[SMEM, VMEM, HBM, VMEM, VMEM],
-        out_specs=cells,
+        out_specs=(cells, VMEM),
         scratch_shapes=[
-            pltpu.VMEM((256, 1792), BF16),
             pltpu.VMEM((VOX, 1792), BF16),
             pltpu.VMEM((QUART, VOX, 256), F32),
             pltpu.SemaphoreType.DMA((QUART,)),
@@ -961,18 +973,17 @@
             "outer2",
             32,
             5,
-            in_specs=[SMEM] + [VMEM] * 11,
+            in_specs=[SMEM] + [VMEM] * 10,
             out_specs=(VMEM,) * 4,
             scratch_shapes=[
                 pltpu.VMEM((4, 56, 32, 128), BF16),
-                pltpu.VMEM((6, 256, 256), BF16),
                 pltpu.VMEM((6, 64 * HALF, 256), F32),
                 pltpu.VMEM((2, VOX, 128), F32),
                 pltpu.VMEM((256, VOX), F32),
                 pltpu.VMEM((VOX, 64), BF16),
             ],
             out_shape=(shape(HALF, 64, VOX),) * 4,
-        )(me, part2, *volumes, *units2, wa, wb)
+        )(me, part2, *volumes, *units2, weights)
         pieces += exchange(parts, (0, 1, 2, 3) if start == 0 else (3, 2, 1, 0))
     return call(
         gather_kernel,

time: 215 us -> 210 us (0.977)
  blocking collectives: 26.8 us -> 22.3 us
    ppermute x21, waiting for transfers between devices: 64.8 us -> 53.4 us  [exchange(): lax.ppermute(parts[r], 'chan', [(i, (i + r) % 4) for i in order])]
    all_to_all x1, waiting for transfers between devices: 1.56 us -> 12.6 us  [over_blocks(): lax.all_to_all(units, 'blocks', split_axis=0, concat_axis=0, tiled=True)]
    all_to_all x1, blocking collectives: 26.8 us -> 22.3 us  [over_blocks(): lax.all_to_all(units, 'blocks', split_axis=0, concat_axis=0, tiled=True)]
  transfers between devices with their start and end apart: 24 -> 24, of which waited for: 11 -> 10; matrix products, arithmetic and copies ran while one was open for 2% -> 1% of each run, Pallas kernels for 17% -> 18%
where the time goes in v4:
time: 210 us; the launch traced here: 209 us
  waiting for transfers between devices  66 us (31%)
  Pallas kernels  55.3 us (26%)
  starting transfers between devices  40.5 us (19%)
  blocking collectives  22.3 us (11%)
  between operations  13.8 us (7%)
  local copies, waits for them, and re-layouts  10.2 us (5%)
    ppermute x21, waiting for transfers between devices, exchange(): lax.ppermute(parts[r], 'chan', [(i, (i + r) % 4) for i in order])  53.4 us
    ppermute x21, starting transfers between devices, exchange(): lax.ppermute(parts[r], 'chan', [(i, (i + r) % 4) for i in order])  29.4 us
    all_to_all x1, blocking collectives, over_blocks(): lax.all_to_all(units, 'blocks', split_axis=0, concat_axis=0, tiled=True)  22.3 us
    all_to_all x1, waiting for transfers between devices, over_blocks(): lax.all_to_all(units, 'blocks', split_axis=0, concat_axis=0, tiled=True)  12.6 us
    all_to_all x1, starting transfers between devices, over_blocks(): lax.all_to_all(units, 'blocks', split_axis=0, concat_axis=0, tiled=True)  9.46 us
    pallas_call x2, Pallas kernels, local(): call(functools.partial(outer2_kernel, start=start), 'outer2', 32, 5, in_s...  7.72 us
    pallas_call x1, Pallas kernels, local(): call(extract_kernel, 'extract', 60, out_shape=(shape(FACES // 2, 64, 128)...  7.67 us
    unnamed x52, local copies, waits for them, and re-layouts  7.58 us
  transfers between devices with their start and end apart: 24, of which 10 were waited for; matrix products, arithmetic and copies ran while one was open for 1% of the time, Pallas kernels for 18%

profile of v4, /device:TPU:1, one launch (start us, length us, event | category | flops | bytes accessed | tf_op | source)
XLA Modules:
  0.0 209.5 jit_solution(1906096892079244271)
XLA Ops:
  6.5 2.6 %constant_dynamic-slice_fusion = (bf16[8,64,512]{2,1,0:T(8,128)(2,1)}, bf16[8,64,512]{2,1,0:T(8,128)(2,1)}, bf16[8,64,512]{2,1,0:T(8,128)(2,1)}) fusion(bf16[32,64,512]{2,1,0:T(8,128)(2,1)} %v0.5, s32[]{:T(128)S(6)} %select_n.34, s32[]{:T(128)S(6)} %select_n.32, s32[]{:T(128)S(6)} %select_n.30), kind=kLoop, calls=%fused_computation.2 | loop fusion | bytes 3145740 | tf_op jit(solution)/shard_map/dynamic_slice | solution.py:799
  9.1 3.6 %collective-permute-start.2 = (bf16[8,64,512]{2,1,0:T(8,128)(2,1)}, bf16[8,64,512]{2,1,0:T(8,128)(2,1)S(1)}, u32[]{:S(2)}, u32[]{:S(2)}) collective-permute-start(bf16[8,64,512]{2,1,0:T(8,128)(2,1)} %get-tuple-element.89), channel_id=1, source_target_pairs={{0,3},{1,0},{2,1},{3,2},{4,7},{5,4},{6,5},{7,6},{8,11},{9,8},{10,9... | collective-permute-start | bytes 1572872 | tf_op jit(solution)/shard_map/ppermute | solution.py:733
  12.7 1.6 collective-permute-start
  14.3 0.7 pad_add_fusion.me
  15.0 7.7 %extract.1 = (bf16[96,64,128]{2,1,0:T(8,128)(2,1)}, bf16[32,144,128]{2,1,0:T(8,128)(2,1)}, bf16[3,7,32,256]{3,2,1,0:T(8,128)(2,1)}) custom-call(s32[2,32]{1,0:T(2,128)} %bitcast.21, s32[2,32]{1,0:T(2,128)} %bitcast.19, s32[2]{0:T(128)} %pad_add_fusion.me, bf16[32,64,512]{2,1,0:T(8,128)(2,1)} %v0.5, bf16[448,512]{1,0:T(8,128)(2,1)} %constant.51.clone.table, ...), custom_call_target="tpu_custom_call" | custom-call | flops 1000000000 | bytes 3000000 | tf_op jit(solution)/shard_map/extract/pallas_call | solution.py:771
  22.7 0.0 copy-start.18
  22.7 0.0 copy-start.19
  22.7 0.0 copy-start.20
  22.7 0.0 copy-start.21
  22.7 0.0 all-gather.3.cloned.1.call-update
  22.7 9.5 %all-to-all-start = ((bf16[32,144,128]{2,1,0:T(8,128)(2,1)}), bf16[32,144,128]{2,1,0:T(8,128)(2,1)S(1)}, u32[]{:S(2)}, u32[]{:S(2)}) async-start(bf16[32,144,128]{2,1,0:T(8,128)(2,1)} %get-tuple-element.52), calls=%async_computation | async-start | bytes 2359296 | tf_op jit(solution)/shard_map/all_to_all | solution.py:739
  32.2 0.0 copy-start.23
  32.2 0.0 copy-start.24
  32.3 0.0 copy-start.25
  32.3 3.1 %plan.1 = (s32[192]{0:T(256)S(1)}, s32[64]{0:T(128)S(1)}, s32[32]{0:T(128)S(1)}, s32[192]{0:T(256)S(1)}, s32[64]{0:T(128)S(1)}) custom-call(s32[6,32]{1,0:T(8,128)S(1)} %bitcast.18, s32[2,32]{1,0:T(2,128)S(1)} %bitcast.22, s32[2,32]{1,0:T(2,128)S(1)} %bitcast.20, s32[2,32]{1,0:T(2,128)S(1)} %bitcast.24), custom_call_target="tpu_custom_call" | custom-call | flops 20000000000 | bytes 60000000 | tf_op jit(solution)/shard_map/plan/pallas_call | solution.py:803
  35.4 0.6 copy-done.11
  35.9 0.5 copy-done.13
  36.5 0.7 select_maximum_fusion.par
  37.2 0.0 collective-permute-done.1.x2.v2
  37.2 12.6 %all-to-all-done.recv = bf16[32,144,128]{2,1,0:T(8,128)(2,1)S(1)} async-done(((bf16[32,144,128]{2,1,0:T(8,128)(2,1)}), bf16[32,144,128]{2,1,0:T(8,128)(2,1)S(1)}, u32[]{:S(2)}, u32[]{:S(2)}) %all-to-all-start) | async-done | bytes 1179680 | tf_op jit(solution)/shard_map/all_to_all | solution.py:739
  49.9 1.0 copy-done.22
  50.9 5.1 %border1.1 = (bf16[17,32,128]{2,1,0:T(8,128)(2,1)}, bf16[17,32,128]{2,1,0:T(8,128)(2,1)}, bf16[17,32,128]{2,1,0:T(8,128)(2,1)}, bf16[17,32,128]{2,1,0:T(8,128)(2...) custom-call(s32[192]{0:T(256)} %copy-done.11, ...), custom_call_target="tpu_custom_call" | custom-call | flops 1000000000 | bytes 3000000 | tf_op jit(solution)/shard_map/border1/pallas_call | solution.py:819
  56.0 0.0 all-gather.3.cloned.1.call-done
  56.1 1.6 collective-permute-start.6
  57.7 1.1 collective-permute-start.3
  58.8 0.5 collective-permute-start.4
  59.3 2.4 %collective-permute-start.5 = (bf16[17,32,128]{2,1,0:T(8,128)(2,1)}, bf16[17,32,128]{2,1,0:T(8,128)(2,1)S(1)}, u32[]{:S(2)}, u32[]{:S(2)}) collective-permute-start(bf16[17,32,128]{2,1,0:T(8,128)(2,1)} %get-tuple-element.56), channel_id=1, source_target_pairs={{3,2},{2,1},{1,0},{0,3},{7,6},{6,5},{5,4},{4,7},{11,10},{10,9},{9,... | collective-permute-start | bytes 417800 | tf_op jit(solution)/shard_map/ppermute | solution.py:733
  61.7 1.2 collective-permute-start.7
  62.9 1.7 collective-permute-done.3.t1.u1
  64.6 1.6 collective-permute-start.8
  66.3 2.2 %collective-permute-done.4.t2.u2 = bf16[17,32,128]{2,1,0:T(8,128)(2,1)S(1)} collective-permute-done((bf16[17,32,128]{2,1,0:T(8,128)(2,1)}, bf16[17,32,128]{2,1,0:T(8,128)(2,1)S(1)}, u32[]{:S(2)}, u32[]{:S(2)}) %collective-permute-start.4) | collective-permute-done | bytes 139296 | tf_op jit(solution)/shard_map/ppermute | solution.py:733
  68.5 1.0 copy-done.2
  69.6 1.0 copy-done.5
  70.6 1.0 copy-done.8
  71.6 1.3 copy-done.14
  73.0 0.9 copy-done.17
  73.9 7.1 %inner1.1 = (f32[8,512,256]{2,1,0:T(8,128)S(1)}, f32[8,256]{1,0:T(8,128)S(1)}, bf16[256,1792]{1,0:T(8,128)(2,1)S(1)}) custom-call(s32[2]{0:T(128)S(1)} %copy-done.10, bf16[17,32,128]{2,1,0:T(8,128)(2,1)S(1)} %copy-done.17, bf16[17,32,128]{2,1,0:T(8,128)(2,1)S(1)} %collective-permute-done.3.t1.u1, bf16[17,32,128]{2,1,0:T(8,128)(2,1)S(1)} %collective-permute-done.4.t2.u2, ...), custom_call_target="tpu_custom_call" | custom-call | flops 8000000000 | bytes 24000000 | tf_op jit(solution)/shard_map/inner1/pallas_call | solution.py:862
  81.0 4.3 %tiles.1 = bf16[4,16,32,128]{3,2,1,0:T(8,128)(2,1)S(1)} custom-call(s32[2]{0:T(128)S(1)} %copy-done.10, bf16[17,32,128]{2,1,0:T(8,128)(2,1)S(1)} %copy-done.17, bf16[17,32,128]{2,1,0:T(8,128)(2,1)S(1)} %collective-permute-done.3.t1.u1, bf16[17,32,128]{2,1,0:T(8,128)(2,1)S(1)} %collective-permute-done.4.t2.u2, ...), custom_call_target="tpu_custom_call" | custom-call | flops 4000000000 | bytes 12000000 | tf_op jit(solution)/shard_map/tiles/pallas_call | solution.py:884
  85.4 5.1 %outer1.1 = (f32[8,512,256]{2,1,0:T(8,128)S(1)}, bf16[65,32,128]{2,1,0:T(8,128)(2,1)S(1)}, bf16[65,32,128]{2,1,0:T(8,128)(2,1)S(1)}, bf16[65,32,128]{2,1,0:T(8,128)(2,1)S(1)}, bf16[65,32,128]{2,1,0:T(8,128)(2,1)S(1)}) custom-call(s32[2]{0:T(128)S(1)} %copy-done.10, f32[8,256]{1,0:T(8,128)S(1)} %get-tuple-element.59.rows, ...), custom_call_target="tpu_custom_call" | custom-call | flops 5000000000 | bytes 15000000 | tf_op jit(solution)/shard_map/outer1/pallas_call | solution.py:901
  90.5 1.5 collective-permute-start.10
  92.0 0.4 collective-permute-start.11
  92.4 2.3 %collective-permute-start.12 = (bf16[65,32,128]{2,1,0:T(8,128)(2,1)S(1)}, bf16[65,32,128]{2,1,0:T(8,128)(2,1)S(1)}, u32[]{:S(2)}, u32[]{:S(2)}) collective-permute-start(bf16[65,32,128]{2,1,0:T(8,128)(2,1)S(1)} %get-tuple-element.70), channel_id=1, source_target_pairs={{0,3},{1,0},{2,1},{3,2},{4,7},{5,4},{6,5},{7,6},{8,11},{9,8},{10,9... | collective-permute-start | bytes 1597448 | tf_op jit(solution)/shard_map/ppermute | solution.py:733
  94.7 10.1 %collective-permute-done.10.v1 = bf16[65,32,128]{2,1,0:T(8,128)(2,1)S(1)} collective-permute-done((bf16[65,32,128]{2,1,0:T(8,128)(2,1)S(1)}, bf16[65,32,128]{2,1,0:T(8,128)(2,1)S(1)}, u32[]{:S(2)}, u32[]{:S(2)}) %collective-permute-start.10) | collective-permute-done | bytes 532512 | tf_op jit(solution)/shard_map/ppermute | solution.py:733
  104.8 12.7 %collective-permute-done.11.v2 = bf16[65,32,128]{2,1,0:T(8,128)(2,1)S(1)} collective-permute-done((bf16[65,32,128]{2,1,0:T(8,128)(2,1)S(1)}, bf16[65,32,128]{2,1,0:T(8,128)(2,1)S(1)}, u32[]{:S(2)}, u32[]{:S(2)}) %collective-permute-start.11) | collective-permute-done | bytes 532512 | tf_op jit(solution)/shard_map/ppermute | solution.py:733
  117.5 1.7 route2.1
  119.3 22.3 %all_to_all.10.recv = bf16[32,144,128]{2,1,0:T(8,128)(2,1)S(1)} all-to-all(bf16[32,144,128]{2,1,0:T(8,128)(2,1)S(1)} %get-tuple-element.72), channel_id=1, replica_groups=mesh['blocks'=32,'chan'=4] {'blocks'}, dimensions={0} | all-to-all | bytes 2359296 | tf_op jit(solution)/shard_map/all_to_all | solution.py:739
  141.6 4.6 %border2.1 = (bf16[56,32,128]{2,1,0:T(8,128)(2,1)S(1)}, bf16[56,32,128]{2,1,0:T(8,128)(2,1)S(1)}, bf16[56,32,128]{2,1,0:T(8,128)(2,1)S(1)}, bf16[56,32,128]{2,1,0:T(8,128)(2,1)S(1)}, f32[8,256]{1,0:T(8,128)S(1)}) custom-call(s32[192]{0:T(256)S(1)} %copy-done.12, s32[32]{0:T(128)S(1)} %get-tuple-element.48.ssel, s32[192]{0:T(256)S(1)} %get-tuple-element.49.owner, ...), custom_call_target="tpu_custom_call" | custom-call | flops 1000000000 | bytes 3000000 | tf_op jit(solution)/shard_map/border2/pallas_call | solution.py:938
  146.3 2.4 %collective-permute-start.13 = (bf16[56,32,128]{2,1,0:T(8,128)(2,1)S(1)}, bf16[56,32,128]{2,1,0:T(8,128)(2,1)S(1)}, u32[]{:S(2)}, u32[]{:S(2)}) collective-permute-start(bf16[56,32,128]{2,1,0:T(8,128)(2,1)S(1)} %get-tuple-element.77), channel_id=1, source_target_pairs={{0,2},{1,3},{2,0},{3,1},{4,6},{5,7},{6,4},{7,5},{8,10},{9,11},{10,... | collective-permute-start | bytes 1376264 | tf_op jit(solution)/shard_map/ppermute | solution.py:733
  148.7 2.7 %collective-permute-start.15 = (bf16[56,32,128]{2,1,0:T(8,128)(2,1)S(1)}, bf16[56,32,128]{2,1,0:T(8,128)(2,1)S(1)}, u32[]{:S(2)}, u32[]{:S(2)}) collective-permute-start(bf16[56,32,128]{2,1,0:T(8,128)(2,1)S(1)} %get-tuple-element.79), channel_id=1, source_target_pairs={{0,3},{1,0},{2,1},{3,2},{4,7},{5,4},{6,5},{7,6},{8,11},{9,8},{10,9... | collective-permute-start | bytes 1376264 | tf_op jit(solution)/shard_map/ppermute | solution.py:733
  151.3 6.9 %inner2.1 = (f32[8,512,256]{2,1,0:T(8,128)S(1)}, bf16[256,1792]{1,0:T(8,128)(2,1)S(1)}) custom-call(s32[2]{0:T(128)S(1)} %copy-done.10, f32[8,256]{1,0:T(8,128)S(1)} %get-tuple-element.73.rows, f32[8,512,256]{2,1,0:T(8,128)S(1)} %get-tuple-element.74.hid, bf16[4,3,7,32,256]{4,3,2,1,0:T(8,128)(2,1)S(1)} %bitcast.17, ...), custom_call_target="tpu_custom_call" | custom-call | flops 8000000000 | bytes 24000000 | tf_op jit(solution)/shard_map/inner2/pallas_call | solution.py:954
  158.3 1.3 collective-permute-done.13.u1
  159.6 10.5 %collective-permute-done.14.u2 = bf16[56,32,128]{2,1,0:T(8,128)(2,1)S(1)} collective-permute-done((bf16[56,32,128]{2,1,0:T(8,128)(2,1)S(1)}, bf16[56,32,128]{2,1,0:T(8,128)(2,1)S(1)}, u32[]{:S(2)}, u32[]{:S(2)}) %collective-permute-start.14) | collective-permute-done | bytes 458784 | tf_op jit(solution)/shard_map/ppermute | solution.py:733
  170.1 3.9 %outer2.3 = (bf16[4,64,512]{2,1,0:T(8,128)(2,1)S(1)}, bf16[4,64,512]{2,1,0:T(8,128)(2,1)S(1)}, bf16[4,64,512]{2,1,0:T(8,128)(2,1)S(1)}, bf16[4,64,512]{2,1,0:T(8,128)(2,1)S(1)}) custom-call(s32[2]{0:T(128)S(1)} %copy-done.10, f32[8,512,256]{2,1,0:T(8,128)S(1)} %get-tuple-element.75.part, bf16[32,64,512]{2,1,0:T(8,128)(2,1)S(1)} %copy-done, ...), custom_call_target="tpu_custom_call" | custom-call | flops 5000000000 | bytes 15000000 | tf_op jit(solution)/shard_map/outer2/pallas_call | solution.py:971
  174.0 1.6 collective-permute-start.19
  175.7 0.4 collective-permute-start.20
  176.1 2.3 %collective-permute-start.21 = (bf16[4,64,512]{2,1,0:T(8,128)(2,1)S(1)}, bf16[4,64,512]{2,1,0:T(8,128)(2,1)S(1)}, u32[]{:S(2)}, u32[]{:S(2)}) collective-permute-start(bf16[4,64,512]{2,1,0:T(8,128)(2,1)S(1)} %get-tuple-element.88), channel_id=1, source_target_pairs={{3,2},{2,1},{1,0},{0,3},{7,6},{6,5},{5,4},{4,7},{11,10},{10,9},{9,... | collective-permute-start | bytes 786440 | tf_op jit(solution)/shard_map/ppermute | solution.py:733
  178.3 3.9 %outer2.2 = (bf16[4,64,512]{2,1,0:T(8,128)(2,1)S(1)}, bf16[4,64,512]{2,1,0:T(8,128)(2,1)S(1)}, bf16[4,64,512]{2,1,0:T(8,128)(2,1)S(1)}, bf16[4,64,512]{2,1,0:T(8,128)(2,1)S(1)}) custom-call(s32[2]{0:T(128)S(1)} %copy-done.10, f32[8,512,256]{2,1,0:T(8,128)S(1)} %get-tuple-element.75.part, bf16[32,64,512]{2,1,0:T(8,128)(2,1)S(1)} %copy-done, ...), custom_call_target="tpu_custom_call" | custom-call | flops 5000000000 | bytes 15000000 | tf_op jit(solution)/shard_map/outer2/pallas_call | solution.py:971
  182.2 1.1 collective-permute-start.16
  183.3 0.9 collective-permute-start.17
  184.1 1.8 collective-permute-start.18
  186.0 4.3 %collective-permute-done.20.refs_6_ = bf16[4,64,512]{2,1,0:T(8,128)(2,1)S(1)} collective-permute-done((bf16[4,64,512]{2,1,0:T(8,128)(2,1)S(1)}, bf16[4,64,512]{2,1,0:T(8,128)(2,1)S(1)}, u32[]{:S(2)}, u32[]{:S(2)}) %collective-permute-start.20) | collective-permute-done | bytes 262176 | tf_op jit(solution)/shard_map/ppermute | solution.py:733
  190.2 4.0 %collective-permute-done.16.refs_1_ = bf16[4,64,512]{2,1,0:T(8,128)(2,1)S(1)} collective-permute-done((bf16[4,64,512]{2,1,0:T(8,128)(2,1)S(1)}, bf16[4,64,512]{2,1,0:T(8,128)(2,1)S(1)}, u32[]{:S(2)}, u32[]{:S(2)}) %collective-permute-start.16) | collective-permute-done | bytes 262176 | tf_op jit(solution)/shard_map/ppermute | solution.py:733
  194.3 6.4 %collective-permute-done.17.refs_2_ = bf16[4,64,512]{2,1,0:T(8,128)(2,1)S(1)} collective-permute-done((bf16[4,64,512]{2,1,0:T(8,128)(2,1)S(1)}, bf16[4,64,512]{2,1,0:T(8,128)(2,1)S(1)}, u32[]{:S(2)}, u32[]{:S(2)}) %collective-permute-start.17) | collective-permute-done | bytes 262176 | tf_op jit(solution)/shard_map/ppermute | solution.py:733
  200.7 1.9 gather.1
  (55 shorter events, 0.1 us)
Async XLA Ops:
  6.5 49.5 %all-gather.3.cloned.1.call-start = ((), (), s32[]{:S(2)}) async-start(), calls=%async_computation.2 | async-start | bytes 1720320 | tf_op jit(solution)/shard_map/all_gather | solution.py:794
  9.1 28.1 %collective-permute-start.2 = (bf16[8,64,512]{2,1,0:T(8,128)(2,1)}, bf16[8,64,512]{2,1,0:T(8,128)(2,1)S(1)}, u32[]{:S(2)}, u32[]{:S(2)}) collective-permute-start(bf16[8,64,512]{2,1,0:T(8,128)(2,1)} %get-tuple-element.89), channel_id=1, source_target_pairs={{0,3},{1,0},{2,1},{3,2},{4,7},{5,4},{6,5},{7,6},{8,11},{9,8},{10,9... | collective-permute-start | bytes 1572872 | tf_op jit(solution)/shard_map/ppermute | solution.py:733
  12.7 24.5 %collective-permute-start.1 = (bf16[8,64,512]{2,1,0:T(8,128)(2,1)}, bf16[8,64,512]{2,1,0:T(8,128)(2,1)S(1)}, u32[]{:S(2)}, u32[]{:S(2)}) collective-permute-start(bf16[8,64,512]{2,1,0:T(8,128)(2,1)} %get-tuple-element.90), channel_id=1, source_target_pairs={{0,1},{1,2},{2,3},{3,0},{4,5},{5,6},{6,7},{7,4},{8,9},{9,10},{10,1... | collective-permute-start | bytes 1572872 | tf_op jit(solution)/shard_map/ppermute | solution.py:733
  12.7 24.5 %collective-permute-start = (bf16[8,64,512]{2,1,0:T(8,128)(2,1)}, bf16[8,64,512]{2,1,0:T(8,128)(2,1)S(1)}, u32[]{:S(2)}, u32[]{:S(2)}) collective-permute-start(bf16[8,64,512]{2,1,0:T(8,128)(2,1)} %get-tuple-element.91), channel_id=1, source_target_pairs={{0,2},{1,3},{2,0},{3,1},{4,6},{5,7},{6,4},{7,5},{8,10},{9,11},{10,... | collective-permute-start | bytes 1572872 | tf_op jit(solution)/shard_map/ppermute | solution.py:733
  22.7 9.5 %copy-start.18 = (s32[32,6]{0,1:T(8,128)S(1)}, s32[32,6]{0,1:T(8,128)}, u32[]{:S(2)}) copy-start(s32[32,6]{0,1:T(8,128)} %param.15) | copy-start | bytes 2308
  22.7 9.5 %copy-start.19 = (s32[1,32,2]{1,2,0:T(2,128)S(1)}, s32[1,32,2]{1,2,0:T(2,128)}, u32[]{:S(2)}) copy-start(s32[1,32,2]{1,2,0:T(2,128)} %param.17) | copy-start | bytes 772
  22.7 9.5 %copy-start.20 = (s32[1,32,2]{1,2,0:T(2,128)S(1)}, s32[1,32,2]{1,2,0:T(2,128)}, u32[]{:S(2)}) copy-start(s32[1,32,2]{1,2,0:T(2,128)} %param.16) | copy-start | bytes 772
  22.7 9.5 %copy-start.21 = (s32[1,32,2]{1,2,0:T(2,128)S(1)}, s32[1,32,2]{1,2,0:T(2,128)}, u32[]{:S(2)}) copy-start(s32[1,32,2]{1,2,0:T(2,128)} %param.18) | copy-start | bytes 772
  22.7 27.2 %all-to-all-start = ((bf16[32,144,128]{2,1,0:T(8,128)(2,1)}), bf16[32,144,128]{2,1,0:T(8,128)(2,1)S(1)}, u32[]{:S(2)}, u32[]{:S(2)}) async-start(bf16[32,144,128]{2,1,0:T(8,128)(2,1)} %get-tuple-element.52), calls=%async_computation | async-start | bytes 2359296 | tf_op jit(solution)/shard_map/all_to_all | solution.py:739
  32.2 4.2 %copy-start.23 = (f32[3,64]{1,0:T(4,128)S(1)}, f32[3,64]{1,0:T(4,128)}, u32[]{:S(2)}) copy-start(f32[3,64]{1,0:T(4,128)} %param.13) | copy-start | bytes 2308
  32.2 4.2 %copy-start.24 = (f32[3,64]{1,0:T(4,128)S(1)}, f32[3,64]{1,0:T(4,128)}, u32[]{:S(2)}) copy-start(f32[3,64]{1,0:T(4,128)} %param.12) | copy-start | bytes 2308
  32.3 4.2 %copy-start.25 = (f32[64]{0:T(128)S(1)}, f32[64]{0:T(128)}, u32[]{:S(2)}) copy-start(f32[64]{0:T(128)} %param.14) | copy-start | bytes 772
  35.4 0.6 copy-start.11
  35.9 0.5 copy-start.13
  37.2 13.7 %copy-start.1 = (bf16[8,64,512]{2,1,0:T(8,128)(2,1)}, bf16[8,64,512]{2,1,0:T(8,128)(2,1)S(1)}, u32[]{:S(2)}) copy-start(bf16[8,64,512]{2,1,0:T(8,128)(2,1)S(1)} %collective-permute-done.2.x3.v3) | copy-start | bytes 1572868
  37.2 13.7 %copy-start.4 = (bf16[8,64,512]{2,1,0:T(8,128)(2,1)}, bf16[8,64,512]{2,1,0:T(8,128)(2,1)S(1)}, u32[]{:S(2)}) copy-start(bf16[8,64,512]{2,1,0:T(8,128)(2,1)S(1)} %collective-permute-done.1.x2.v2) | copy-start | bytes 1572868
  37.2 12.7 %copy-start.7 = (bf16[8,64,512]{2,1,0:T(8,128)(2,1)}, bf16[8,64,512]{2,1,0:T(8,128)(2,1)S(1)}, u32[]{:S(2)}) copy-start(bf16[8,64,512]{2,1,0:T(8,128)(2,1)S(1)} %collective-permute-done.x1.v1) | copy-start | bytes 1572868
  49.9 1.0 copy-start.22
  50.9 17.6 %copy-start = (bf16[32,64,512]{2,1,0:T(8,128)(2,1)S(1)}, bf16[32,64,512]{2,1,0:T(8,128)(2,1)}, u32[]{:S(2)}) copy-start(bf16[32,64,512]{2,1,0:T(8,128)(2,1)} %v0.5) | copy-start | bytes 6291460
  50.9 17.6 %copy-start.10 = (s32[2]{0:T(128)S(1)}, s32[2]{0:T(128)}, u32[]{:S(2)}) copy-start(s32[2]{0:T(128)} %pad_add_fusion.me) | copy-start | bytes 28
  56.1 12.4 %collective-permute-start.6 = (bf16[4,3,7,32,256]{4,3,2,1,0:T(8,128)(2,1)}, bf16[4,3,7,32,256]{4,3,2,1,0:T(8,128)(2,1)S(1)}, u32[]{:S(2)}, u32[]{:S(2)}) collective-permute-start(bf16[4,3,7,32,256]{4,3,2,1,0:T(8,128)(2,1)} %bitcast.14), channel_id=1, source_target_pairs={{0,4},{4,0},{8,12},{12,8},{16,20},{20,16},{24,28},{28,24},{32,36},... | collective-permute-start | bytes 4128776 | tf_op jit(solution)/shard_map/ppermute | solution.py:841
  57.7 6.9 %collective-permute-start.3 = (bf16[17,32,128]{2,1,0:T(8,128)(2,1)}, bf16[17,32,128]{2,1,0:T(8,128)(2,1)S(1)}, u32[]{:S(2)}, u32[]{:S(2)}) collective-permute-start(bf16[17,32,128]{2,1,0:T(8,128)(2,1)} %get-tuple-element.54), channel_id=1, source_target_pairs={{3,1},{2,0},{1,3},{0,2},{7,5},{6,4},{5,7},{4,6},{11,9},{10,8},{9,1... | collective-permute-start | bytes 417800 | tf_op jit(solution)/shard_map/ppermute | solution.py:733
  58.8 9.7 %collective-permute-start.4 = (bf16[17,32,128]{2,1,0:T(8,128)(2,1)}, bf16[17,32,128]{2,1,0:T(8,128)(2,1)S(1)}, u32[]{:S(2)}, u32[]{:S(2)}) collective-permute-start(bf16[17,32,128]{2,1,0:T(8,128)(2,1)} %get-tuple-element.55), channel_id=1, source_target_pairs={{3,0},{2,3},{1,2},{0,1},{7,4},{6,7},{5,6},{4,5},{11,8},{10,11},{9,... | collective-permute-start | bytes 417800 | tf_op jit(solution)/shard_map/ppermute | solution.py:733
  59.3 9.2 %collective-permute-start.5 = (bf16[17,32,128]{2,1,0:T(8,128)(2,1)}, bf16[17,32,128]{2,1,0:T(8,128)(2,1)S(1)}, u32[]{:S(2)}, u32[]{:S(2)}) collective-permute-start(bf16[17,32,128]{2,1,0:T(8,128)(2,1)} %get-tuple-element.56), channel_id=1, source_target_pairs={{3,2},{2,1},{1,0},{0,3},{7,6},{6,5},{5,4},{4,7},{11,10},{10,9},{9,... | collective-permute-start | bytes 417800 | tf_op jit(solution)/shard_map/ppermute | solution.py:733
  61.7 23.7 %collective-permute-start.7 = (bf16[48,32,128]{2,1,0:T(8,128)(2,1)}, bf16[48,32,128]{2,1,0:T(8,128)(2,1)S(1)}, u32[]{:S(2)}, u32[]{:S(2)}) collective-permute-start(bf16[48,32,128]{2,1,0:T(8,128)(2,1)} %get-tuple-element.63), channel_id=1, source_target_pairs={{0,2},{1,3},{2,0},{3,1},{4,6},{5,7},{6,4},{7,5},{8,10},{9,11},{10,... | collective-permute-start | bytes 1179656 | tf_op jit(solution)/shard_map/ppermute | solution.py:733
  64.6 20.8 %collective-permute-start.8 = (bf16[48,32,128]{2,1,0:T(8,128)(2,1)}, bf16[48,32,128]{2,1,0:T(8,128)(2,1)S(1)}, u32[]{:S(2)}, u32[]{:S(2)}) collective-permute-start(bf16[48,32,128]{2,1,0:T(8,128)(2,1)} %get-tuple-element.64), channel_id=1, source_target_pairs={{0,1},{1,2},{2,3},{3,0},{4,5},{5,6},{6,7},{7,4},{8,9},{9,10},{10,1... | collective-permute-start | bytes 1179656 | tf_op jit(solution)/shard_map/ppermute | solution.py:733
  68.5 16.9 %collective-permute-start.9 = (bf16[48,32,128]{2,1,0:T(8,128)(2,1)}, bf16[48,32,128]{2,1,0:T(8,128)(2,1)S(1)}, u32[]{:S(2)}, u32[]{:S(2)}) collective-permute-start(bf16[48,32,128]{2,1,0:T(8,128)(2,1)} %get-tuple-element.65), channel_id=1, source_target_pairs={{0,3},{1,0},{2,1},{3,2},{4,7},{5,4},{6,5},{7,6},{8,11},{9,8},{10,9... | collective-permute-start | bytes 1179656 | tf_op jit(solution)/shard_map/ppermute | solution.py:733
  68.5 1.0 copy-start.2
  69.6 1.0 copy-start.5
  70.6 1.0 copy-start.8
  71.6 1.3 copy-start.14
  73.0 0.9 copy-start.17
  81.0 4.4 %copy-start.16 = (bf16[48,32,128]{2,1,0:T(8,128)(2,1)S(1)}, bf16[48,32,128]{2,1,0:T(8,128)(2,1)}, u32[]{:S(2)}) copy-start(bf16[48,32,128]{2,1,0:T(8,128)(2,1)} %get-tuple-element.62.u0) | copy-start | bytes 1179652
  90.5 14.3 %collective-permute-start.10 = (bf16[65,32,128]{2,1,0:T(8,128)(2,1)S(1)}, bf16[65,32,128]{2,1,0:T(8,128)(2,1)S(1)}, u32[]{:S(2)}, u32[]{:S(2)}) collective-permute-start(bf16[65,32,128]{2,1,0:T(8,128)(2,1)S(1)} %get-tuple-element.68), channel_id=1, source_target_pairs={{0,2},{1,3},{2,0},{3,1},{4,6},{5,7},{6,4},{7,5},{8,10},{9,11},{10,... | collective-permute-start | bytes 1597448 | tf_op jit(solution)/shard_map/ppermute | solution.py:733
  92.0 25.5 %collective-permute-start.11 = (bf16[65,32,128]{2,1,0:T(8,128)(2,1)S(1)}, bf16[65,32,128]{2,1,0:T(8,128)(2,1)S(1)}, u32[]{:S(2)}, u32[]{:S(2)}) collective-permute-start(bf16[65,32,128]{2,1,0:T(8,128)(2,1)S(1)} %get-tuple-element.69), channel_id=1, source_target_pairs={{0,1},{1,2},{2,3},{3,0},{4,5},{5,6},{6,7},{7,4},{8,9},{9,10},{10,1... | collective-permute-start | bytes 1597448 | tf_op jit(solution)/shard_map/ppermute | solution.py:733
  92.4 25.2 %collective-permute-start.12 = (bf16[65,32,128]{2,1,0:T(8,128)(2,1)S(1)}, bf16[65,32,128]{2,1,0:T(8,128)(2,1)S(1)}, u32[]{:S(2)}, u32[]{:S(2)}) collective-permute-start(bf16[65,32,128]{2,1,0:T(8,128)(2,1)S(1)} %get-tuple-element.70), channel_id=1, source_target_pairs={{0,3},{1,0},{2,1},{3,2},{4,7},{5,4},{6,5},{7,6},{8,11},{9,8},{10,9... | collective-permute-start | bytes 1597448 | tf_op jit(solution)/shard_map/ppermute | solution.py:733
  119.3 22.4 %copy-start.12 = (s32[192]{0:T(256)S(1)}, s32[192]{0:T(256)}, u32[]{:S(2)}) copy-start(s32[192]{0:T(256)} %copy-done.11) | copy-start | bytes 2308
  141.6 9.7 %copy-start.15 = (bf16[12,7,32,256]{3,2,1,0:T(8,128)(2,1)S(1)}, bf16[12,7,32,256]{3,2,1,0:T(8,128)(2,1)}, u32[]{:S(2)}) copy-start(bf16[12,7,32,256]{3,2,1,0:T(8,128)(2,1)} %all-gather.3.cloned.1.call-done) | copy-start | bytes 4128772
  146.3 13.3 %collective-permute-start.13 = (bf16[56,32,128]{2,1,0:T(8,128)(2,1)S(1)}, bf16[56,32,128]{2,1,0:T(8,128)(2,1)S(1)}, u32[]{:S(2)}, u32[]{:S(2)}) collective-permute-start(bf16[56,32,128]{2,1,0:T(8,128)(2,1)S(1)} %get-tuple-element.77), channel_id=1, source_target_pairs={{0,2},{1,3},{2,0},{3,1},{4,6},{5,7},{6,4},{7,5},{8,10},{9,11},{10,... | collective-permute-start | bytes 1376264 | tf_op jit(solution)/shard_map/ppermute | solution.py:733
  148.7 21.5 %collective-permute-start.14 = (bf16[56,32,128]{2,1,0:T(8,128)(2,1)S(1)}, bf16[56,32,128]{2,1,0:T(8,128)(2,1)S(1)}, u32[]{:S(2)}, u32[]{:S(2)}) collective-permute-start(bf16[56,32,128]{2,1,0:T(8,128)(2,1)S(1)} %get-tuple-element.78), channel_id=1, source_target_pairs={{0,1},{1,2},{2,3},{3,0},{4,5},{5,6},{6,7},{7,4},{8,9},{9,10},{10,1... | collective-permute-start | bytes 1376264 | tf_op jit(solution)/shard_map/ppermute | solution.py:733
  148.7 21.5 %collective-permute-start.15 = (bf16[56,32,128]{2,1,0:T(8,128)(2,1)S(1)}, bf16[56,32,128]{2,1,0:T(8,128)(2,1)S(1)}, u32[]{:S(2)}, u32[]{:S(2)}) collective-permute-start(bf16[56,32,128]{2,1,0:T(8,128)(2,1)S(1)} %get-tuple-element.79), channel_id=1, source_target_pairs={{0,3},{1,0},{2,1},{3,2},{4,7},{5,4},{6,5},{7,6},{8,11},{9,8},{10,9... | collective-permute-start | bytes 1376264 | tf_op jit(solution)/shard_map/ppermute | solution.py:733
  151.3 18.8 %copy-start.3 = (bf16[8,64,512]{2,1,0:T(8,128)(2,1)S(1)}, bf16[8,64,512]{2,1,0:T(8,128)(2,1)}, u32[]{:S(2)}) copy-start(bf16[8,64,512]{2,1,0:T(8,128)(2,1)} %copy-done.1) | copy-start | bytes 1572868
  151.3 18.8 %copy-start.6 = (bf16[8,64,512]{2,1,0:T(8,128)(2,1)S(1)}, bf16[8,64,512]{2,1,0:T(8,128)(2,1)}, u32[]{:S(2)}) copy-start(bf16[8,64,512]{2,1,0:T(8,128)(2,1)} %copy-done.4) | copy-start | bytes 1572868
  151.3 18.8 %copy-start.9 = (bf16[8,64,512]{2,1,0:T(8,128)(2,1)S(1)}, bf16[8,64,512]{2,1,0:T(8,128)(2,1)}, u32[]{:S(2)}) copy-start(bf16[8,64,512]{2,1,0:T(8,128)(2,1)} %copy-done.7) | copy-start | bytes 1572868
  174.0 10.1 %collective-permute-start.19 = (bf16[4,64,512]{2,1,0:T(8,128)(2,1)S(1)}, bf16[4,64,512]{2,1,0:T(8,128)(2,1)S(1)}, u32[]{:S(2)}, u32[]{:S(2)}) collective-permute-start(bf16[4,64,512]{2,1,0:T(8,128)(2,1)S(1)} %get-tuple-element.86), channel_id=1, source_target_pairs={{3,1},{2,0},{1,3},{0,2},{7,5},{6,4},{5,7},{4,6},{11,9},{10,8},{9,1... | collective-permute-start | bytes 786440 | tf_op jit(solution)/shard_map/ppermute | solution.py:733
  175.7 14.6 %collective-permute-start.20 = (bf16[4,64,512]{2,1,0:T(8,128)(2,1)S(1)}, bf16[4,64,512]{2,1,0:T(8,128)(2,1)S(1)}, u32[]{:S(2)}, u32[]{:S(2)}) collective-permute-start(bf16[4,64,512]{2,1,0:T(8,128)(2,1)S(1)} %get-tuple-element.87), channel_id=1, source_target_pairs={{3,0},{2,3},{1,2},{0,1},{7,4},{6,7},{5,6},{4,5},{11,8},{10,11},{9,... | collective-permute-start | bytes 786440 | tf_op jit(solution)/shard_map/ppermute | solution.py:733
  176.1 14.2 %collective-permute-start.21 = (bf16[4,64,512]{2,1,0:T(8,128)(2,1)S(1)}, bf16[4,64,512]{2,1,0:T(8,128)(2,1)S(1)}, u32[]{:S(2)}, u32[]{:S(2)}) collective-permute-start(bf16[4,64,512]{2,1,0:T(8,128)(2,1)S(1)} %get-tuple-element.88), channel_id=1, source_target_pairs={{3,2},{2,1},{1,0},{0,3},{7,6},{6,5},{5,4},{4,7},{11,10},{10,9},{9,... | collective-permute-start | bytes 786440 | tf_op jit(solution)/shard_map/ppermute | solution.py:733
  182.2 12.1 %collective-permute-start.16 = (bf16[4,64,512]{2,1,0:T(8,128)(2,1)S(1)}, bf16[4,64,512]{2,1,0:T(8,128)(2,1)S(1)}, u32[]{:S(2)}, u32[]{:S(2)}) collective-permute-start(bf16[4,64,512]{2,1,0:T(8,128)(2,1)S(1)} %get-tuple-element.82), channel_id=1, source_target_pairs={{0,2},{1,3},{2,0},{3,1},{4,6},{5,7},{6,4},{7,5},{8,10},{9,11},{10,... | collective-permute-start | bytes 786440 | tf_op jit(solution)/shard_map/ppermute | solution.py:733
  183.3 17.4 %collective-permute-start.17 = (bf16[4,64,512]{2,1,0:T(8,128)(2,1)S(1)}, bf16[4,64,512]{2,1,0:T(8,128)(2,1)S(1)}, u32[]{:S(2)}, u32[]{:S(2)}) collective-permute-start(bf16[4,64,512]{2,1,0:T(8,128)(2,1)S(1)} %get-tuple-element.83), channel_id=1, source_target_pairs={{0,1},{1,2},{2,3},{3,0},{4,5},{5,6},{6,7},{7,4},{8,9},{9,10},{10,1... | collective-permute-start | bytes 786440 | tf_op jit(solution)/shard_map/ppermute | solution.py:733
  184.1 16.5 %collective-permute-start.18 = (bf16[4,64,512]{2,1,0:T(8,128)(2,1)S(1)}, bf16[4,64,512]{2,1,0:T(8,128)(2,1)S(1)}, u32[]{:S(2)}, u32[]{:S(2)}) collective-permute-start(bf16[4,64,512]{2,1,0:T(8,128)(2,1)S(1)} %get-tuple-element.84), channel_id=1, source_target_pairs={{0,3},{1,0},{2,1},{3,2},{4,7},{5,4},{6,5},{7,6},{8,11},{9,8},{10,9... | collective-permute-start | bytes 786440 | tf_op jit(solution)/shard_map/ppermute | solution.py:733
Sparse Core Ops, SparseCore 0:
  22.9 27.4 all-gather.2

commit v5 on v4

--- a/solution.py
+++ b/solution.py
@@ -609,8 +609,9 @@
 
 
 def border2_kernel(
-    sel, ssel, owner, me, rows, held, recv, o0, o1, o2, o3, norm, src, cen, buf, sem, load
+    sel, ssel, owner, me, rows, held, recv, *refs, away
 ):
+    *outs, norm, src, cen, buf, sem, load = refs
     y = me[0]
     fetches = []
     for q in range(4):
@@ -651,7 +652,7 @@
     for q in range(4):
         cen[8 * q : 8 * q + 8, :] = buf[q, 0].astype(F32)[0:8]
     copies = []
-    for r, o in enumerate((o0, o1, o2, o3)):
+    for r, o in zip(away, outs):
         q = (y + r) & 3
 
         def face(i, _):
@@ -935,21 +936,26 @@
     )(links, lslot, crecv, me, *units)
     arrived = over_blocks(outgoing)
 
-    *parts, norm = call(
-        border2_kernel,
-        "border2",
-        12,
-        out_shape=(shape(56, 32, 128),) * 4 + (shape(8, 256, dtype=F32),),
-        in_specs=[SMEM] * 4 + [VMEM, HBM, VMEM],
-        out_specs=(ANY,) * 4 + (VMEM,),
-        scratch_shapes=[
-            pltpu.VMEM((FACES + 2 * DEVS + 1, 32, 128), BF16),
-            pltpu.VMEM((SLOTS + 2 * DEVS + 8, 128), F32),
-            pltpu.VMEM((4, 56, 32, 128), BF16),
-            pltpu.SemaphoreType.DMA((4,)),
-            pltpu.SemaphoreType.DMA((8,)),
-        ],
-    )(sel, ssel, owner, me, rows, held, arrived)
+    def border2(*away):
+        return call(
+            functools.partial(border2_kernel, away=away),
+            "border2",
+            12,
+            out_shape=(shape(56, 32, 128),) * len(away) + (shape(8, 256, dtype=F32),),
+            in_specs=[SMEM] * 4 + [VMEM, HBM, VMEM],
+            out_specs=(ANY,) * len(away) + (VMEM,),
+            scratch_shapes=[
+                pltpu.VMEM((FACES + 2 * DEVS + 1, 32, 128), BF16),
+                pltpu.VMEM((SLOTS + 2 * DEVS + 8, 128), F32),
+                pltpu.VMEM((4, 56, 32, 128), BF16),
+                pltpu.SemaphoreType.DMA((4,)),
+                pltpu.SemaphoreType.DMA((8,)),
+            ],
+        )(sel, ssel, owner, me, rows, held, arrived)
+
+    first, norm = border2(2)
+    own, *rest, _ = border2(0, 1, 3)
+    parts = [own, rest[0], first, rest[1]]
     units2 = exchange(parts)
     part2, weights = call(
         inner2_kernel,

time: 210 us -> 208 us (level)
  waiting for transfers between devices: 66 us -> 61.5 us
  Pallas kernels: 55.3 us -> 57.8 us
    ppermute x21, waiting for transfers between devices: 53.4 us -> 48.8 us  [exchange(): lax.ppermute(parts[r], 'chan', [(i, (i + r) % 4) for i in order])]
    pallas_call x1 -> x2, Pallas kernels: 4.65 us -> 7.19 us  [border2(): call(functools.partial(border2_kernel, away=away), 'border2', 12, out_sha...]
  transfers between devices with their start and end apart: 24 -> 24, of which waited for: 10 -> 9; matrix products, arithmetic and copies ran while one was open for 1% -> 1% of each run, Pallas kernels for 18% -> 21%
where the time goes in v5:
time: 208 us; the launch traced here: 207 us
  waiting for transfers between devices  61.5 us (30%)
  Pallas kernels  57.8 us (28%)
  starting transfers between devices  40.5 us (19%)
  blocking collectives  22.4 us (11%)
  between operations  13.8 us (7%)
  local copies, waits for them, and re-layouts  10.2 us (5%)
    ppermute x21, waiting for transfers between devices, exchange(): lax.ppermute(parts[r], 'chan', [(i, (i + r) % 4) for i in order])  48.8 us
    ppermute x21, starting transfers between devices, exchange(): lax.ppermute(parts[r], 'chan', [(i, (i + r) % 4) for i in order])  29.4 us
    all_to_all x1, blocking collectives, over_blocks(): lax.all_to_all(units, 'blocks', split_axis=0, concat_axis=0, tiled=True)  22.4 us
    all_to_all x1, waiting for transfers between devices, over_blocks(): lax.all_to_all(units, 'blocks', split_axis=0, concat_axis=0, tiled=True)  12.6 us
    all_to_all x1, starting transfers between devices, over_blocks(): lax.all_to_all(units, 'blocks', split_axis=0, concat_axis=0, tiled=True)  9.46 us
    pallas_call x2, Pallas kernels, local(): call(functools.partial(outer2_kernel, start=start), 'outer2', 32, 5, in_s...  7.72 us
    pallas_call x1, Pallas kernels, local(): call(extract_kernel, 'extract', 60, out_shape=(shape(FACES // 2, 64, 128)...  7.66 us
    unnamed x52, local copies, waits for them, and re-layouts  7.59 us
  transfers between devices with their start and end apart: 24, of which 9 were waited for; matrix products, arithmetic and copies ran while one was open for 1% of the time, Pallas kernels for 21%

profile of v5, /device:TPU:1, one launch (start us, length us, event | category | flops | bytes accessed | tf_op | source)
XLA Modules:
  0.0 207.3 jit_solution(13783742355347877054)
XLA Ops:
  6.5 2.6 %constant_dynamic-slice_fusion = (bf16[8,64,512]{2,1,0:T(8,128)(2,1)}, bf16[8,64,512]{2,1,0:T(8,128)(2,1)}, bf16[8,64,512]{2,1,0:T(8,128)(2,1)}) fusion(bf16[32,64,512]{2,1,0:T(8,128)(2,1)} %v0.5, s32[]{:T(128)S(6)} %select_n.34, s32[]{:T(128)S(6)} %select_n.32, s32[]{:T(128)S(6)} %select_n.30), kind=kLoop, calls=%fused_computation.2 | loop fusion | bytes 3145740 | tf_op jit(solution)/shard_map/dynamic_slice | solution.py:800
  9.1 3.6 %collective-permute-start.2 = (bf16[8,64,512]{2,1,0:T(8,128)(2,1)}, bf16[8,64,512]{2,1,0:T(8,128)(2,1)S(1)}, u32[]{:S(2)}, u32[]{:S(2)}) collective-permute-start(bf16[8,64,512]{2,1,0:T(8,128)(2,1)} %get-tuple-element.89), channel_id=1, source_target_pairs={{0,3},{1,0},{2,1},{3,2},{4,7},{5,4},{6,5},{7,6},{8,11},{9,8},{10,9... | collective-permute-start | bytes 1572872 | tf_op jit(solution)/shard_map/ppermute | solution.py:734
  12.7 0.0 collective-permute-start.1
  12.7 1.6 collective-permute-start
  14.3 0.6 pad_add_fusion.me
  14.9 7.7 %extract.1 = (bf16[96,64,128]{2,1,0:T(8,128)(2,1)}, bf16[32,144,128]{2,1,0:T(8,128)(2,1)}, bf16[3,7,32,256]{3,2,1,0:T(8,128)(2,1)}) custom-call(s32[2,32]{1,0:T(2,128)} %bitcast.21, s32[2,32]{1,0:T(2,128)} %bitcast.19, s32[2]{0:T(128)} %pad_add_fusion.me, bf16[32,64,512]{2,1,0:T(8,128)(2,1)} %v0.5, bf16[448,512]{1,0:T(8,128)(2,1)} %constant.51.clone.table, ...), custom_call_target="tpu_custom_call" | custom-call | flops 1000000000 | bytes 3000000 | tf_op jit(solution)/shard_map/extract/pallas_call | solution.py:772
  22.6 0.0 copy-start.18
  22.6 0.0 copy-start.19
  22.6 0.0 copy-start.20
  22.6 0.0 copy-start.21
  22.7 0.0 all-gather.3.cloned.1.call-update
  22.7 9.5 %all-to-all-start = ((bf16[32,144,128]{2,1,0:T(8,128)(2,1)}), bf16[32,144,128]{2,1,0:T(8,128)(2,1)S(1)}, u32[]{:S(2)}, u32[]{:S(2)}) async-start(bf16[32,144,128]{2,1,0:T(8,128)(2,1)} %get-tuple-element.52), calls=%async_computation | async-start | bytes 2359296 | tf_op jit(solution)/shard_map/all_to_all | solution.py:740
  32.2 0.0 copy-start.23
  32.2 0.0 copy-start.24
  32.2 0.0 copy-start.25
  32.2 3.1 %plan.1 = (s32[192]{0:T(256)S(1)}, s32[64]{0:T(128)S(1)}, s32[32]{0:T(128)S(1)}, s32[192]{0:T(256)S(1)}, s32[64]{0:T(128)S(1)}) custom-call(s32[6,32]{1,0:T(8,128)S(1)} %bitcast.18, s32[2,32]{1,0:T(2,128)S(1)} %bitcast.22, s32[2,32]{1,0:T(2,128)S(1)} %bitcast.20, s32[2,32]{1,0:T(2,128)S(1)} %bitcast.24), custom_call_target="tpu_custom_call" | custom-call | flops 20000000000 | bytes 60000000 | tf_op jit(solution)/shard_map/plan/pallas_call | solution.py:804
  35.3 0.6 copy-done.11
  35.9 0.5 copy-done.13
  36.5 0.7 select_maximum_fusion.par
  37.2 12.6 %all-to-all-done.recv = bf16[32,144,128]{2,1,0:T(8,128)(2,1)S(1)} async-done(((bf16[32,144,128]{2,1,0:T(8,128)(2,1)}), bf16[32,144,128]{2,1,0:T(8,128)(2,1)S(1)}, u32[]{:S(2)}, u32[]{:S(2)}) %all-to-all-start) | async-done | bytes 1179680 | tf_op jit(solution)/shard_map/all_to_all | solution.py:740
  49.8 1.0 copy-done.22
  50.9 5.1 %border1.1 = (bf16[17,32,128]{2,1,0:T(8,128)(2,1)}, bf16[17,32,128]{2,1,0:T(8,128)(2,1)}, bf16[17,32,128]{2,1,0:T(8,128)(2,1)}, bf16[17,32,128]{2,1,0:T(8,128)(2...) custom-call(s32[192]{0:T(256)} %copy-done.11, ...), custom_call_target="tpu_custom_call" | custom-call | flops 1000000000 | bytes 3000000 | tf_op jit(solution)/shard_map/border1/pallas_call | solution.py:820
  56.0 0.0 all-gather.3.cloned.1.call-done
  56.0 1.6 collective-permute-start.6
  57.6 1.1 collective-permute-start.3
  58.7 0.5 collective-permute-start.4
  59.2 2.4 %collective-permute-start.5 = (bf16[17,32,128]{2,1,0:T(8,128)(2,1)}, bf16[17,32,128]{2,1,0:T(8,128)(2,1)S(1)}, u32[]{:S(2)}, u32[]{:S(2)}) collective-permute-start(bf16[17,32,128]{2,1,0:T(8,128)(2,1)} %get-tuple-element.56), channel_id=1, source_target_pairs={{3,2},{2,1},{1,0},{0,3},{7,6},{6,5},{5,4},{4,7},{11,10},{10,9},{9,... | collective-permute-start | bytes 417800 | tf_op jit(solution)/shard_map/ppermute | solution.py:734
  61.7 1.2 collective-permute-start.7
  62.8 1.7 collective-permute-done.3.t1.u1
  64.6 1.6 collective-permute-start.8
  66.2 2.2 %collective-permute-done.4.t2.u2 = bf16[17,32,128]{2,1,0:T(8,128)(2,1)S(1)} collective-permute-done((bf16[17,32,128]{2,1,0:T(8,128)(2,1)}, bf16[17,32,128]{2,1,0:T(8,128)(2,1)S(1)}, u32[]{:S(2)}, u32[]{:S(2)}) %collective-permute-start.4) | collective-permute-done | bytes 139296 | tf_op jit(solution)/shard_map/ppermute | solution.py:734
  68.5 1.0 copy-done.2
  69.5 1.0 copy-done.5
  70.5 1.0 copy-done.8
  71.6 1.3 copy-done.14
  72.9 0.9 copy-done.17
  73.8 7.1 %inner1.1 = (f32[8,512,256]{2,1,0:T(8,128)S(1)}, f32[8,256]{1,0:T(8,128)S(1)}, bf16[256,1792]{1,0:T(8,128)(2,1)S(1)}) custom-call(s32[2]{0:T(128)S(1)} %copy-done.10, bf16[17,32,128]{2,1,0:T(8,128)(2,1)S(1)} %copy-done.17, bf16[17,32,128]{2,1,0:T(8,128)(2,1)S(1)} %collective-permute-done.3.t1.u1, bf16[17,32,128]{2,1,0:T(8,128)(2,1)S(1)} %collective-permute-done.4.t2.u2, ...), custom_call_target="tpu_custom_call" | custom-call | flops 8000000000 | bytes 24000000 | tf_op jit(solution)/shard_map/inner1/pallas_call | solution.py:863
  80.9 4.3 %tiles.1 = bf16[4,16,32,128]{3,2,1,0:T(8,128)(2,1)S(1)} custom-call(s32[2]{0:T(128)S(1)} %copy-done.10, bf16[17,32,128]{2,1,0:T(8,128)(2,1)S(1)} %copy-done.17, bf16[17,32,128]{2,1,0:T(8,128)(2,1)S(1)} %collective-permute-done.3.t1.u1, bf16[17,32,128]{2,1,0:T(8,128)(2,1)S(1)} %collective-permute-done.4.t2.u2, ...), custom_call_target="tpu_custom_call" | custom-call | flops 4000000000 | bytes 12000000 | tf_op jit(solution)/shard_map/tiles/pallas_call | solution.py:885
  85.3 5.1 %outer1.1 = (f32[8,512,256]{2,1,0:T(8,128)S(1)}, bf16[65,32,128]{2,1,0:T(8,128)(2,1)S(1)}, bf16[65,32,128]{2,1,0:T(8,128)(2,1)S(1)}, bf16[65,32,128]{2,1,0:T(8,128)(2,1)S(1)}, bf16[65,32,128]{2,1,0:T(8,128)(2,1)S(1)}) custom-call(s32[2]{0:T(128)S(1)} %copy-done.10, f32[8,256]{1,0:T(8,128)S(1)} %get-tuple-element.59.rows, ...), custom_call_target="tpu_custom_call" | custom-call | flops 5000000000 | bytes 15000000 | tf_op jit(solution)/shard_map/outer1/pallas_call | solution.py:902
  90.4 1.5 collective-permute-start.10
  91.9 0.4 collective-permute-start.11
  92.3 2.3 %collective-permute-start.12 = (bf16[65,32,128]{2,1,0:T(8,128)(2,1)S(1)}, bf16[65,32,128]{2,1,0:T(8,128)(2,1)S(1)}, u32[]{:S(2)}, u32[]{:S(2)}) collective-permute-start(bf16[65,32,128]{2,1,0:T(8,128)(2,1)S(1)} %get-tuple-element.70), channel_id=1, source_target_pairs={{0,3},{1,0},{2,1},{3,2},{4,7},{5,4},{6,5},{7,6},{8,11},{9,8},{10,9... | collective-permute-start | bytes 1597448 | tf_op jit(solution)/shard_map/ppermute | solution.py:734
  94.6 10.0 %collective-permute-done.10.v1 = bf16[65,32,128]{2,1,0:T(8,128)(2,1)S(1)} collective-permute-done((bf16[65,32,128]{2,1,0:T(8,128)(2,1)S(1)}, bf16[65,32,128]{2,1,0:T(8,128)(2,1)S(1)}, u32[]{:S(2)}, u32[]{:S(2)}) %collective-permute-start.10) | collective-permute-done | bytes 532512 | tf_op jit(solution)/shard_map/ppermute | solution.py:734
  104.6 12.9 %collective-permute-done.11.v2 = bf16[65,32,128]{2,1,0:T(8,128)(2,1)S(1)} collective-permute-done((bf16[65,32,128]{2,1,0:T(8,128)(2,1)S(1)}, bf16[65,32,128]{2,1,0:T(8,128)(2,1)S(1)}, u32[]{:S(2)}, u32[]{:S(2)}) %collective-permute-start.11) | collective-permute-done | bytes 532512 | tf_op jit(solution)/shard_map/ppermute | solution.py:734
  117.4 1.7 route2.1
  119.1 22.4 %all_to_all.10.recv = bf16[32,144,128]{2,1,0:T(8,128)(2,1)S(1)} all-to-all(bf16[32,144,128]{2,1,0:T(8,128)(2,1)S(1)} %get-tuple-element.72), channel_id=1, replica_groups=mesh['blocks'=32,'chan'=4] {'blocks'}, dimensions={0} | all-to-all | bytes 2359296 | tf_op jit(solution)/shard_map/all_to_all | solution.py:740
  141.5 2.6 %border2.2 = (bf16[56,32,128]{2,1,0:T(8,128)(2,1)S(1)}, f32[8,256]{1,0:T(8,128)S(1)}) custom-call(s32[192]{0:T(256)S(1)} %copy-done.12, s32[32]{0:T(128)S(1)} %get-tuple-element.48.ssel, s32[192]{0:T(256)S(1)} %get-tuple-element.49.owner, s32[2]{0:T(128)S(1)} %copy-done.10, f32[8,256]{1,0:T(8,128)S(1)} %get-tuple-element.59.rows, ...), custom_call_target="tpu_custom_call" | custom-call | flops 1000000000 | bytes 3000000 | tf_op jit(solution)/shard_map/border2/pallas_call | solution.py:940
  144.1 2.4 %collective-permute-start.13 = (bf16[56,32,128]{2,1,0:T(8,128)(2,1)S(1)}, bf16[56,32,128]{2,1,0:T(8,128)(2,1)S(1)}, u32[]{:S(2)}, u32[]{:S(2)}) collective-permute-start(bf16[56,32,128]{2,1,0:T(8,128)(2,1)S(1)} %get-tuple-element.77), channel_id=1, source_target_pairs={{0,2},{1,3},{2,0},{3,1},{4,6},{5,7},{6,4},{7,5},{8,10},{9,11},{10,... | collective-permute-start | bytes 1376264 | tf_op jit(solution)/shard_map/ppermute | solution.py:734
  146.5 4.6 %border2.3 = (bf16[56,32,128]{2,1,0:T(8,128)(2,1)S(1)}, bf16[56,32,128]{2,1,0:T(8,128)(2,1)S(1)}, bf16[56,32,128]{2,1,0:T(8,128)(2,1)S(1)}, f32[8,256]{1,0:T(8,128)}) custom-call(s32[192]{0:T(256)S(1)} %copy-done.12, s32[32]{0:T(128)S(1)} %get-tuple-element.48.ssel, s32[192]{0:T(256)S(1)} %get-tuple-element.49.owner, s32[2]{0:T(128)S(1)} %copy-done.10, ...), custom_call_target="tpu_custom_call" | custom-call | flops 1000000000 | bytes 3000000 | tf_op jit(solution)/shard_map/border2/pallas_call | solution.py:940
  151.1 0.1 collective-permute-start.14
  151.2 2.7 %collective-permute-start.15 = (bf16[56,32,128]{2,1,0:T(8,128)(2,1)S(1)}, bf16[56,32,128]{2,1,0:T(8,128)(2,1)S(1)}, u32[]{:S(2)}, u32[]{:S(2)}) collective-permute-start(bf16[56,32,128]{2,1,0:T(8,128)(2,1)S(1)} %get-tuple-element.79), channel_id=1, source_target_pairs={{0,3},{1,0},{2,1},{3,2},{4,7},{5,4},{6,5},{7,6},{8,11},{9,8},{10,9... | collective-permute-start | bytes 1376264 | tf_op jit(solution)/shard_map/ppermute | solution.py:734
  153.8 6.9 %inner2.1 = (f32[8,512,256]{2,1,0:T(8,128)S(1)}, bf16[256,1792]{1,0:T(8,128)(2,1)S(1)}) custom-call(s32[2]{0:T(128)S(1)} %copy-done.10, f32[8,256]{1,0:T(8,128)S(1)} %get-tuple-element.73.rows, f32[8,512,256]{2,1,0:T(8,128)S(1)} %get-tuple-element.74.hid, bf16[4,3,7,32,256]{4,3,2,1,0:T(8,128)(2,1)S(1)} %bitcast.17, ...), custom_call_target="tpu_custom_call" | custom-call | flops 8000000000 | bytes 24000000 | tf_op jit(solution)/shard_map/inner2/pallas_call | solution.py:960
  160.8 7.2 %collective-permute-done.14.u2 = bf16[56,32,128]{2,1,0:T(8,128)(2,1)S(1)} collective-permute-done((bf16[56,32,128]{2,1,0:T(8,128)(2,1)S(1)}, bf16[56,32,128]{2,1,0:T(8,128)(2,1)S(1)}, u32[]{:S(2)}, u32[]{:S(2)}) %collective-permute-start.14) | collective-permute-done | bytes 458784 | tf_op jit(solution)/shard_map/ppermute | solution.py:734
  168.0 3.9 %outer2.3 = (bf16[4,64,512]{2,1,0:T(8,128)(2,1)S(1)}, bf16[4,64,512]{2,1,0:T(8,128)(2,1)S(1)}, bf16[4,64,512]{2,1,0:T(8,128)(2,1)S(1)}, bf16[4,64,512]{2,1,0:T(8,128)(2,1)S(1)}) custom-call(s32[2]{0:T(128)S(1)} %copy-done.10, f32[8,512,256]{2,1,0:T(8,128)S(1)} %get-tuple-element.75.part, bf16[32,64,512]{2,1,0:T(8,128)(2,1)S(1)} %copy-done, ...), custom_call_target="tpu_custom_call" | custom-call | flops 5000000000 | bytes 15000000 | tf_op jit(solution)/shard_map/outer2/pallas_call | solution.py:977
  171.9 2.4 %collective-permute-start.19 = (bf16[4,64,512]{2,1,0:T(8,128)(2,1)S(1)}, bf16[4,64,512]{2,1,0:T(8,128)(2,1)S(1)}, u32[]{:S(2)}, u32[]{:S(2)}) collective-permute-start(bf16[4,64,512]{2,1,0:T(8,128)(2,1)S(1)} %get-tuple-element.86), channel_id=1, source_target_pairs={{3,1},{2,0},{1,3},{0,2},{7,5},{6,4},{5,7},{4,6},{11,9},{10,8},{9,1... | collective-permute-start | bytes 786440 | tf_op jit(solution)/shard_map/ppermute | solution.py:734
  174.3 2.7 %collective-permute-start.21 = (bf16[4,64,512]{2,1,0:T(8,128)(2,1)S(1)}, bf16[4,64,512]{2,1,0:T(8,128)(2,1)S(1)}, u32[]{:S(2)}, u32[]{:S(2)}) collective-permute-start(bf16[4,64,512]{2,1,0:T(8,128)(2,1)S(1)} %get-tuple-element.88), channel_id=1, source_target_pairs={{3,2},{2,1},{1,0},{0,3},{7,6},{6,5},{5,4},{4,7},{11,10},{10,9},{9,... | collective-permute-start | bytes 786440 | tf_op jit(solution)/shard_map/ppermute | solution.py:734
  176.9 3.9 %outer2.2 = (bf16[4,64,512]{2,1,0:T(8,128)(2,1)S(1)}, bf16[4,64,512]{2,1,0:T(8,128)(2,1)S(1)}, bf16[4,64,512]{2,1,0:T(8,128)(2,1)S(1)}, bf16[4,64,512]{2,1,0:T(8,128)(2,1)S(1)}) custom-call(s32[2]{0:T(128)S(1)} %copy-done.10, f32[8,512,256]{2,1,0:T(8,128)S(1)} %get-tuple-element.75.part, bf16[32,64,512]{2,1,0:T(8,128)(2,1)S(1)} %copy-done, ...), custom_call_target="tpu_custom_call" | custom-call | flops 5000000000 | bytes 15000000 | tf_op jit(solution)/shard_map/outer2/pallas_call | solution.py:977
  180.8 0.3 collective-permute-start.16
  181.1 0.9 collective-permute-start.17
  182.0 1.8 collective-permute-start.18
  183.8 4.3 %collective-permute-done.20.refs_6_ = bf16[4,64,512]{2,1,0:T(8,128)(2,1)S(1)} collective-permute-done((bf16[4,64,512]{2,1,0:T(8,128)(2,1)S(1)}, bf16[4,64,512]{2,1,0:T(8,128)(2,1)S(1)}, u32[]{:S(2)}, u32[]{:S(2)}) %collective-permute-start.20) | collective-permute-done | bytes 262176 | tf_op jit(solution)/shard_map/ppermute | solution.py:734
  188.1 4.0 %collective-permute-done.16.refs_1_ = bf16[4,64,512]{2,1,0:T(8,128)(2,1)S(1)} collective-permute-done((bf16[4,64,512]{2,1,0:T(8,128)(2,1)S(1)}, bf16[4,64,512]{2,1,0:T(8,128)(2,1)S(1)}, u32[]{:S(2)}, u32[]{:S(2)}) %collective-permute-start.16) | collective-permute-done | bytes 262176 | tf_op jit(solution)/shard_map/ppermute | solution.py:734
  192.2 6.4 %collective-permute-done.17.refs_2_ = bf16[4,64,512]{2,1,0:T(8,128)(2,1)S(1)} collective-permute-done((bf16[4,64,512]{2,1,0:T(8,128)(2,1)S(1)}, bf16[4,64,512]{2,1,0:T(8,128)(2,1)S(1)}, u32[]{:S(2)}, u32[]{:S(2)}) %collective-permute-start.17) | collective-permute-done | bytes 262176 | tf_op jit(solution)/shard_map/ppermute | solution.py:734
  198.6 1.9 gather.1
  (56 shorter events, 0.1 us)
Async XLA Ops:
  6.5 49.4 %all-gather.3.cloned.1.call-start = ((), (), s32[]{:S(2)}) async-start(), calls=%async_computation.2 | async-start | bytes 1720320 | tf_op jit(solution)/shard_map/all_gather | solution.py:795
  9.1 28.1 %collective-permute-start.2 = (bf16[8,64,512]{2,1,0:T(8,128)(2,1)}, bf16[8,64,512]{2,1,0:T(8,128)(2,1)S(1)}, u32[]{:S(2)}, u32[]{:S(2)}) collective-permute-start(bf16[8,64,512]{2,1,0:T(8,128)(2,1)} %get-tuple-element.89), channel_id=1, source_target_pairs={{0,3},{1,0},{2,1},{3,2},{4,7},{5,4},{6,5},{7,6},{8,11},{9,8},{10,9... | collective-permute-start | bytes 1572872 | tf_op jit(solution)/shard_map/ppermute | solution.py:734
  12.7 24.5 %collective-permute-start.1 = (bf16[8,64,512]{2,1,0:T(8,128)(2,1)}, bf16[8,64,512]{2,1,0:T(8,128)(2,1)S(1)}, u32[]{:S(2)}, u32[]{:S(2)}) collective-permute-start(bf16[8,64,512]{2,1,0:T(8,128)(2,1)} %get-tuple-element.90), channel_id=1, source_target_pairs={{0,1},{1,2},{2,3},{3,0},{4,5},{5,6},{6,7},{7,4},{8,9},{9,10},{10,1... | collective-permute-start | bytes 1572872 | tf_op jit(solution)/shard_map/ppermute | solution.py:734
  12.7 24.5 %collective-permute-start = (bf16[8,64,512]{2,1,0:T(8,128)(2,1)}, bf16[8,64,512]{2,1,0:T(8,128)(2,1)S(1)}, u32[]{:S(2)}, u32[]{:S(2)}) collective-permute-start(bf16[8,64,512]{2,1,0:T(8,128)(2,1)} %get-tuple-element.91), channel_id=1, source_target_pairs={{0,2},{1,3},{2,0},{3,1},{4,6},{5,7},{6,4},{7,5},{8,10},{9,11},{10,... | collective-permute-start | bytes 1572872 | tf_op jit(solution)/shard_map/ppermute | solution.py:734
  22.6 9.5 %copy-start.18 = (s32[32,6]{0,1:T(8,128)S(1)}, s32[32,6]{0,1:T(8,128)}, u32[]{:S(2)}) copy-start(s32[32,6]{0,1:T(8,128)} %param.15) | copy-start | bytes 2308
  22.6 9.5 %copy-start.19 = (s32[1,32,2]{1,2,0:T(2,128)S(1)}, s32[1,32,2]{1,2,0:T(2,128)}, u32[]{:S(2)}) copy-start(s32[1,32,2]{1,2,0:T(2,128)} %param.17) | copy-start | bytes 772
  22.6 9.5 %copy-start.20 = (s32[1,32,2]{1,2,0:T(2,128)S(1)}, s32[1,32,2]{1,2,0:T(2,128)}, u32[]{:S(2)}) copy-start(s32[1,32,2]{1,2,0:T(2,128)} %param.16) | copy-start | bytes 772
  22.6 9.5 %copy-start.21 = (s32[1,32,2]{1,2,0:T(2,128)S(1)}, s32[1,32,2]{1,2,0:T(2,128)}, u32[]{:S(2)}) copy-start(s32[1,32,2]{1,2,0:T(2,128)} %param.18) | copy-start | bytes 772
  22.7 27.2 %all-to-all-start = ((bf16[32,144,128]{2,1,0:T(8,128)(2,1)}), bf16[32,144,128]{2,1,0:T(8,128)(2,1)S(1)}, u32[]{:S(2)}, u32[]{:S(2)}) async-start(bf16[32,144,128]{2,1,0:T(8,128)(2,1)} %get-tuple-element.52), calls=%async_computation | async-start | bytes 2359296 | tf_op jit(solution)/shard_map/all_to_all | solution.py:740
  32.2 4.3 %copy-start.23 = (f32[3,64]{1,0:T(4,128)S(1)}, f32[3,64]{1,0:T(4,128)}, u32[]{:S(2)}) copy-start(f32[3,64]{1,0:T(4,128)} %param.13) | copy-start | bytes 2308
  32.2 4.3 %copy-start.24 = (f32[3,64]{1,0:T(4,128)S(1)}, f32[3,64]{1,0:T(4,128)}, u32[]{:S(2)}) copy-start(f32[3,64]{1,0:T(4,128)} %param.12) | copy-start | bytes 2308
  32.2 4.3 %copy-start.25 = (f32[64]{0:T(128)S(1)}, f32[64]{0:T(128)}, u32[]{:S(2)}) copy-start(f32[64]{0:T(128)} %param.14) | copy-start | bytes 772
  35.3 0.6 copy-start.11
  35.9 0.5 copy-start.13
  37.2 13.7 %copy-start.1 = (bf16[8,64,512]{2,1,0:T(8,128)(2,1)}, bf16[8,64,512]{2,1,0:T(8,128)(2,1)S(1)}, u32[]{:S(2)}) copy-start(bf16[8,64,512]{2,1,0:T(8,128)(2,1)S(1)} %collective-permute-done.2.x3.v3) | copy-start | bytes 1572868
  37.2 13.7 %copy-start.4 = (bf16[8,64,512]{2,1,0:T(8,128)(2,1)}, bf16[8,64,512]{2,1,0:T(8,128)(2,1)S(1)}, u32[]{:S(2)}) copy-start(bf16[8,64,512]{2,1,0:T(8,128)(2,1)S(1)} %collective-permute-done.1.x2.v2) | copy-start | bytes 1572868
  37.2 12.6 %copy-start.7 = (bf16[8,64,512]{2,1,0:T(8,128)(2,1)}, bf16[8,64,512]{2,1,0:T(8,128)(2,1)S(1)}, u32[]{:S(2)}) copy-start(bf16[8,64,512]{2,1,0:T(8,128)(2,1)S(1)} %collective-permute-done.x1.v1) | copy-start | bytes 1572868
  49.8 1.0 copy-start.22
  50.9 17.6 %copy-start = (bf16[32,64,512]{2,1,0:T(8,128)(2,1)S(1)}, bf16[32,64,512]{2,1,0:T(8,128)(2,1)}, u32[]{:S(2)}) copy-start(bf16[32,64,512]{2,1,0:T(8,128)(2,1)} %v0.5) | copy-start | bytes 6291460
  50.9 17.6 %copy-start.10 = (s32[2]{0:T(128)S(1)}, s32[2]{0:T(128)}, u32[]{:S(2)}) copy-start(s32[2]{0:T(128)} %pad_add_fusion.me) | copy-start | bytes 28
  56.0 12.4 %collective-permute-start.6 = (bf16[4,3,7,32,256]{4,3,2,1,0:T(8,128)(2,1)}, bf16[4,3,7,32,256]{4,3,2,1,0:T(8,128)(2,1)S(1)}, u32[]{:S(2)}, u32[]{:S(2)}) collective-permute-start(bf16[4,3,7,32,256]{4,3,2,1,0:T(8,128)(2,1)} %bitcast.14), channel_id=1, source_target_pairs={{0,4},{4,0},{8,12},{12,8},{16,20},{20,16},{24,28},{28,24},{32,36},... | collective-permute-start | bytes 4128776 | tf_op jit(solution)/shard_map/ppermute | solution.py:842
  57.6 6.9 %collective-permute-start.3 = (bf16[17,32,128]{2,1,0:T(8,128)(2,1)}, bf16[17,32,128]{2,1,0:T(8,128)(2,1)S(1)}, u32[]{:S(2)}, u32[]{:S(2)}) collective-permute-start(bf16[17,32,128]{2,1,0:T(8,128)(2,1)} %get-tuple-element.54), channel_id=1, source_target_pairs={{3,1},{2,0},{1,3},{0,2},{7,5},{6,4},{5,7},{4,6},{11,9},{10,8},{9,1... | collective-permute-start | bytes 417800 | tf_op jit(solution)/shard_map/ppermute | solution.py:734
  58.7 9.7 %collective-permute-start.4 = (bf16[17,32,128]{2,1,0:T(8,128)(2,1)}, bf16[17,32,128]{2,1,0:T(8,128)(2,1)S(1)}, u32[]{:S(2)}, u32[]{:S(2)}) collective-permute-start(bf16[17,32,128]{2,1,0:T(8,128)(2,1)} %get-tuple-element.55), channel_id=1, source_target_pairs={{3,0},{2,3},{1,2},{0,1},{7,4},{6,7},{5,6},{4,5},{11,8},{10,11},{9,... | collective-permute-start | bytes 417800 | tf_op jit(solution)/shard_map/ppermute | solution.py:734
  59.2 9.2 %collective-permute-start.5 = (bf16[17,32,128]{2,1,0:T(8,128)(2,1)}, bf16[17,32,128]{2,1,0:T(8,128)(2,1)S(1)}, u32[]{:S(2)}, u32[]{:S(2)}) collective-permute-start(bf16[17,32,128]{2,1,0:T(8,128)(2,1)} %get-tuple-element.56), channel_id=1, source_target_pairs={{3,2},{2,1},{1,0},{0,3},{7,6},{6,5},{5,4},{4,7},{11,10},{10,9},{9,... | collective-permute-start | bytes 417800 | tf_op jit(solution)/shard_map/ppermute | solution.py:734
  61.7 23.6 %collective-permute-start.7 = (bf16[48,32,128]{2,1,0:T(8,128)(2,1)}, bf16[48,32,128]{2,1,0:T(8,128)(2,1)S(1)}, u32[]{:S(2)}, u32[]{:S(2)}) collective-permute-start(bf16[48,32,128]{2,1,0:T(8,128)(2,1)} %get-tuple-element.63), channel_id=1, source_target_pairs={{0,2},{1,3},{2,0},{3,1},{4,6},{5,7},{6,4},{7,5},{8,10},{9,11},{10,... | collective-permute-start | bytes 1179656 | tf_op jit(solution)/shard_map/ppermute | solution.py:734
  64.6 20.7 %collective-permute-start.8 = (bf16[48,32,128]{2,1,0:T(8,128)(2,1)}, bf16[48,32,128]{2,1,0:T(8,128)(2,1)S(1)}, u32[]{:S(2)}, u32[]{:S(2)}) collective-permute-start(bf16[48,32,128]{2,1,0:T(8,128)(2,1)} %get-tuple-element.64), channel_id=1, source_target_pairs={{0,1},{1,2},{2,3},{3,0},{4,5},{5,6},{6,7},{7,4},{8,9},{9,10},{10,1... | collective-permute-start | bytes 1179656 | tf_op jit(solution)/shard_map/ppermute | solution.py:734
  68.4 16.9 %collective-permute-start.9 = (bf16[48,32,128]{2,1,0:T(8,128)(2,1)}, bf16[48,32,128]{2,1,0:T(8,128)(2,1)S(1)}, u32[]{:S(2)}, u32[]{:S(2)}) collective-permute-start(bf16[48,32,128]{2,1,0:T(8,128)(2,1)} %get-tuple-element.65), channel_id=1, source_target_pairs={{0,3},{1,0},{2,1},{3,2},{4,7},{5,4},{6,5},{7,6},{8,11},{9,8},{10,9... | collective-permute-start | bytes 1179656 | tf_op jit(solution)/shard_map/ppermute | solution.py:734
  68.4 1.0 copy-start.2
  69.5 1.0 copy-start.5
  70.5 1.0 copy-start.8
  71.6 1.3 copy-start.14
  72.9 0.9 copy-start.17
  80.9 4.4 %copy-start.16 = (bf16[48,32,128]{2,1,0:T(8,128)(2,1)S(1)}, bf16[48,32,128]{2,1,0:T(8,128)(2,1)}, u32[]{:S(2)}) copy-start(bf16[48,32,128]{2,1,0:T(8,128)(2,1)} %get-tuple-element.62.u0) | copy-start | bytes 1179652
  90.4 14.2 %collective-permute-start.10 = (bf16[65,32,128]{2,1,0:T(8,128)(2,1)S(1)}, bf16[65,32,128]{2,1,0:T(8,128)(2,1)S(1)}, u32[]{:S(2)}, u32[]{:S(2)}) collective-permute-start(bf16[65,32,128]{2,1,0:T(8,128)(2,1)S(1)} %get-tuple-element.68), channel_id=1, source_target_pairs={{0,2},{1,3},{2,0},{3,1},{4,6},{5,7},{6,4},{7,5},{8,10},{9,11},{10,... | collective-permute-start | bytes 1597448 | tf_op jit(solution)/shard_map/ppermute | solution.py:734
  91.9 25.5 %collective-permute-start.11 = (bf16[65,32,128]{2,1,0:T(8,128)(2,1)S(1)}, bf16[65,32,128]{2,1,0:T(8,128)(2,1)S(1)}, u32[]{:S(2)}, u32[]{:S(2)}) collective-permute-start(bf16[65,32,128]{2,1,0:T(8,128)(2,1)S(1)} %get-tuple-element.69), channel_id=1, source_target_pairs={{0,1},{1,2},{2,3},{3,0},{4,5},{5,6},{6,7},{7,4},{8,9},{9,10},{10,1... | collective-permute-start | bytes 1597448 | tf_op jit(solution)/shard_map/ppermute | solution.py:734
  92.3 25.1 %collective-permute-start.12 = (bf16[65,32,128]{2,1,0:T(8,128)(2,1)S(1)}, bf16[65,32,128]{2,1,0:T(8,128)(2,1)S(1)}, u32[]{:S(2)}, u32[]{:S(2)}) collective-permute-start(bf16[65,32,128]{2,1,0:T(8,128)(2,1)S(1)} %get-tuple-element.70), channel_id=1, source_target_pairs={{0,3},{1,0},{2,1},{3,2},{4,7},{5,4},{6,5},{7,6},{8,11},{9,8},{10,9... | collective-permute-start | bytes 1597448 | tf_op jit(solution)/shard_map/ppermute | solution.py:734
  119.1 22.4 %copy-start.12 = (s32[192]{0:T(256)S(1)}, s32[192]{0:T(256)}, u32[]{:S(2)}) copy-start(s32[192]{0:T(256)} %copy-done.11) | copy-start | bytes 2308
  144.1 9.7 %copy-start.15 = (bf16[12,7,32,256]{3,2,1,0:T(8,128)(2,1)S(1)}, bf16[12,7,32,256]{3,2,1,0:T(8,128)(2,1)}, u32[]{:S(2)}) copy-start(bf16[12,7,32,256]{3,2,1,0:T(8,128)(2,1)} %all-gather.3.cloned.1.call-done) | copy-start | bytes 4128772
  144.1 16.6 %collective-permute-start.13 = (bf16[56,32,128]{2,1,0:T(8,128)(2,1)S(1)}, bf16[56,32,128]{2,1,0:T(8,128)(2,1)S(1)}, u32[]{:S(2)}, u32[]{:S(2)}) collective-permute-start(bf16[56,32,128]{2,1,0:T(8,128)(2,1)S(1)} %get-tuple-element.77), channel_id=1, source_target_pairs={{0,2},{1,3},{2,0},{3,1},{4,6},{5,7},{6,4},{7,5},{8,10},{9,11},{10,... | collective-permute-start | bytes 1376264 | tf_op jit(solution)/shard_map/ppermute | solution.py:734
  151.1 16.9 %collective-permute-start.14 = (bf16[56,32,128]{2,1,0:T(8,128)(2,1)S(1)}, bf16[56,32,128]{2,1,0:T(8,128)(2,1)S(1)}, u32[]{:S(2)}, u32[]{:S(2)}) collective-permute-start(bf16[56,32,128]{2,1,0:T(8,128)(2,1)S(1)} %get-tuple-element.78), channel_id=1, source_target_pairs={{0,1},{1,2},{2,3},{3,0},{4,5},{5,6},{6,7},{7,4},{8,9},{9,10},{10,1... | collective-permute-start | bytes 1376264 | tf_op jit(solution)/shard_map/ppermute | solution.py:734
  151.2 16.8 %collective-permute-start.15 = (bf16[56,32,128]{2,1,0:T(8,128)(2,1)S(1)}, bf16[56,32,128]{2,1,0:T(8,128)(2,1)S(1)}, u32[]{:S(2)}, u32[]{:S(2)}) collective-permute-start(bf16[56,32,128]{2,1,0:T(8,128)(2,1)S(1)} %get-tuple-element.79), channel_id=1, source_target_pairs={{0,3},{1,0},{2,1},{3,2},{4,7},{5,4},{6,5},{7,6},{8,11},{9,8},{10,9... | collective-permute-start | bytes 1376264 | tf_op jit(solution)/shard_map/ppermute | solution.py:734
  153.8 14.2 %copy-start.3 = (bf16[8,64,512]{2,1,0:T(8,128)(2,1)S(1)}, bf16[8,64,512]{2,1,0:T(8,128)(2,1)}, u32[]{:S(2)}) copy-start(bf16[8,64,512]{2,1,0:T(8,128)(2,1)} %copy-done.1) | copy-start | bytes 1572868
  153.8 14.2 %copy-start.6 = (bf16[8,64,512]{2,1,0:T(8,128)(2,1)S(1)}, bf16[8,64,512]{2,1,0:T(8,128)(2,1)}, u32[]{:S(2)}) copy-start(bf16[8,64,512]{2,1,0:T(8,128)(2,1)} %copy-done.4) | copy-start | bytes 1572868
  153.8 14.2 %copy-start.9 = (bf16[8,64,512]{2,1,0:T(8,128)(2,1)S(1)}, bf16[8,64,512]{2,1,0:T(8,128)(2,1)}, u32[]{:S(2)}) copy-start(bf16[8,64,512]{2,1,0:T(8,128)(2,1)} %copy-done.7) | copy-start | bytes 1572868
  171.9 10.1 %collective-permute-start.19 = (bf16[4,64,512]{2,1,0:T(8,128)(2,1)S(1)}, bf16[4,64,512]{2,1,0:T(8,128)(2,1)S(1)}, u32[]{:S(2)}, u32[]{:S(2)}) collective-permute-start(bf16[4,64,512]{2,1,0:T(8,128)(2,1)S(1)} %get-tuple-element.86), channel_id=1, source_target_pairs={{3,1},{2,0},{1,3},{0,2},{7,5},{6,4},{5,7},{4,6},{11,9},{10,8},{9,1... | collective-permute-start | bytes 786440 | tf_op jit(solution)/shard_map/ppermute | solution.py:734
  174.3 13.9 %collective-permute-start.20 = (bf16[4,64,512]{2,1,0:T(8,128)(2,1)S(1)}, bf16[4,64,512]{2,1,0:T(8,128)(2,1)S(1)}, u32[]{:S(2)}, u32[]{:S(2)}) collective-permute-start(bf16[4,64,512]{2,1,0:T(8,128)(2,1)S(1)} %get-tuple-element.87), channel_id=1, source_target_pairs={{3,0},{2,3},{1,2},{0,1},{7,4},{6,7},{5,6},{4,5},{11,8},{10,11},{9,... | collective-permute-start | bytes 786440 | tf_op jit(solution)/shard_map/ppermute | solution.py:734
  174.3 13.9 %collective-permute-start.21 = (bf16[4,64,512]{2,1,0:T(8,128)(2,1)S(1)}, bf16[4,64,512]{2,1,0:T(8,128)(2,1)S(1)}, u32[]{:S(2)}, u32[]{:S(2)}) collective-permute-start(bf16[4,64,512]{2,1,0:T(8,128)(2,1)S(1)} %get-tuple-element.88), channel_id=1, source_target_pairs={{3,2},{2,1},{1,0},{0,3},{7,6},{6,5},{5,4},{4,7},{11,10},{10,9},{9,... | collective-permute-start | bytes 786440 | tf_op jit(solution)/shard_map/ppermute | solution.py:734
  180.8 11.4 %collective-permute-start.16 = (bf16[4,64,512]{2,1,0:T(8,128)(2,1)S(1)}, bf16[4,64,512]{2,1,0:T(8,128)(2,1)S(1)}, u32[]{:S(2)}, u32[]{:S(2)}) collective-permute-start(bf16[4,64,512]{2,1,0:T(8,128)(2,1)S(1)} %get-tuple-element.82), channel_id=1, source_target_pairs={{0,2},{1,3},{2,0},{3,1},{4,6},{5,7},{6,4},{7,5},{8,10},{9,11},{10,... | collective-permute-start | bytes 786440 | tf_op jit(solution)/shard_map/ppermute | solution.py:734
  181.1 17.4 %collective-permute-start.17 = (bf16[4,64,512]{2,1,0:T(8,128)(2,1)S(1)}, bf16[4,64,512]{2,1,0:T(8,128)(2,1)S(1)}, u32[]{:S(2)}, u32[]{:S(2)}) collective-permute-start(bf16[4,64,512]{2,1,0:T(8,128)(2,1)S(1)} %get-tuple-element.83), channel_id=1, source_target_pairs={{0,1},{1,2},{2,3},{3,0},{4,5},{5,6},{6,7},{7,4},{8,9},{9,10},{10,1... | collective-permute-start | bytes 786440 | tf_op jit(solution)/shard_map/ppermute | solution.py:734
  182.0 16.6 %collective-permute-start.18 = (bf16[4,64,512]{2,1,0:T(8,128)(2,1)S(1)}, bf16[4,64,512]{2,1,0:T(8,128)(2,1)S(1)}, u32[]{:S(2)}, u32[]{:S(2)}) collective-permute-start(bf16[4,64,512]{2,1,0:T(8,128)(2,1)S(1)} %get-tuple-element.84), channel_id=1, source_target_pairs={{0,3},{1,0},{2,1},{3,2},{4,7},{5,4},{6,5},{7,6},{8,11},{9,8},{10,9... | collective-permute-start | bytes 786440 | tf_op jit(solution)/shard_map/ppermute | solution.py:734
Sparse Core Ops, SparseCore 0:
  22.8 27.4 all-gather.2
